TPU v7x, 128 devices: a whole 4x4x4 slice. The times are simulated.
128 devices in a mesh: tm: 16 (over x, y), space: 8 (over z, core).
Axes of the slice: x: 4, y: 4, z: 4, core: 2. Of those that a mesh axis runs over, the one named last changes fastest.
Arguments:
- trajectory: float32 [64, 512, 1024], P('tm', 'space'), may hold values from -1.2 to 1.2
- initial_state: float32 [512, 1024], P('space'), may hold values from -1 to 1
- residual: float32 [64, 512, 1024], P('tm', 'space'), may hold values from -3000 to 3000
- mobility: float32 [512, 1024], P('space'), may hold values from 20 to 200
Outputs:
- update: float32 [64, 512, 1024], P('tm', 'space')
- reduction: float32 [], replicated
All inputs are finite; a program needn't handle non-finite values.
Results may differ from a plain program's by a relative error of at most 0.00015.
Values sent between devices are 32-bit elements; how exact they have to be, the bound alone decides.
No kernel may reach another device: no remote copies, remote signals or barrier semaphores. Data moves between devices by JAX's collectives and lax.ppermute only.
A program may use at most 64 MiB of HBM per device.

v0:
```python
import functools

import jax
import jax.numpy as jnp
from jax import lax
from jax.sharding import Mesh
from jax.sharding import PartitionSpec as P

NT = 64
SWEEPS = 16
SPACE = ("space_0", "space_1")
TM = ("tm_0", "tm_1")
TM_SPACE = ("tm_0", "tm_1", "space_0", "space_1")


circ_weight = 0.2
time_step = 0.01
damping = 0.8
reaction_scale = 40.0


def padded_2(block, sides, width):
    for axis, dim in sides:
        count = lax.axis_size(axis)
        forward = [(i, i + 1) for i in range(count - 1)]
        forward.append((count - 1, 0))
        backward = [(target, source) for source, target in forward]
        low = lax.ppermute(
            lax.slice_in_dim(block, block.shape[dim] - width, None, axis=dim), axis, forward
        )
        high = lax.ppermute(lax.slice_in_dim(block, 0, width, axis=dim), axis, backward)
        block = jnp.concatenate([low, block, high], axis=dim)
    return block


def passed_along(block, axis, distance):
    devices = range(lax.axis_size(axis))
    route = [(i - distance, i) for i in devices if i - distance in devices]
    return lax.ppermute(block, axis, route)


def one_axis_at_a_time(array, axes):
    return functools.reduce(lax.psum, axes, array)


def time_tables(step_count):
    positions = jnp.arange(step_count).astype(jnp.float32)
    pair_ids = jnp.arange(step_count // 2).astype(jnp.float32)
    phases = 2.0 * jnp.pi * pair_ids / step_count
    angles = phases[:, None] * positions[None, :]
    forward = jnp.stack([jnp.cos(angles), -jnp.sin(angles)], axis=1).reshape(step_count, step_count)
    row_id = jnp.arange(step_count)[:, None]
    forward = jnp.where(row_id == 1, jnp.cos(jnp.pi * positions)[None, :], forward)
    scaling = jnp.where(jnp.arange(step_count) < 2, 1.0, 2.0) / step_count
    inverse = forward.T * scaling[None, :]
    factor = circ_weight ** (1.0 / step_count)
    shift_pair = (1.0 - factor * jnp.cos(phases)) / time_step
    shifts = jnp.stack([shift_pair, shift_pair], axis=1).reshape(step_count)
    shifts = shifts.at[1].set((1.0 + factor) / time_step)
    coupling = factor * jnp.sin(phases) / time_step
    signed = jnp.stack([-coupling, coupling], axis=1).reshape(step_count)
    weights = circ_weight ** (positions / step_count)
    return (forward, inverse, shifts, signed, weights)


def neg_laplace(values):
    padded = padded_2(values, ((SPACE, 1),), 1)
    middle = padded[:, 1:-1, :]
    neighbours = padded[:, 2:, :] + padded[:, :-2, :]
    neighbours = neighbours + jnp.roll(middle, 1, axis=2) + jnp.roll(middle, -1, axis=2)
    return 4.0 * values - neighbours


def partner(values):
    extent = values.shape
    return jnp.flip(values.reshape(extent[0] // 2, 2, extent[1], extent[2]), axis=1).reshape(extent)


def make_sweep(spectrum, shifts, signed, frozen, mobility, laplace_fn):
    shift_col = shifts[:, None, None]
    signed_col = signed[:, None, None]
    diagonal = shift_col + (frozen + 4.0 * mobility)[None]
    partner_diag = partner(diagonal)
    denominator = diagonal * partner_diag + signed_col * signed_col

    def one_sweep(sweep_id, values):
        applied = (
            (shift_col + frozen[None]) * values
            + mobility[None] * laplace_fn(values)
            + signed_col * partner(values)
        )
        defect = spectrum - applied
        return (
            values + damping * (partner_diag * defect - signed_col * partner(defect)) / denominator
        )

    return one_sweep


def relax_pairs(spectrum, shifts, signed, frozen, mobility):
    one_sweep = make_sweep(spectrum, shifts, signed, frozen, mobility, neg_laplace)
    return lax.fori_loop(0, SWEEPS, one_sweep, jnp.zeros_like(spectrum))


def precondition(values, frozen, mobility, tables):
    forward, inverse, shifts, signed, weights = tables
    steps_dev = values.shape[0]
    time_rank = lax.axis_index(TM)
    offset = time_rank * steps_dev
    own_weights = lax.dynamic_slice_in_dim(weights, offset, steps_dev)
    own_shifts = lax.dynamic_slice_in_dim(shifts, offset, steps_dev)
    own_signed = lax.dynamic_slice_in_dim(signed, offset, steps_dev)
    weighted = own_weights[:, None, None] * values
    spectrum = jnp.einsum(
        "mj,jrc->mrc",
        forward,
        lax.all_to_all(weighted, TM, split_axis=1, concat_axis=0, tiled=True),
        precision=lax.Precision.HIGHEST,
    )
    owned_part = lax.all_to_all(spectrum, TM, split_axis=0, concat_axis=1, tiled=True)
    solved = relax_pairs(owned_part, own_shifts, own_signed, frozen, mobility)
    in_time = jnp.einsum(
        "jm,mrc->jrc",
        inverse,
        lax.all_to_all(solved, TM, split_axis=1, concat_axis=0, tiled=True),
        precision=lax.Precision.HIGHEST,
    )
    restored = lax.all_to_all(in_time, TM, split_axis=0, concat_axis=1, tiled=True)
    return restored / own_weights[:, None, None]


def jacobian(values, trajectory, mobility):
    arriving = passed_along(values[-1:], TM, 1)
    earlier = jnp.concatenate([arriving, values[:-1]], axis=0)
    reaction = reaction_scale * (3.0 * trajectory * trajectory - 1.0)
    return (values - earlier) / time_step + mobility[None] * neg_laplace(values) + reaction * values


def on_device(trajectory, initial_state, residual, mobility):
    tables = time_tables(NT)
    frozen = reaction_scale * jnp.maximum(3.0 * initial_state * initial_state - 1.0, 0.0)
    direction = precondition(residual, frozen, mobility, tables)
    applied = jacobian(direction, trajectory, mobility)
    norm_square, cross_sum, squared_applied = (
        one_axis_at_a_time(jnp.sum(residual * residual), TM_SPACE),
        one_axis_at_a_time(jnp.sum(residual * applied), TM_SPACE),
        one_axis_at_a_time(jnp.sum(applied * applied), TM_SPACE),
    )
    projection = cross_sum / norm_square
    squared_sum = squared_applied / norm_square
    remainder = jnp.maximum(squared_sum - projection * projection, 0.0)
    update = cross_sum / squared_applied * direction
    reduction = jnp.sqrt(remainder / squared_sum)
    return (update, reduction)


def solution(mesh):
    torus = Mesh(mesh.devices.reshape(4, 4, 4, 2), ("tm_0", "tm_1", "space_0", "space_1"))
    in_specs = (P(TM, SPACE, None), P(SPACE, None), P(TM, SPACE, None), P(SPACE, None))
    out_specs = (P(TM, SPACE, None), P())
    return jax.shard_map(
        on_device, mesh=torus, in_specs=in_specs, out_specs=out_specs, check_vma=False
    )
```

profile of v0, /device:TPU:6, one launch (start us, length us, event | category | flops | bytes accessed | tf_op | source)
XLA Modules:
  0.0 336.4 jit_solution(7587826208372566848)
XLA Ops:
  3.6 7.6 %all-to-all-start = ((f32[4,64,1024]{2,0,1:T(4,128)}), f32[4,64,1024]{2,0,1:T(4,128)S(1)}, u32[]{:S(2)}, u32[]{:S(2)}) async-start(f32[4,64,1024]{2,0,1:T(4,128)} %copy_multiply_fusion), calls=%async_computation | async-start | bytes 2097152 | tf_op jit(solution)/shard_map/all_to_all | solution.py:117
  13.7 12.7 %all-to-all-done = f32[4,64,1024]{2,0,1:T(4,128)S(1)} async-done(((f32[4,64,1024]{2,0,1:T(4,128)}), f32[4,64,1024]{2,0,1:T(4,128)S(1)}, u32[]{:S(2)}, u32[]{:S(2)}) %all-to-all-start) | async-done | bytes 1048608 | tf_op jit(solution)/shard_map/all_to_all | solution.py:117
  29.5 6.1 %all-to-all-start.1 = ((f32[64,4,1024]{2,1,0:T(4,128)}), f32[64,4,1024]{2,1,0:T(4,128)S(1)}, u32[]{:S(2)}, u32[]{:S(2)}) async-start(f32[64,4,1024]{2,1,0:T(4,128)} %copy.72), calls=%async_computation.1 | async-start | bytes 2097152 | tf_op jit(solution)/shard_map/all_to_all | solution.py:120
  39.7 9.3 %all-to-all-done.1 = f32[64,4,1024]{2,1,0:T(4,128)S(1)} async-done(((f32[64,4,1024]{2,1,0:T(4,128)}), f32[64,4,1024]{2,1,0:T(4,128)S(1)}, u32[]{:S(2)}, u32[]{:S(2)}) %all-to-all-start.1) | async-done | bytes 1048608 | tf_op jit(solution)/shard_map/all_to_all | solution.py:120
  50.5 181.2 %while.12 = (s32[]{:T(128)}, f32[4,64,1024]{2,1,0:T(8,128)S(1)}, f32[4,1,1]{0,2,1:T(1,128)S(1)}, f32[64,1024]{1,0:T(8,128)}, f32[64,1024]{1,0:T(8,128)}, /*index...) while((s32[]{:T(128)}, f32[4,64,1024]{2,1,0:T(8,128)S(1)}, ...), condition=%wide.region_1.2_spmd.clone, body=%wide.region_0.1_spmd.clone.sunk | while | flops 6291459 | bytes 23822584 | solution.py:102
  56.4 3.0 fusion.54
  67.7 3.0 fusion.54
  79.1 3.0 fusion.54
  90.4 3.0 fusion.54
  101.7 3.0 fusion.54
  113.0 3.0 fusion.54
  192.3 3.0 fusion.54
  203.7 3.0 fusion.54
  233.3 5.5 %all-to-all-start.2 = ((f32[4,64,1024]{2,0,1:T(4,128)}), f32[4,64,1024]{2,0,1:T(4,128)S(1)}, u32[]{:S(2)}, u32[]{:S(2)}) async-start(f32[4,64,1024]{2,0,1:T(4,128)} %copy.74), calls=%async_computation.2 | async-start | bytes 2097152 | tf_op jit(solution)/shard_map/all_to_all | solution.py:125
  238.9 13.1 %all-to-all-done.2 = f32[4,64,1024]{2,0,1:T(4,128)S(1)} async-done(((f32[4,64,1024]{2,0,1:T(4,128)}), f32[4,64,1024]{2,0,1:T(4,128)S(1)}, u32[]{:S(2)}, u32[]{:S(2)}) %all-to-all-start.2) | async-done | bytes 1048608 | tf_op jit(solution)/shard_map/all_to_all | solution.py:125
  255.2 5.7 %all-to-all-start.3 = ((f32[64,4,1024]{2,1,0:T(4,128)}), f32[64,4,1024]{2,1,0:T(4,128)S(1)}, u32[]{:S(2)}, u32[]{:S(2)}) async-start(f32[64,4,1024]{2,1,0:T(4,128)} %copy.77), calls=%async_computation.3 | async-start | bytes 2097152 | tf_op jit(solution)/shard_map/all_to_all | solution.py:128
  261.8 12.9 %all-to-all-done.3 = f32[64,4,1024]{2,1,0:T(4,128)S(1)} async-done(((f32[64,4,1024]{2,1,0:T(4,128)}), f32[64,4,1024]{2,1,0:T(4,128)S(1)}, u32[]{:S(2)}, u32[]{:S(2)}) %all-to-all-start.3) | async-done | bytes 1048608 | tf_op jit(solution)/shard_map/all_to_all | solution.py:128
  279.3 4.3 %collective-permute-start.3 = (f32[4,1,1024]{2,0,1:T(4,128)S(1)}, f32[4,1,1024]{2,0,1:T(4,128)S(1)}, u32[]{:S(2)}, u32[]{:S(2)}) collective-permute-start(f32[4,1,1024]{2,0,1:T(4,128)S(1)} %get-tuple-element.142), channel_id=1, source_target_pairs={{1,0},{2,1},{3,2},{4,3},{5,4},{6,5},{7,6},{0,7},{9,8},{10,9},{11,1... | collective-permute-start | bytes 49160 | tf_op jit(solution)/shard_map/ppermute | solution.py:31
  283.7 3.5 %collective-permute-done.2 = f32[1,64,1024]{2,1,0:T(8,128)S(1)} collective-permute-done((f32[1,64,1024]{2,1,0:T(8,128)S(1)}, f32[1,64,1024]{2,1,0:T(8,128)S(1)}, u32[]{:S(2)}, u32[]{:S(2)}) %collective-permute-start.2) | collective-permute-done | bytes 262176 | tf_op jit(solution)/shard_map/ppermute | solution.py:39
  288.0 5.8 %multiply_reduce_fusion.1 = (f32[]{:T(128)}, f32[]{:T(128)}) fusion(f32[4,64,1024]{2,1,0:T(8,128)S(1)} %copy-done, f32[4,64,1024]{2,0,1:T(4,128)S(1)} %bitcast_divide_fusion, f32[4,64,1024]{2,1,0:T(8,128)S(1)} %copy-done.1, f32[4,64,1]{2,0,1:T(4,128)S(1)} %get-tuple-element.140, f32[4,64,1023]{2,0,1:T(4,128)S(1)} %get-tuple-element.138, ...), kind=kLoop, calls=%fused_computation.36 | loop fusion | flops 6291454 | bytes 6586376 | tf_op jit(solution)/shard_map/reduce_sum | solution.py:147
  293.8 9.6 %all-reduce.2 = (f32[]{:T(128)}, f32[]{:T(128)}, f32[]{:T(128)}) all-reduce(f32[]{:T(128)} %get-tuple-element.101, f32[]{:T(128)} %get-tuple-element.100, f32[]{:T(128)} %multiply_reduce_fusion), channel_id=1, replica_groups=mesh['tm_0'=4,'tm_1'=4,'space_0'=4,'space_1'=2] {'tm_0'}, use_global_device_ids=true, to_apply=%region_3.4 | all-reduce | flops 3 | bytes 24 | tf_op jit(solution)/shard_map/psum | solution.py:43
  303.4 10.2 %all-reduce.1 = (f32[]{:T(128)}, f32[]{:T(128)}, f32[]{:T(128)}) all-reduce(f32[]{:T(128)} %get-tuple-element.126, f32[]{:T(128)} %get-tuple-element.127, f32[]{:T(128)} %get-tuple-element.128), channel_id=1, replica_groups=mesh['tm_0'=4,'tm_1'=4,'space_0'=4,'space_1'=2] {'tm_1'}, use_global_device_ids=true, to_apply=%region_4.5 | all-reduce | flops 3 | bytes 24 | tf_op jit(solution)/shard_map/psum | solution.py:43
  313.6 11.5 %all-reduce = (f32[]{:T(128)}, f32[]{:T(128)}, f32[]{:T(128)}) all-reduce(f32[]{:T(128)} %get-tuple-element.123, f32[]{:T(128)} %get-tuple-element.124, f32[]{:T(128)} %get-tuple-element.125), channel_id=1, replica_groups=mesh['tm_0'=4,'tm_1'=4,'space_0'=4,'space_1'=2] {'space_0'}, use_global_device_ids=true, to_apply=%region_5.6 | all-reduce | flops 3 | bytes 24 | tf_op jit(solution)/shard_map/psum | solution.py:43
  325.1 3.1 all-reduce.3
  (246 shorter events, 183.2 us)
Async XLA Ops:
  3.6 22.8 %all-to-all-start = ((f32[4,64,1024]{2,0,1:T(4,128)}), f32[4,64,1024]{2,0,1:T(4,128)S(1)}, u32[]{:S(2)}, u32[]{:S(2)}) async-start(f32[4,64,1024]{2,0,1:T(4,128)} %copy_multiply_fusion), calls=%async_computation | async-start | bytes 2097152 | tf_op jit(solution)/shard_map/all_to_all | solution.py:117
  29.5 19.5 %all-to-all-start.1 = ((f32[64,4,1024]{2,1,0:T(4,128)}), f32[64,4,1024]{2,1,0:T(4,128)S(1)}, u32[]{:S(2)}, u32[]{:S(2)}) async-start(f32[64,4,1024]{2,1,0:T(4,128)} %copy.72), calls=%async_computation.1 | async-start | bytes 2097152 | tf_op jit(solution)/shard_map/all_to_all | solution.py:120
  50.6 5.8 %collective-permute-start = (f32[4,1,1024]{2,1,0:T(1,128)S(1)}, f32[4,1,1024]{2,1,0:T(1,128)S(1)}, u32[]{:S(2)}, u32[]{:S(2)}) collective-permute-start(f32[4,1,1024]{2,1,0:T(1,128)S(1)} %get-tuple-element.217), channel_id=1, source_target_pairs={{0,1},{1,2},{2,3},{3,4},{4,5},{5,6},{6,7},{7,0},{8,9},{9,10},{10,1... | collective-permute-start | bytes 49160 | tf_op jit(solution)/shard_map/while/body/eval_jaxpr/ppermute | solution.py:28
  50.6 5.8 %collective-permute-start.1 = (f32[4,1,1024]{2,1,0:T(1,128)S(1)}, f32[4,1,1024]{2,1,0:T(1,128)S(1)}, u32[]{:S(2)}, u32[]{:S(2)}) collective-permute-start(f32[4,1,1024]{2,1,0:T(1,128)S(1)} %get-tuple-element.218), channel_id=1, source_target_pairs={{1,0},{2,1},{3,2},{4,3},{5,4},{6,5},{7,6},{0,7},{9,8},{10,9},{11,1... | collective-permute-start | bytes 49160 | tf_op jit(solution)/shard_map/while/body/eval_jaxpr/ppermute | solution.py:31
  61.9 5.8 %collective-permute-start = (f32[4,1,1024]{2,1,0:T(1,128)S(1)}, f32[4,1,1024]{2,1,0:T(1,128)S(1)}, u32[]{:S(2)}, u32[]{:S(2)}) collective-permute-start(f32[4,1,1024]{2,1,0:T(1,128)S(1)} %get-tuple-element.217), channel_id=1, source_target_pairs={{0,1},{1,2},{2,3},{3,4},{4,5},{5,6},{6,7},{7,0},{8,9},{9,10},{10,1... | collective-permute-start | bytes 49160 | tf_op jit(solution)/shard_map/while/body/eval_jaxpr/ppermute | solution.py:28
  62.0 5.8 %collective-permute-start.1 = (f32[4,1,1024]{2,1,0:T(1,128)S(1)}, f32[4,1,1024]{2,1,0:T(1,128)S(1)}, u32[]{:S(2)}, u32[]{:S(2)}) collective-permute-start(f32[4,1,1024]{2,1,0:T(1,128)S(1)} %get-tuple-element.218), channel_id=1, source_target_pairs={{1,0},{2,1},{3,2},{4,3},{5,4},{6,5},{7,6},{0,7},{9,8},{10,9},{11,1... | collective-permute-start | bytes 49160 | tf_op jit(solution)/shard_map/while/body/eval_jaxpr/ppermute | solution.py:31
  73.3 5.8 %collective-permute-start = (f32[4,1,1024]{2,1,0:T(1,128)S(1)}, f32[4,1,1024]{2,1,0:T(1,128)S(1)}, u32[]{:S(2)}, u32[]{:S(2)}) collective-permute-start(f32[4,1,1024]{2,1,0:T(1,128)S(1)} %get-tuple-element.217), channel_id=1, source_target_pairs={{0,1},{1,2},{2,3},{3,4},{4,5},{5,6},{6,7},{7,0},{8,9},{9,10},{10,1... | collective-permute-start | bytes 49160 | tf_op jit(solution)/shard_map/while/body/eval_jaxpr/ppermute | solution.py:28
  84.6 5.8 %collective-permute-start = (f32[4,1,1024]{2,1,0:T(1,128)S(1)}, f32[4,1,1024]{2,1,0:T(1,128)S(1)}, u32[]{:S(2)}, u32[]{:S(2)}) collective-permute-start(f32[4,1,1024]{2,1,0:T(1,128)S(1)} %get-tuple-element.217), channel_id=1, source_target_pairs={{0,1},{1,2},{2,3},{3,4},{4,5},{5,6},{6,7},{7,0},{8,9},{9,10},{10,1... | collective-permute-start | bytes 49160 | tf_op jit(solution)/shard_map/while/body/eval_jaxpr/ppermute | solution.py:28
  95.9 5.8 %collective-permute-start = (f32[4,1,1024]{2,1,0:T(1,128)S(1)}, f32[4,1,1024]{2,1,0:T(1,128)S(1)}, u32[]{:S(2)}, u32[]{:S(2)}) collective-permute-start(f32[4,1,1024]{2,1,0:T(1,128)S(1)} %get-tuple-element.217), channel_id=1, source_target_pairs={{0,1},{1,2},{2,3},{3,4},{4,5},{5,6},{6,7},{7,0},{8,9},{9,10},{10,1... | collective-permute-start | bytes 49160 | tf_op jit(solution)/shard_map/while/body/eval_jaxpr/ppermute | solution.py:28
  107.2 5.8 %collective-permute-start = (f32[4,1,1024]{2,1,0:T(1,128)S(1)}, f32[4,1,1024]{2,1,0:T(1,128)S(1)}, u32[]{:S(2)}, u32[]{:S(2)}) collective-permute-start(f32[4,1,1024]{2,1,0:T(1,128)S(1)} %get-tuple-element.217), channel_id=1, source_target_pairs={{0,1},{1,2},{2,3},{3,4},{4,5},{5,6},{6,7},{7,0},{8,9},{9,10},{10,1... | collective-permute-start | bytes 49160 | tf_op jit(solution)/shard_map/while/body/eval_jaxpr/ppermute | solution.py:28
  118.6 5.8 %collective-permute-start = (f32[4,1,1024]{2,1,0:T(1,128)S(1)}, f32[4,1,1024]{2,1,0:T(1,128)S(1)}, u32[]{:S(2)}, u32[]{:S(2)}) collective-permute-start(f32[4,1,1024]{2,1,0:T(1,128)S(1)} %get-tuple-element.217), channel_id=1, source_target_pairs={{0,1},{1,2},{2,3},{3,4},{4,5},{5,6},{6,7},{7,0},{8,9},{9,10},{10,1... | collective-permute-start | bytes 49160 | tf_op jit(solution)/shard_map/while/body/eval_jaxpr/ppermute | solution.py:28
  129.9 5.8 %collective-permute-start = (f32[4,1,1024]{2,1,0:T(1,128)S(1)}, f32[4,1,1024]{2,1,0:T(1,128)S(1)}, u32[]{:S(2)}, u32[]{:S(2)}) collective-permute-start(f32[4,1,1024]{2,1,0:T(1,128)S(1)} %get-tuple-element.217), channel_id=1, source_target_pairs={{0,1},{1,2},{2,3},{3,4},{4,5},{5,6},{6,7},{7,0},{8,9},{9,10},{10,1... | collective-permute-start | bytes 49160 | tf_op jit(solution)/shard_map/while/body/eval_jaxpr/ppermute | solution.py:28
  141.2 5.8 %collective-permute-start = (f32[4,1,1024]{2,1,0:T(1,128)S(1)}, f32[4,1,1024]{2,1,0:T(1,128)S(1)}, u32[]{:S(2)}, u32[]{:S(2)}) collective-permute-start(f32[4,1,1024]{2,1,0:T(1,128)S(1)} %get-tuple-element.217), channel_id=1, source_target_pairs={{0,1},{1,2},{2,3},{3,4},{4,5},{5,6},{6,7},{7,0},{8,9},{9,10},{10,1... | collective-permute-start | bytes 49160 | tf_op jit(solution)/shard_map/while/body/eval_jaxpr/ppermute | solution.py:28
  152.5 5.8 %collective-permute-start = (f32[4,1,1024]{2,1,0:T(1,128)S(1)}, f32[4,1,1024]{2,1,0:T(1,128)S(1)}, u32[]{:S(2)}, u32[]{:S(2)}) collective-permute-start(f32[4,1,1024]{2,1,0:T(1,128)S(1)} %get-tuple-element.217), channel_id=1, source_target_pairs={{0,1},{1,2},{2,3},{3,4},{4,5},{5,6},{6,7},{7,0},{8,9},{9,10},{10,1... | collective-permute-start | bytes 49160 | tf_op jit(solution)/shard_map/while/body/eval_jaxpr/ppermute | solution.py:28
  163.9 5.8 %collective-permute-start = (f32[4,1,1024]{2,1,0:T(1,128)S(1)}, f32[4,1,1024]{2,1,0:T(1,128)S(1)}, u32[]{:S(2)}, u32[]{:S(2)}) collective-permute-start(f32[4,1,1024]{2,1,0:T(1,128)S(1)} %get-tuple-element.217), channel_id=1, source_target_pairs={{0,1},{1,2},{2,3},{3,4},{4,5},{5,6},{6,7},{7,0},{8,9},{9,10},{10,1... | collective-permute-start | bytes 49160 | tf_op jit(solution)/shard_map/while/body/eval_jaxpr/ppermute | solution.py:28
  175.2 5.8 %collective-permute-start = (f32[4,1,1024]{2,1,0:T(1,128)S(1)}, f32[4,1,1024]{2,1,0:T(1,128)S(1)}, u32[]{:S(2)}, u32[]{:S(2)}) collective-permute-start(f32[4,1,1024]{2,1,0:T(1,128)S(1)} %get-tuple-element.217), channel_id=1, source_target_pairs={{0,1},{1,2},{2,3},{3,4},{4,5},{5,6},{6,7},{7,0},{8,9},{9,10},{10,1... | collective-permute-start | bytes 49160 | tf_op jit(solution)/shard_map/while/body/eval_jaxpr/ppermute | solution.py:28
  186.5 5.8 %collective-permute-start = (f32[4,1,1024]{2,1,0:T(1,128)S(1)}, f32[4,1,1024]{2,1,0:T(1,128)S(1)}, u32[]{:S(2)}, u32[]{:S(2)}) collective-permute-start(f32[4,1,1024]{2,1,0:T(1,128)S(1)} %get-tuple-element.217), channel_id=1, source_target_pairs={{0,1},{1,2},{2,3},{3,4},{4,5},{5,6},{6,7},{7,0},{8,9},{9,10},{10,1... | collective-permute-start | bytes 49160 | tf_op jit(solution)/shard_map/while/body/eval_jaxpr/ppermute | solution.py:28
  197.9 5.8 %collective-permute-start = (f32[4,1,1024]{2,1,0:T(1,128)S(1)}, f32[4,1,1024]{2,1,0:T(1,128)S(1)}, u32[]{:S(2)}, u32[]{:S(2)}) collective-permute-start(f32[4,1,1024]{2,1,0:T(1,128)S(1)} %get-tuple-element.217), channel_id=1, source_target_pairs={{0,1},{1,2},{2,3},{3,4},{4,5},{5,6},{6,7},{7,0},{8,9},{9,10},{10,1... | collective-permute-start | bytes 49160 | tf_op jit(solution)/shard_map/while/body/eval_jaxpr/ppermute | solution.py:28
  209.2 5.8 %collective-permute-start = (f32[4,1,1024]{2,1,0:T(1,128)S(1)}, f32[4,1,1024]{2,1,0:T(1,128)S(1)}, u32[]{:S(2)}, u32[]{:S(2)}) collective-permute-start(f32[4,1,1024]{2,1,0:T(1,128)S(1)} %get-tuple-element.217), channel_id=1, source_target_pairs={{0,1},{1,2},{2,3},{3,4},{4,5},{5,6},{6,7},{7,0},{8,9},{9,10},{10,1... | collective-permute-start | bytes 49160 | tf_op jit(solution)/shard_map/while/body/eval_jaxpr/ppermute | solution.py:28
  220.5 5.8 %collective-permute-start = (f32[4,1,1024]{2,1,0:T(1,128)S(1)}, f32[4,1,1024]{2,1,0:T(1,128)S(1)}, u32[]{:S(2)}, u32[]{:S(2)}) collective-permute-start(f32[4,1,1024]{2,1,0:T(1,128)S(1)} %get-tuple-element.217), channel_id=1, source_target_pairs={{0,1},{1,2},{2,3},{3,4},{4,5},{5,6},{6,7},{7,0},{8,9},{9,10},{10,1... | collective-permute-start | bytes 49160 | tf_op jit(solution)/shard_map/while/body/eval_jaxpr/ppermute | solution.py:28
  233.3 18.7 %all-to-all-start.2 = ((f32[4,64,1024]{2,0,1:T(4,128)}), f32[4,64,1024]{2,0,1:T(4,128)S(1)}, u32[]{:S(2)}, u32[]{:S(2)}) async-start(f32[4,64,1024]{2,0,1:T(4,128)} %copy.74), calls=%async_computation.2 | async-start | bytes 2097152 | tf_op jit(solution)/shard_map/all_to_all | solution.py:125
  255.2 19.5 %all-to-all-start.3 = ((f32[64,4,1024]{2,1,0:T(4,128)}), f32[64,4,1024]{2,1,0:T(4,128)S(1)}, u32[]{:S(2)}, u32[]{:S(2)}) async-start(f32[64,4,1024]{2,1,0:T(4,128)} %copy.77), calls=%async_computation.3 | async-start | bytes 2097152 | tf_op jit(solution)/shard_map/all_to_all | solution.py:128
  276.8 10.4 %collective-permute-start.2 = (f32[1,64,1024]{2,1,0:T(8,128)S(1)}, f32[1,64,1024]{2,1,0:T(8,128)S(1)}, u32[]{:S(2)}, u32[]{:S(2)}) collective-permute-start(f32[1,64,1024]{2,1,0:T(8,128)S(1)} %copy.79), channel_id=1, source_target_pairs={{0,8},{8,16},{16,24},{24,32},{32,40},{40,48},{48,56},{56,64},{64,7... | collective-permute-start | bytes 786440 | tf_op jit(solution)/shard_map/ppermute | solution.py:39
  279.3 8.2 %collective-permute-start.3 = (f32[4,1,1024]{2,0,1:T(4,128)S(1)}, f32[4,1,1024]{2,0,1:T(4,128)S(1)}, u32[]{:S(2)}, u32[]{:S(2)}) collective-permute-start(f32[4,1,1024]{2,0,1:T(4,128)S(1)} %get-tuple-element.142), channel_id=1, source_target_pairs={{1,0},{2,1},{3,2},{4,3},{5,4},{6,5},{7,6},{0,7},{9,8},{10,9},{11,1... | collective-permute-start | bytes 49160 | tf_op jit(solution)/shard_map/ppermute | solution.py:31
  (18 other events, 110.7 us)
where the time goes:
time: 342 us; the launch traced here: 336 us
  other arithmetic  101 us (30%)
  starting transfers between devices  79 us (23%)
  local copies, waits for them, and re-layouts  59.9 us (18%)
  waiting for transfers between devices  52 us (15%)
  blocking collectives  34.4 us (10%)
  between operations  7.14 us (2%)
    ppermute x17, starting transfers between devices, padded_2(): lax.ppermute(lax.slice_in_dim(block, 0, width, axis=dim), axis, backward)  51.4 us
    sub x16, other arithmetic, one_sweep(): defect = spectrum - applied  48.7 us
    add x16, other arithmetic, one_sweep(): values + damping * (partner_diag * defect - signed_col * partner(defect))...  35.2 us
    psum x4, blocking collectives, one_axis_at_a_time(): return functools.reduce(lax.psum, axes, array)  34.4 us
    slice x34, local copies, waits for them, and re-layouts, neg_laplace(): jnp.roll(middle, -1, axis=2)  29.2 us
    rev x33, local copies, waits for them, and re-layouts, partner(): jnp.flip(values.reshape(extent[0] // 2, 2, extent[1], extent[2]), axis=1)  19.3 us
    all_to_all x1, waiting for transfers between devices, precondition(): lax.all_to_all(solved, TM, split_axis=1, concat_axis=0, tiled=True)  13.1 us
    all_to_all x1, waiting for transfers between devices, precondition(): lax.all_to_all(in_time, TM, split_axis=0, concat_axis=1, tiled=True)  12.9 us
  transfers between devices with their start and end apart: 39, of which 6 were waited for; matrix products, arithmetic and copies ran while one was open for 16% of the time, Pallas kernels for 0%

commit v1 on v0

v1 whole, which is shorter than its diff:
```python
import functools

import jax
import jax.numpy as jnp
import ml_dtypes
import numpy as np
from jax import lax
from jax.experimental import pallas as pl
from jax.experimental.pallas import tpu as pltpu
from jax.sharding import Mesh
from jax.sharding import PartitionSpec as P

NT = 64
SPACE = ("space_0", "space_1")
TM = ("tm_0", "tm_1")
NTM = 16
NSP = 8
STEPS = NT // NTM
ROWS = 64
COLS = 1024
HALO = 16
WIDE = ROWS + 2 * HALO
PAD = WIDE + 8
FIRST = HALO - 1
KEPT = ROWS + 2
GROUPS = 4
BLOCK = 8
GROUP_SETS = ((0, 1), (2, 3))

circ_weight = 0.2
time_step = 0.01
reaction_scale = 40.0

F32 = jnp.float32
BF16 = jnp.bfloat16
VMEM_LIMIT = 56 * 1024 * 1024


def time_tables():
    steps = np.arange(NT)
    theta = 2.0 * np.pi * np.arange(NT // 2) / NT
    angles = theta[:, None] * steps[None, :]
    forward = np.stack([np.cos(angles), -np.sin(angles)], axis=1).reshape(NT, NT)
    forward[1] = np.cos(np.pi * steps)
    inverse = forward.T * (np.where(steps < 2, 1.0, 2.0) / NT)[None, :]
    factor = circ_weight ** (1.0 / NT)
    shifts = np.repeat((1.0 - factor * np.cos(theta)) / time_step, 2)
    shifts[1] = (1.0 + factor) / time_step
    coupling = np.repeat(-factor * np.sin(theta) / time_step, 2)
    weights = circ_weight ** (steps / NT)
    step_order = np.array([4 * src + q for q in range(4) for src in range(16)])
    coef_order = np.array(
        [2 * (8 * g + p) + half for g in range(GROUPS) for half in range(2) for p in range(8)]
    )
    forward = (forward * weights[None, :])[coef_order][:, step_order]
    inverse = (inverse / weights[:, None])[step_order][:, coef_order]
    wide = lambda v: np.repeat(v[coef_order][:, None], 128, axis=1).astype(np.float32)
    return split_matrix(forward), split_matrix(inverse), wide(shifts), wide(coupling)


def split_matrix(matrix):
    high = matrix.astype(ml_dtypes.bfloat16)
    low = (matrix - high.astype(np.float64)).astype(ml_dtypes.bfloat16)
    return np.concatenate([high, high, low, low], axis=1)


def transform(matrix, values):
    high = values.astype(BF16)
    low = (values - high.astype(F32)).astype(BF16)
    stacked = jnp.concatenate([high, low, high, low], axis=0)
    return jnp.dot(matrix, stacked, preferred_element_type=F32)


def lanes(rows=8):
    return lax.broadcasted_iota(jnp.int32, (rows, 128), 1)


def roll(values, shift):
    shift %= 128
    return values if shift == 0 else pltpu.roll(values, shift, 1)


def pack_kernel(with_halo, in_ref, out_ref):
    lane = lanes()
    low_half = lane < 64
    slot = lane // 16

    def rows_body(i, _):
        rows = pl.ds(pl.multiple_of(i * 8, 8), 8)
        v = [[in_ref[t, rows, 128 * k : 128 * k + 128] for k in range(8)] for t in range(4)]
        for b in range(NTM):
            k = b // 2
            for j in range(2):
                first, second = v[2 * j][k], v[2 * j + 1][k]
                if b % 2 == 0:
                    second = roll(second, 64)
                else:
                    first = roll(first, 64)
                out_ref[b, j, rows, :] = jnp.where(low_half, first, second)
            if with_halo:
                halo = None
                for t in range(4):
                    if b % 2 == 0:
                        both = jnp.where(lane < 112, v[t][k], v[t][(k - 1) % 8])
                        both = roll(both, (2 * t - 4) * 16)
                    else:
                        both = jnp.where(lane < 16, v[t][(k + 1) % 8], v[t][k])
                        both = roll(both, 2 * t * 16)
                    if halo is None:
                        halo = both
                    else:
                        mine = (slot == 2 * t) | (slot == (2 * t + 3) % 8)
                        halo = jnp.where(mine, both, halo)
                out_ref[b, 2, rows, :] = halo
        return 0

    lax.fori_loop(0, ROWS // 8, rows_body, 0)


def pack(array, with_halo):
    slabs = 3 if with_halo else 2
    return pl.pallas_call(
        functools.partial(pack_kernel, with_halo),
        out_shape=jax.ShapeDtypeStruct((NTM, slabs, ROWS, 128), F32),
        compiler_params=pltpu.CompilerParams(vmem_limit_bytes=VMEM_LIMIT),
        name="pack_halo" if with_halo else "pack",
    )(array)


def steps_tile(ref, row, rows, slabs, low_half):
    tiles = []
    loaded = [ref[pl.ds(row + rows * j, NTM, stride=rows * slabs), :] for j in range(slabs)]
    for q in range(4):
        own = roll(loaded[q // 2], 64 * (q % 2))
        if slabs == 3:
            own = jnp.where(low_half, own, roll(loaded[2], 64 - 32 * q))
        tiles.append(own)
    return jnp.concatenate(tiles, axis=0)


def solve_kernel(
    x_ref, low_ref, high_ref, mob_ref, ini_ref, fwd_ref, inv_ref, shift_ref, couple_ref,
    out_ref, dir_ref, s_ref, u_ref, w_ref, p_ref, q_ref, pb_ref,
):
    low_half = lanes(NTM) < 64

    def spectrum(source, rows, offset):
        def pair_body(i, _):
            first = 2 * i
            x = jnp.concatenate(
                [steps_tile(source, first + e, rows, 3, low_half) for e in range(2)], axis=1
            )
            coefs = transform(fwd_ref[...], x)
            for e in range(2):
                row = first + e + offset
                mob = jnp.broadcast_to(mob_ref[pl.ds(row, 1), :], (8, 128))
                ini = jnp.broadcast_to(ini_ref[pl.ds(row, 1), :], (8, 128))
                frozen = reaction_scale * jnp.maximum(3.0 * ini * ini - 1.0, 0.0)
                base = frozen + 4.0 * mob
                for g in range(GROUPS):
                    a, b = 16 * g, 16 * g + 8
                    s_a = coefs[a : a + 8, 128 * e : 128 * e + 128]
                    s_b = coefs[b : b + 8, 128 * e : 128 * e + 128]
                    c = couple_ref[a : a + 8, :]
                    diag_a = shift_ref[a : a + 8, :] + base
                    diag_b = shift_ref[b : b + 8, :] + base if g == 0 else diag_a
                    scale = 0.8 / (diag_a * diag_b + c * c)
                    k_a = diag_b * scale
                    k_b = diag_a * scale
                    k_c = c * scale
                    s_ref[row, a : a + 8, :] = k_a * s_a - k_c * s_b
                    s_ref[row, b : b + 8, :] = k_b * s_b + k_c * s_a
                    mob5 = 5.0 * mob
                    p_ref[row, 8 * g : 8 * g + 8, :] = mob5 * k_a
                    q_ref[row, 8 * g : 8 * g + 8, :] = mob5 * k_c
                    if g == 0:
                        pb_ref[row, :, :] = mob5 * k_b
            return 0

        lax.fori_loop(0, rows // 2, pair_body, 0)

    spectrum(low_ref, HALO, 0)
    spectrum(x_ref, ROWS, HALO)
    spectrum(high_ref, HALO, HALO + ROWS)

    def apply(k, source, target, join=None, old=None):
        count = WIDE - 2 * k

        for groups in GROUP_SETS:
            tiles = [16 * g + 8 * half for g in groups for half in range(2)]

            def load(row):
                return [source[row, m : m + 8, :] for m in tiles]

            def diagonal(here, below):
                return [h + roll(b, -1) for h, b in zip(here, below)]

            def body(i, carry):
                here, diag = carry
                start = k + i * BLOCK
                for e in range(BLOCK):
                    row = start + e
                    below = load(row + 1)
                    diag_now = diagonal(here, below)
                    n = [up + roll(d, 1) for up, d in zip(diag, diag_now)]
                    for j, g in enumerate(groups):
                        n_a, n_b = n[2 * j], n[2 * j + 1]
                        p = p_ref[row, 8 * g : 8 * g + 8, :]
                        q = q_ref[row, 8 * g : 8 * g + 8, :]
                        p_b = pb_ref[row, :, :] if g == 0 else p
                        new = [
                            here[2 * j] + (p * n_a - q * n_b),
                            here[2 * j + 1] + (p_b * n_b + q * n_a),
                        ]
                        for half in range(2):
                            m = tiles[2 * j + half]
                            value = new[half]
                            if join is not None:
                                kept = here[2 * j + half] if old is source else old[row, m : m + 8, :]
                                value = kept + join * value
                            target[row, m : m + 8, :] = value
                    here, diag = below, diag_now
                return here, diag

            above, here = load(k - 1), load(k)
            lax.fori_loop(0, -(-count // BLOCK), body, (list(here), diagonal(above, here)))

    apply(1, s_ref, u_ref, 0.2, s_ref)
    k = 1
    for power in (2, 4, 8):
        source = u_ref
        for step in range(power - 1):
            k += 1
            target = (s_ref, w_ref)[step % 2]
            apply(k, source, target)
            source = target
        k += 1
        apply(k, source, u_ref, 0.2**power, u_ref)

    def back_body(i, _):
        y = jnp.concatenate([u_ref[FIRST + 2 * i + e] for e in range(2)], axis=1)
        values = transform(inv_ref[...], y)
        for e in range(2):
            dir_ref[2 * i + e] = values[:, 128 * e : 128 * e + 128]
        return 0

    lax.fori_loop(0, KEPT // 2, back_body, 0)

    def out_body(r, _):
        v = dir_ref[r + 1]
        for j in range(2):
            first = v[32 * j : 32 * j + 16]
            second = roll(v[32 * j + 16 : 32 * j + 32], 64)
            out_ref[pl.ds(r + ROWS * j, NTM, stride=2 * ROWS), :] = jnp.where(low_half, first, second)
        return 0

    lax.fori_loop(0, ROWS, out_body, 0)


def solve(x, low, high, mob, ini):
    forward, inverse, shifts, coupling = time_tables()
    wide = pltpu.VMEM((PAD, NT, 128), F32)
    half = pltpu.VMEM((PAD, NT // 2, 128), F32)
    return pl.pallas_call(
        solve_kernel,
        out_shape=(
            jax.ShapeDtypeStruct((NTM * 2 * ROWS, 128), F32),
            jax.ShapeDtypeStruct((KEPT, NT, 128), F32),
        ),
        scratch_shapes=[wide, wide, wide, half, half, pltpu.VMEM((PAD, 8, 128), F32)],
        compiler_params=pltpu.CompilerParams(vmem_limit_bytes=VMEM_LIMIT),
        name="solve",
    )(x, low, high, mob, ini, forward, inverse, shifts, coupling)


def jacobian_kernel(dir_ref, traj_ref, x_ref, mob_ref, out_ref):
    first_row = lax.broadcasted_iota(jnp.int32, (NTM, 128), 0) == 0

    def own(ref, row, slabs):
        loaded = [ref[pl.ds(row + ROWS * j, NTM, stride=ROWS * slabs), :] for j in range(2)]
        return jnp.concatenate([roll(loaded[q // 2], 64 * (q % 2)) for q in range(4)], axis=0)

    def fold(values):
        return functools.reduce(jnp.add, [values[8 * i : 8 * i + 8] for i in range(8)])

    def body(r, sums):
        v = dir_ref[r + 1]
        neighbours = (dir_ref[r] + dir_ref[r + 2]) + (roll(v, 1) + roll(v, -1))
        carried = jnp.where(first_row, 0.0, pltpu.roll(v[48:64], 1, 0))
        earlier = jnp.concatenate([carried, v[:48]], axis=0)
        mob = mob_ref[pl.ds(r + HALO, 1), :]
        traj = own(traj_ref, r, 2)
        res = own(x_ref, r, 3)
        reaction = reaction_scale * (3.0 * traj * traj - 1.0)
        applied = (v - earlier) / time_step + mob * (4.0 * v - neighbours) + reaction * v
        new = (res * res, res * applied, applied * applied)
        return tuple(s + fold(n) for s, n in zip(sums, new))

    zero = jnp.zeros((8, 128), F32)
    sums = lax.fori_loop(0, ROWS, body, (zero, zero, zero))
    totals = [jnp.sum(jnp.where(lanes() < 64, s, 0.0)) for s in sums]
    row = lax.broadcasted_iota(jnp.int32, (8, 128), 0)
    out_ref[...] = jnp.where(row == 0, totals[0], jnp.where(row == 1, totals[1], totals[2]))


def jacobian_sums(direction, traj, x, mob):
    return pl.pallas_call(
        jacobian_kernel,
        out_shape=jax.ShapeDtypeStruct((8, 128), F32),
        compiler_params=pltpu.CompilerParams(vmem_limit_bytes=VMEM_LIMIT),
        name="jacobian_sums",
    )(direction, traj, x, mob)


def finish_kernel(blocks_ref, sums_ref, out_ref):
    low_half = lanes() < 64
    row = lambda i: jnp.broadcast_to(sums_ref[i : i + 1, :], (8, 128))
    scale = row(1) / row(2)

    def body(i, _):
        rows = pl.ds(pl.multiple_of(i * 8, 8), 8)
        for k in range(8):
            for j in range(2):
                even = blocks_ref[2 * k, j, rows, :] * scale
                odd = blocks_ref[2 * k + 1, j, rows, :] * scale
                lane = slice(128 * k, 128 * k + 128)
                out_ref[2 * j, rows, lane] = jnp.where(low_half, even, roll(odd, 64))
                out_ref[2 * j + 1, rows, lane] = jnp.where(low_half, roll(even, 64), odd)
        return 0

    lax.fori_loop(0, ROWS // 8, body, 0)


def finish(blocks, sums):
    return pl.pallas_call(
        finish_kernel,
        out_shape=jax.ShapeDtypeStruct((STEPS, ROWS, COLS), F32),
        compiler_params=pltpu.CompilerParams(vmem_limit_bytes=VMEM_LIMIT),
        name="finish",
    )(blocks, sums)


def swap(blocks):
    return lax.all_to_all(blocks, TM, split_axis=0, concat_axis=0, tiled=True)


def shifted(array, axes, size, distance):
    return lax.ppermute(array, axes, [(i, (i + distance) % size) for i in range(size)])


def row_halos(array, dim):
    last = lax.slice_in_dim(array, ROWS - HALO, ROWS, axis=dim)
    first = lax.slice_in_dim(array, 0, HALO, axis=dim)
    return shifted(last, SPACE, NSP, 1), shifted(first, SPACE, NSP, -1)


def own_columns(array):
    block = lax.axis_index(TM)
    padded = jnp.concatenate([array[:, :, -128:], array, array[:, :, :128]], axis=2)
    here = lax.dynamic_slice_in_dim(padded, 64 * block + 128, 128, axis=2)
    before = lax.dynamic_slice_in_dim(padded, 64 * block, 128, axis=2)
    return jnp.where(jnp.arange(128) < 112, here, before)


def total(sums):
    sums = sums + shifted(sums, "space_1", 2, 1)
    for axis in ("space_0", "tm_1", "tm_0"):
        one, two, three = (shifted(sums, axis, 4, d) for d in (1, 2, 3))
        sums = (sums + two) + (one + three)
    return sums


def on_device(trajectory, initial_state, residual, mobility):
    x = swap(pack(residual, True))
    low, high = row_halos(x, 2)
    fields = own_columns(jnp.stack([mobility, initial_state]))
    below, above = row_halos(fields, 1)
    mob, ini = jnp.concatenate([below, fields, above], axis=1)
    traj = swap(pack(trajectory, False))
    flat = lambda a: a.reshape(-1, 128)
    packed, direction = solve(flat(x), flat(low), flat(high), mob, ini)
    blocks = swap(packed.reshape(NTM, 2, ROWS, 128))
    sums = total(jacobian_sums(direction, flat(traj), flat(x), mob))
    norm_square, cross_sum, squared_applied = sums[0, 0], sums[1, 0], sums[2, 0]
    projection = cross_sum / norm_square
    squared_sum = squared_applied / norm_square
    remainder = jnp.maximum(squared_sum - projection * projection, 0.0)
    return finish(blocks, sums), jnp.sqrt(remainder / squared_sum)


def solution(mesh):
    torus = Mesh(mesh.devices.reshape(4, 4, 4, 2), TM + SPACE)
    in_specs = (P(TM, SPACE, None), P(SPACE, None), P(TM, SPACE, None), P(SPACE, None))
    out_specs = (P(TM, SPACE, None), P())
    return jax.shard_map(
        on_device, mesh=torus, in_specs=in_specs, out_specs=out_specs, check_vma=False
    )
```

time: 342 us -> 186 us (0.54); the launches traced: 336 us -> 186 us
  Pallas kernels: 0 us -> 102 us
  other arithmetic: 101 us -> 0.87 us
  local copies, waits for them, and re-layouts: 59.9 us -> 3.18 us
  starting transfers between devices: 79 us -> 37 us
  blocking collectives: 34.4 us -> 0 us
  waiting for transfers between devices: 52 us -> 36.6 us
    pallas_call x0 -> x5, Pallas kernels: none -> 102 us  [the longest x1 82.4 us: solve(): pl.pallas_call(solve_kernel, out_shape=(jax.ShapeDtypeStruct((NTM * 2 * R...]
    sub x16 -> x0, other arithmetic: 48.7 us -> none  [one_sweep(): defect = spectrum - applied]
    add x19 -> x4, other arithmetic: 39.6 us -> 0.7 us  [the longest x1 0.68 us: total(): sums = sums + shifted(sums, 'space_1', 2, 1)]
    ppermute x35 -> x14, starting transfers between devices: 54.1 us -> 16.2 us  [shifted(): lax.ppermute(array, axes, [(i, (i + distance) % size) for i in range(size)])]
    psum x4 -> x0, blocking collectives: 34.4 us -> none  [one_axis_at_a_time(): return functools.reduce(lax.psum, axes, array)]
    all_to_all x4 -> x3, waiting for transfers between devices: 48 us -> 18.4 us  [swap(): return lax.all_to_all(blocks, TM, split_axis=0, concat_axis=0, tiled=True)]
    slice x53 -> x3, local copies, waits for them, and re-layouts: 30 us -> 0.66 us  [the longest x1 0.59 us: on_device(): sums[1, 0]]
    rev x33 -> x0, local copies, waits for them, and re-layouts: 19.3 us -> none  [partner(): jnp.flip(values.reshape(extent[0] // 2, 2, extent[1], extent[2]), axis=1)]
  transfers between devices with their start and end apart: 39 -> 17, of which waited for: 6 -> 10; matrix products, arithmetic and copies ran while one was open for 16% -> 1% of each run, Pallas kernels for 0% -> 52%
where the time goes in v1:
time: 186 us
  Pallas kernels  102 us (55%)
  starting transfers between devices  37 us (20%)
  waiting for transfers between devices  36.6 us (20%)
  between operations  5.68 us (3%)
  local copies, waits for them, and re-layouts  3.18 us (2%)
    pallas_call x1, Pallas kernels, solve(): pl.pallas_call(solve_kernel, out_shape=(jax.ShapeDtypeStruct((NTM * 2 * R...  82.4 us
    all_to_all x3, starting transfers between devices, swap(): return lax.all_to_all(blocks, TM, split_axis=0, concat_axis=0, tiled=True)  20.8 us
    all_to_all x3, waiting for transfers between devices, swap(): return lax.all_to_all(blocks, TM, split_axis=0, concat_axis=0, tiled=True)  18.4 us
    ppermute x14, waiting for transfers between devices, shifted(): lax.ppermute(array, axes, [(i, (i + distance) % size) for i in range(size)])  18.3 us
    ppermute x14, starting transfers between devices, shifted(): lax.ppermute(array, axes, [(i, (i + distance) % size) for i in range(size)])  16.2 us
    pallas_call x1, Pallas kernels, jacobian_sums(): pl.pallas_call(jacobian_kernel, out_shape=jax.ShapeDtypeStruct((8, 128),...  10.2 us
    pallas_call x2, Pallas kernels, pack(): pl.pallas_call(functools.partial(pack_kernel, with_halo), out_shape=jax.S...  6.72 us
  transfers between devices with their start and end apart: 17, of which 10 were waited for; matrix products, arithmetic and copies ran while one was open for 1% of the time, Pallas kernels for 52%

profile of v1, /device:TPU:6, one launch (start us, length us, event | category | flops | bytes accessed | tf_op | source)
XLA Modules:
  0.0 185.7 jit_solution(1781783033449109368)
XLA Ops:
  0.6 3.6 %pack_halo.1 = f32[16,3,64,128]{3,2,1,0:T(8,128)} custom-call(f32[4,64,1024]{2,1,0:T(8,128)} %in_ref.2), custom_call_target="tpu_custom_call" | custom-call | tf_op jit(solution)/shard_map/pack_halo/pallas_call | solution.py:122
  4.3 7.4 %all-to-all-start = ((f32[16,3,64,128]{3,2,1,0:T(8,128)}), f32[16,3,64,128]{3,2,1,0:T(8,128)S(1)}, u32[]{:S(2)}, u32[]{:S(2)}) async-start(f32[16,3,64,128]{3,2,1,0:T(8,128)} %pack_halo.1), calls=%async_computation | async-start | bytes 3145728 | tf_op jit(solution)/shard_map/all_to_all | solution.py:344
  11.7 3.1 %pack.1 = f32[16,2,64,128]{3,2,1,0:T(8,128)} custom-call(f32[4,64,1024]{2,1,0:T(8,128)} %in_ref.3), custom_call_target="tpu_custom_call" | custom-call | tf_op jit(solution)/shard_map/pack/pallas_call | solution.py:122
  14.9 18.3 %all-to-all-done = f32[16,3,64,128]{3,2,1,0:T(8,128)S(1)} async-done(((f32[16,3,64,128]{3,2,1,0:T(8,128)}), f32[16,3,64,128]{3,2,1,0:T(8,128)S(1)}, u32[]{:S(2)}, u32[]{:S(2)}) %all-to-all-start) | async-done | bytes 1572896 | tf_op jit(solution)/shard_map/all_to_all | solution.py:344
  33.2 6.1 %all-to-all-start.2 = ((f32[16,2,64,128]{3,2,1,0:T(8,128)}), f32[16,2,64,128]{3,2,1,0:T(8,128)S(1)}, u32[]{:S(2)}, u32[]{:S(2)}) async-start(f32[16,2,64,128]{3,2,1,0:T(8,128)} %pack.1), calls=%async_computation.2 | async-start | bytes 2097152 | tf_op jit(solution)/shard_map/all_to_all | solution.py:344
  39.6 1.2 collective-permute-start.1
  41.6 2.1 %collective-permute-start.3 = (f32[2,16,128]{2,1,0:T(8,128)S(1)}, f32[2,16,128]{2,1,0:T(8,128)S(1)}, u32[]{:S(2)}, u32[]{:S(2)}) collective-permute-start(f32[2,16,128]{2,1,0:T(8,128)S(1)} %get-tuple-element.11), channel_id=1, source_target_pairs={{0,7},{1,0},{2,1},{3,2},{4,3},{5,4},{6,5},{7,6},{8,15},{9,8},{10,9... | collective-permute-start | bytes 49160 | tf_op jit(solution)/shard_map/ppermute | solution.py:348
  43.8 5.6 %collective-permute-done.2 = f32[2,16,128]{2,1,0:T(8,128)S(1)} collective-permute-done((f32[2,16,128]{2,1,0:T(8,128)S(1)}, f32[2,16,128]{2,1,0:T(8,128)S(1)}, u32[]{:S(2)}, u32[]{:S(2)}) %collective-permute-start.2) | collective-permute-done | bytes 16416 | tf_op jit(solution)/shard_map/ppermute | solution.py:348
  50.9 82.4 %solve.1 = (f32[2048,128]{1,0:T(8,128)}, f32[66,64,128]{2,1,0:T(8,128)}) custom-call(f32[3072,128]{1,0:T(8,128)} %bitcast.14, f32[768,128]{1,0:T(8,128)} %bitcast.19, f32[768,128]{1,0:T(8,128)} %bitcast.18, f32[96,128]{1,0:T(8,128)} %get-tuple-element.9.mob_ref, f32[96,128]{1,0:T(8,128)} %get-tuple-element.8.ini_ref, ...), custom_call_target="tpu_custom_call" | custom-call | tf_op jit(solution)/shard_map/solve/pallas_call | solution.py:264
  133.4 7.2 %all-to-all-start.1 = ((f32[16,2,64,128]{3,2,1,0:T(8,128)}), f32[16,2,64,128]{3,2,1,0:T(8,128)S(1)}, u32[]{:S(2)}, u32[]{:S(2)}) async-start(f32[16,2,64,128]{3,2,1,0:T(8,128)} %bitcast.17), calls=%async_computation.1 | async-start | bytes 2097152 | tf_op jit(solution)/shard_map/all_to_all | solution.py:344
  140.6 10.2 %jacobian_sums.1 = f32[8,128]{1,0:T(8,128)} custom-call(f32[66,64,128]{2,1,0:T(8,128)} %get-tuple-element.5.dir_ref, f32[2048,128]{1,0:T(8,128)} %bitcast.16, f32[3072,128]{1,0:T(8,128)} %bitcast.15, f32[96,128]{1,0:T(8,128)} %get-tuple-element.9.mob_ref), custom_call_target="tpu_custom_call" | custom-call | tf_op jit(solution)/shard_map/jacobian_sums/pallas_call | solution.py:307
  150.8 1.4 collective-permute-done.4
  152.8 1.6 collective-permute-start.7
  154.9 1.5 collective-permute-start.5
  156.5 2.8 %collective-permute-done.6 = f32[8,128]{1,0:T(8,128)S(1)} collective-permute-done((f32[8,128]{1,0:T(8,128)S(1)}, f32[8,128]{1,0:T(8,128)S(1)}, u32[]{:S(2)}, u32[]{:S(2)}) %collective-permute-start.6) | collective-permute-done | bytes 4128 | tf_op jit(solution)/shard_map/ppermute | solution.py:348
  160.0 2.7 %collective-permute-start.10 = (f32[8,128]{1,0:T(8,128)S(1)}, f32[8,128]{1,0:T(8,128)S(1)}, u32[]{:S(2)}, u32[]{:S(2)}) collective-permute-start(f32[8,128]{1,0:T(8,128)S(1)} %add_add_fusion.2), channel_id=1, source_target_pairs={{0,24},{8,0},{16,8},{24,16},{1,25},{9,1},{17,9},{25,17},{2,26},{10... | collective-permute-start | bytes 12296 | tf_op jit(solution)/shard_map/ppermute | solution.py:348
  162.7 2.3 %collective-permute-start.8 = (f32[8,128]{1,0:T(8,128)S(1)}, f32[8,128]{1,0:T(8,128)S(1)}, u32[]{:S(2)}, u32[]{:S(2)}) collective-permute-start(f32[8,128]{1,0:T(8,128)S(1)} %add_add_fusion.2), channel_id=1, source_target_pairs={{0,16},{8,24},{16,0},{24,8},{1,17},{9,25},{17,1},{25,9},{2,18},{10... | collective-permute-start | bytes 12296 | tf_op jit(solution)/shard_map/ppermute | solution.py:348
  165.0 2.5 %collective-permute-done.9 = f32[8,128]{1,0:T(8,128)S(1)} collective-permute-done((f32[8,128]{1,0:T(8,128)S(1)}, f32[8,128]{1,0:T(8,128)S(1)}, u32[]{:S(2)}, u32[]{:S(2)}) %collective-permute-start.9) | collective-permute-done | bytes 4128 | tf_op jit(solution)/shard_map/ppermute | solution.py:348
  167.8 0.9 collective-permute-start.13
  168.6 2.4 %collective-permute-start.12 = (f32[8,128]{1,0:T(8,128)S(1)}, f32[8,128]{1,0:T(8,128)S(1)}, u32[]{:S(2)}, u32[]{:S(2)}) collective-permute-start(f32[8,128]{1,0:T(8,128)S(1)} %add_add_fusion.1), channel_id=1, source_target_pairs={{0,32},{32,64},{64,96},{96,0},{1,33},{33,65},{65,97},{97,1},{2,34}... | collective-permute-start | bytes 12296 | tf_op jit(solution)/shard_map/ppermute | solution.py:348
  171.3 1.3 collective-permute-done.13
  172.6 3.5 %collective-permute-done.11 = f32[8,128]{1,0:T(8,128)S(1)} collective-permute-done((f32[8,128]{1,0:T(8,128)S(1)}, f32[8,128]{1,0:T(8,128)S(1)}, u32[]{:S(2)}, u32[]{:S(2)}) %collective-permute-start.11) | collective-permute-done | bytes 4128 | tf_op jit(solution)/shard_map/ppermute | solution.py:348
  180.6 1.0 copy-done.1
  181.5 3.0 %finish.1 = f32[4,64,1024]{2,1,0:T(8,128)} custom-call(f32[16,2,64,128]{3,2,1,0:T(8,128)} %copy-done.1, f32[8,128]{1,0:T(8,128)} %copy-done.7), custom_call_target="tpu_custom_call" | custom-call | tf_op jit(solution)/shard_map/finish/pallas_call | solution.py:335
  (43 shorter events, 5.7 us)
Async XLA Ops:
  4.3 28.9 %all-to-all-start = ((f32[16,3,64,128]{3,2,1,0:T(8,128)}), f32[16,3,64,128]{3,2,1,0:T(8,128)S(1)}, u32[]{:S(2)}, u32[]{:S(2)}) async-start(f32[16,3,64,128]{3,2,1,0:T(8,128)} %pack_halo.1), calls=%async_computation | async-start | bytes 3145728 | tf_op jit(solution)/shard_map/all_to_all | solution.py:344
  11.7 3.1 %copy-start.5 = (f32[64,1024]{1,0:T(8,128)S(1)}, f32[64,1024]{1,0:T(8,128)}, u32[]{:S(2)}) copy-start(f32[64,1024]{1,0:T(8,128)} %param.9) | copy-start | bytes 786436
  11.7 3.1 %copy-start.6 = (f32[64,1024]{1,0:T(8,128)S(1)}, f32[64,1024]{1,0:T(8,128)}, u32[]{:S(2)}) copy-start(f32[64,1024]{1,0:T(8,128)} %param.11) | copy-start | bytes 786436
  33.2 6.3 %copy-start = (f32[16,3,64,128]{3,2,1,0:T(8,128)}, f32[16,3,64,128]{3,2,1,0:T(8,128)S(1)}, u32[]{:S(2)}) copy-start(f32[16,3,64,128]{3,2,1,0:T(8,128)S(1)} %all-to-all-done) | copy-start | bytes 4718596
  33.2 100.1 %all-to-all-start.2 = ((f32[16,2,64,128]{3,2,1,0:T(8,128)}), f32[16,2,64,128]{3,2,1,0:T(8,128)S(1)}, u32[]{:S(2)}, u32[]{:S(2)}) async-start(f32[16,2,64,128]{3,2,1,0:T(8,128)} %pack.1), calls=%async_computation.2 | async-start | bytes 2097152 | tf_op jit(solution)/shard_map/all_to_all | solution.py:344
  39.6 10.5 %collective-permute-start.1 = (f32[16,3,16,128]{3,2,1,0:T(8,128)S(1)}, f32[16,3,16,128]{3,2,1,0:T(8,128)S(1)}, u32[]{:S(2)}, u32[]{:S(2)}) collective-permute-start(f32[16,3,16,128]{3,2,1,0:T(8,128)S(1)} %get-tuple-element.6), channel_id=1, source_target_pairs={{0,7},{1,0},{2,1},{3,2},{4,3},{5,4},{6,5},{7,6},{8,15},{9,8},{10,9... | collective-permute-start | bytes 1179656 | tf_op jit(solution)/shard_map/ppermute | solution.py:348
  40.8 9.3 %collective-permute-start = (f32[16,3,16,128]{3,2,1,0:T(8,128)S(1)}, f32[16,3,16,128]{3,2,1,0:T(8,128)S(1)}, u32[]{:S(2)}, u32[]{:S(2)}) collective-permute-start(f32[16,3,16,128]{3,2,1,0:T(8,128)S(1)} %get-tuple-element.7), channel_id=1, source_target_pairs={{0,1},{1,2},{2,3},{3,4},{4,5},{5,6},{6,7},{7,0},{8,9},{9,10},{10,1... | collective-permute-start | bytes 1179656 | tf_op jit(solution)/shard_map/ppermute | solution.py:348
  40.8 8.6 %collective-permute-start.2 = (f32[2,16,128]{2,1,0:T(8,128)S(1)}, f32[2,16,128]{2,1,0:T(8,128)S(1)}, u32[]{:S(2)}, u32[]{:S(2)}) collective-permute-start(f32[2,16,128]{2,1,0:T(8,128)S(1)} %get-tuple-element.10), channel_id=1, source_target_pairs={{0,1},{1,2},{2,3},{3,4},{4,5},{5,6},{6,7},{7,0},{8,9},{9,10},{10,1... | collective-permute-start | bytes 49160 | tf_op jit(solution)/shard_map/ppermute | solution.py:348
  41.6 7.7 %collective-permute-start.3 = (f32[2,16,128]{2,1,0:T(8,128)S(1)}, f32[2,16,128]{2,1,0:T(8,128)S(1)}, u32[]{:S(2)}, u32[]{:S(2)}) collective-permute-start(f32[2,16,128]{2,1,0:T(8,128)S(1)} %get-tuple-element.11), channel_id=1, source_target_pairs={{0,7},{1,0},{2,1},{3,2},{4,3},{5,4},{6,5},{7,6},{8,15},{9,8},{10,9... | collective-permute-start | bytes 49160 | tf_op jit(solution)/shard_map/ppermute | solution.py:348
  50.1 0.9 copy-start.4
  133.4 7.2 %copy-start.2 = (f32[16,2,64,128]{3,2,1,0:T(8,128)}, f32[16,2,64,128]{3,2,1,0:T(8,128)S(1)}, u32[]{:S(2)}) copy-start(f32[16,2,64,128]{3,2,1,0:T(8,128)S(1)} %all-to-all-done.2) | copy-start | bytes 3145732
  133.4 47.1 %all-to-all-start.1 = ((f32[16,2,64,128]{3,2,1,0:T(8,128)}), f32[16,2,64,128]{3,2,1,0:T(8,128)S(1)}, u32[]{:S(2)}, u32[]{:S(2)}) async-start(f32[16,2,64,128]{3,2,1,0:T(8,128)} %bitcast.17), calls=%async_computation.1 | async-start | bytes 2097152 | tf_op jit(solution)/shard_map/all_to_all | solution.py:344
  150.8 1.4 collective-permute-start.4
  152.8 3.6 %collective-permute-start.7 = (f32[8,128]{1,0:T(8,128)S(1)}, f32[8,128]{1,0:T(8,128)S(1)}, u32[]{:S(2)}, u32[]{:S(2)}) collective-permute-start(f32[8,128]{1,0:T(8,128)S(1)} %add.48), channel_id=1, source_target_pairs={{0,6},{2,0},{4,2},{6,4},{1,7},{3,1},{5,3},{7,5},{8,14},{10,8},{12,... | collective-permute-start | bytes 12296 | tf_op jit(solution)/shard_map/ppermute | solution.py:348
  154.5 4.8 %collective-permute-start.6 = (f32[8,128]{1,0:T(8,128)S(1)}, f32[8,128]{1,0:T(8,128)S(1)}, u32[]{:S(2)}, u32[]{:S(2)}) collective-permute-start(f32[8,128]{1,0:T(8,128)S(1)} %add.48), channel_id=1, source_target_pairs={{0,2},{2,4},{4,6},{6,0},{1,3},{3,5},{5,7},{7,1},{8,10},{10,12},{12... | collective-permute-start | bytes 12296 | tf_op jit(solution)/shard_map/ppermute | solution.py:348
  154.9 5.1 %collective-permute-start.5 = (f32[8,128]{1,0:T(8,128)S(1)}, f32[8,128]{1,0:T(8,128)S(1)}, u32[]{:S(2)}, u32[]{:S(2)}) collective-permute-start(f32[8,128]{1,0:T(8,128)S(1)} %add.48), channel_id=1, source_target_pairs={{0,4},{2,6},{4,0},{6,2},{1,5},{3,7},{5,1},{7,3},{8,12},{10,14},{12... | collective-permute-start | bytes 12296 | tf_op jit(solution)/shard_map/ppermute | solution.py:348
  160.0 5.0 %collective-permute-start.10 = (f32[8,128]{1,0:T(8,128)S(1)}, f32[8,128]{1,0:T(8,128)S(1)}, u32[]{:S(2)}, u32[]{:S(2)}) collective-permute-start(f32[8,128]{1,0:T(8,128)S(1)} %add_add_fusion.2), channel_id=1, source_target_pairs={{0,24},{8,0},{16,8},{24,16},{1,25},{9,1},{17,9},{25,17},{2,26},{10... | collective-permute-start | bytes 12296 | tf_op jit(solution)/shard_map/ppermute | solution.py:348
  162.7 4.8 %collective-permute-start.9 = (f32[8,128]{1,0:T(8,128)S(1)}, f32[8,128]{1,0:T(8,128)S(1)}, u32[]{:S(2)}, u32[]{:S(2)}) collective-permute-start(f32[8,128]{1,0:T(8,128)S(1)} %add_add_fusion.2), channel_id=1, source_target_pairs={{0,8},{8,16},{16,24},{24,0},{1,9},{9,17},{17,25},{25,1},{2,10},{10... | collective-permute-start | bytes 12296 | tf_op jit(solution)/shard_map/ppermute | solution.py:348
  162.7 5.1 %collective-permute-start.8 = (f32[8,128]{1,0:T(8,128)S(1)}, f32[8,128]{1,0:T(8,128)S(1)}, u32[]{:S(2)}, u32[]{:S(2)}) collective-permute-start(f32[8,128]{1,0:T(8,128)S(1)} %add_add_fusion.2), channel_id=1, source_target_pairs={{0,16},{8,24},{16,0},{24,8},{1,17},{9,25},{17,1},{25,9},{2,18},{10... | collective-permute-start | bytes 12296 | tf_op jit(solution)/shard_map/ppermute | solution.py:348
  167.8 4.8 %collective-permute-start.13 = (f32[8,128]{1,0:T(8,128)S(1)}, f32[8,128]{1,0:T(8,128)S(1)}, u32[]{:S(2)}, u32[]{:S(2)}) collective-permute-start(f32[8,128]{1,0:T(8,128)S(1)} %add_add_fusion.1), channel_id=1, source_target_pairs={{0,96},{32,0},{64,32},{96,64},{1,97},{33,1},{65,33},{97,65},{2,98}... | collective-permute-start | bytes 12296 | tf_op jit(solution)/shard_map/ppermute | solution.py:348
  168.6 4.0 %collective-permute-start.12 = (f32[8,128]{1,0:T(8,128)S(1)}, f32[8,128]{1,0:T(8,128)S(1)}, u32[]{:S(2)}, u32[]{:S(2)}) collective-permute-start(f32[8,128]{1,0:T(8,128)S(1)} %add_add_fusion.1), channel_id=1, source_target_pairs={{0,32},{32,64},{64,96},{96,0},{1,33},{33,65},{65,97},{97,1},{2,34}... | collective-permute-start | bytes 12296 | tf_op jit(solution)/shard_map/ppermute | solution.py:348
  171.0 5.1 %collective-permute-start.11 = (f32[8,128]{1,0:T(8,128)S(1)}, f32[8,128]{1,0:T(8,128)S(1)}, u32[]{:S(2)}, u32[]{:S(2)}) collective-permute-start(f32[8,128]{1,0:T(8,128)S(1)} %add_add_fusion.1), channel_id=1, source_target_pairs={{0,64},{32,96},{64,0},{96,32},{1,65},{33,97},{65,1},{97,33},{2,66}... | collective-permute-start | bytes 12296 | tf_op jit(solution)/shard_map/ppermute | solution.py:348
  176.1 4.4 %copy-start.7 = (f32[8,128]{1,0:T(8,128)}, f32[8,128]{1,0:T(8,128)S(1)}, u32[]{:S(2)}) copy-start(f32[8,128]{1,0:T(8,128)S(1)} %add_add_fusion.sums_ref) | copy-start | bytes 12292
  180.5 1.0 copy-start.1
  (1 other events, 0.8 us)

commit v2 on v1

v2 whole, which is shorter than its diff:
```python
import functools

import jax
import jax.numpy as jnp
import ml_dtypes
import numpy as np
from jax import lax
from jax.experimental import pallas as pl
from jax.experimental.pallas import tpu as pltpu
from jax.sharding import Mesh
from jax.sharding import PartitionSpec as P

NT = 64
SPACE = ("space_0", "space_1")
TM = ("tm_0", "tm_1")
NTM = 16
NSP = 8
STEPS = NT // NTM
ROWS = 64
COLS = 1024
HALO = 16
WIDE = ROWS + 2 * HALO
PAD = WIDE + 16
FIRST = HALO - 1
KEPT = ROWS + 2
GROUPS = 4
BLOCK = 16
BATCH = 8
JBATCH = 4

circ_weight = 0.2
time_step = 0.01
reaction_scale = 40.0

F32 = jnp.float32
BF16 = jnp.bfloat16
VMEM_LIMIT = 56 * 1024 * 1024


def time_tables():
    steps = np.arange(NT)
    theta = 2.0 * np.pi * np.arange(NT // 2) / NT
    angles = theta[:, None] * steps[None, :]
    forward = np.stack([np.cos(angles), -np.sin(angles)], axis=1).reshape(NT, NT)
    forward[1] = np.cos(np.pi * steps)
    inverse = forward.T * (np.where(steps < 2, 1.0, 2.0) / NT)[None, :]
    factor = circ_weight ** (1.0 / NT)
    shifts = np.repeat((1.0 - factor * np.cos(theta)) / time_step, 2)
    shifts[1] = (1.0 + factor) / time_step
    coupling = np.repeat(-factor * np.sin(theta) / time_step, 2)
    weights = circ_weight ** (steps / NT)
    step_order = np.array([4 * src + q for q in range(4) for src in range(16)])
    coef_order = np.array(
        [2 * (8 * g + p) + half for g in range(GROUPS) for half in range(2) for p in range(8)]
    )
    forward = (forward * weights[None, :])[coef_order][:, step_order]
    inverse = (inverse / weights[:, None])[step_order][:, coef_order]
    by_pair = lambda v: np.repeat(v.reshape(GROUPS, 8).T, 32, axis=1)
    coefs = [by_pair(shifts[0::2]), by_pair(shifts[1::2]), by_pair(coupling[0::2])]
    return split_matrix(forward), split_matrix(inverse), np.stack(coefs).astype(np.float32)


def split_matrix(matrix):
    high = matrix.astype(ml_dtypes.bfloat16)
    low = (matrix - high.astype(np.float64)).astype(ml_dtypes.bfloat16)
    return np.concatenate([high, high, low, low], axis=1)


def transform(matrix, values):
    high = values.astype(BF16)
    low = (values - high.astype(F32)).astype(BF16)
    stacked = jnp.concatenate([high, low, high, low], axis=0)
    return jnp.dot(matrix, stacked, preferred_element_type=F32)


def lanes(rows=8):
    return lax.broadcasted_iota(jnp.int32, (rows, 128), 1)


def roll(values, shift):
    shift %= 128
    return values if shift == 0 else pltpu.roll(values, shift, 1)


def permute_lanes(values, index):
    return jnp.take_along_axis(values, index, axis=1, mode="promise_in_bounds")


def pack_kernel(in_ref, out_ref):
    low_half = lanes() < 64

    def rows_body(i, _):
        rows = pl.ds(pl.multiple_of(i * 8, 8), 8)
        for k in range(8):
            for j in range(2):
                lane = slice(128 * k, 128 * k + 128)
                first, second = in_ref[2 * j, rows, lane], in_ref[2 * j + 1, rows, lane]
                out_ref[2 * k, j, rows, :] = jnp.where(low_half, first, roll(second, 64))
                out_ref[2 * k + 1, j, rows, :] = jnp.where(low_half, roll(first, 64), second)
        return 0

    lax.fori_loop(0, ROWS // 8, rows_body, 0)


def pack_halo_kernel(in_ref, out_ref):
    lane = lanes()
    slot, q = lane // 32, lane % 32

    def rows_body(i, _):
        rows = pl.ds(pl.multiple_of(i * 8, 8), 8)
        for odd in range(2):
            base = 48 if odd else -16
            index = [(3 * q + jnp.where(slot < 3, slot, j) + base) & 127 for j in range(3)]
            for b in range(odd, NTM, 2):
                k = b // 2
                both = []
                for t in range(4):
                    v = lambda k: in_ref[t, rows, 128 * (k % 8) : 128 * (k % 8) + 128]
                    if odd:
                        both.append(jnp.where(lane < 16, v(k + 1), v(k)))
                    else:
                        both.append(jnp.where(lane < 112, v(k), v(k - 1)))
                for j in range(3):
                    source = permute_lanes(both[j], index[j])
                    out_ref[b, j, rows, :] = jnp.where(
                        slot < 3, source, permute_lanes(both[3], index[j])
                    )
        return 0

    lax.fori_loop(0, ROWS // 8, rows_body, 0)


def pack(array, kernel, slabs, name):
    return pl.pallas_call(
        kernel,
        out_shape=jax.ShapeDtypeStruct((NTM, slabs, ROWS, 128), F32),
        compiler_params=pltpu.CompilerParams(vmem_limit_bytes=VMEM_LIMIT),
        name=name,
    )(array)


def halo_tiles(ref, row, rows, slot):
    slabs = [ref[pl.ds(row + rows * j, NTM, stride=3 * rows), :] for j in range(3)]
    last = jnp.where(slot == 0, roll(slabs[0], 32), jnp.where(slot == 1, roll(slabs[1], 64), roll(slabs[2], 96)))
    return slabs + [last]


def swap_blocks(d, slot, count):
    low_half, even = slot < 2, slot % 2 == 0
    d0 = jnp.where(low_half, d[0], roll(d[2], 64))
    d1 = jnp.where(low_half, d[1], roll(d[3], 64))
    d2 = jnp.where(low_half, roll(d[0], 64), d[2])
    d3 = jnp.where(low_half, roll(d[1], 64), d[3])
    out = [
        jnp.where(even, d0, roll(d1, 32)),
        jnp.where(even, roll(d0, -32), d1),
        jnp.where(even, d2, roll(d3, 32)),
    ]
    if count == 4:
        out.append(jnp.where(even, roll(d2, -32), d3))
    return out


def natural_index(rows):
    lane = lanes(rows)
    column = jnp.where(lane < 80, lane + 16, jnp.where(lane < 112, 0, lane - 112))
    return 32 * (column % 3) + column // 3


def solve_kernel(
    x_ref, low_ref, high_ref, mob_ref, ini_ref, fwd_ref, inv_ref, coef_ref,
    out_ref, dir_ref, s_ref, u_ref, w_ref, pa_ref, pb_ref, q_ref,
):
    slot = lanes() // 32
    slot16 = lanes(NTM) // 32

    def spectrum(source, rows, offset):
        def body(i, _):
            first = i * BATCH
            x = [
                jnp.concatenate(halo_tiles(source, first + e, rows, slot16), axis=0)
                for e in range(BATCH)
            ]
            coefs = transform(fwd_ref[...], jnp.concatenate(x, axis=1))
            c = coef_ref[2]
            for e in range(BATCH):
                row = first + e + offset
                here = coefs[:, 128 * e : 128 * e + 128]
                parts = [
                    swap_blocks([here[16 * g + 8 * h : 16 * g + 8 * h + 8] for g in range(4)], slot, 3)
                    for h in range(2)
                ]
                for k in range(3):
                    mob = jnp.broadcast_to(mob_ref[k, pl.ds(row, 1), :], (8, 128))
                    ini = jnp.broadcast_to(ini_ref[k, pl.ds(row, 1), :], (8, 128))
                    frozen = reaction_scale * jnp.maximum(3.0 * ini * ini - 1.0, 0.0)
                    base = frozen + 4.0 * mob
                    diag_a = coef_ref[0] + base
                    diag_b = coef_ref[1] + base
                    scale = 0.8 / (diag_a * diag_b + c * c)
                    k_a, k_b, k_c = diag_b * scale, diag_a * scale, c * scale
                    s_a, s_b = parts[0][k], parts[1][k]
                    s_ref[row, 16 * k : 16 * k + 8, :] = k_a * s_a - k_c * s_b
                    s_ref[row, 16 * k + 8 : 16 * k + 16, :] = k_b * s_b + k_c * s_a
                    mob5 = 5.0 * mob
                    tile = slice(8 * k, 8 * k + 8)
                    pa_ref[row, tile, :] = mob5 * k_a
                    pb_ref[row, tile, :] = mob5 * k_b
                    q_ref[row, tile, :] = mob5 * k_c
            return 0

        lax.fori_loop(0, rows // BATCH, body, 0)

    spectrum(low_ref, HALO, 0)
    spectrum(x_ref, ROWS, HALO)
    spectrum(high_ref, HALO, HALO + ROWS)

    def apply(k, source, target, join=None, old=None):
        count = WIDE - 2 * k

        def load(row):
            return [source[row, 8 * m : 8 * m + 8, :] for m in range(6)]

        def body(i, carry):
            above, here = carry
            start = k + i * BLOCK
            for e in range(BLOCK):
                row = start + e
                below = load(row + 1)
                n = [a + b for a, b in zip(above, below)]
                for h in range(2):
                    t0, t1, t2 = here[h], here[2 + h], here[4 + h]
                    n[h] += roll(t2, 1) + t1
                    n[2 + h] += t0 + t2
                    n[4 + h] += t1 + roll(t0, -1)
                for j in range(3):
                    tile = slice(8 * j, 8 * j + 8)
                    p_a, p_b, q = pa_ref[row, tile, :], pb_ref[row, tile, :], q_ref[row, tile, :]
                    n_a, n_b = n[2 * j], n[2 * j + 1]
                    new = [
                        here[2 * j] + (p_a * n_a - q * n_b),
                        here[2 * j + 1] + (p_b * n_b + q * n_a),
                    ]
                    for h in range(2):
                        m = slice(16 * j + 8 * h, 16 * j + 8 * h + 8)
                        value = new[h]
                        if join is not None:
                            kept = here[2 * j + h] if old is source else old[row, m, :]
                            value = kept + join * value
                        target[row, m, :] = value
                above, here = here, below
            return above, here

        lax.fori_loop(0, -(-count // BLOCK), body, (load(k - 1), load(k)))

    apply(1, s_ref, u_ref, 0.2, s_ref)
    k = 1
    for power in (2, 4, 8):
        source = u_ref
        for step in range(power - 1):
            k += 1
            target = (s_ref, w_ref)[step % 2]
            apply(k, source, target)
            source = target
        k += 1
        apply(k, source, u_ref, 0.2**power, u_ref)

    natural = natural_index(NT)
    low_half = lanes(NTM) < 64

    def back(rows):
        y = []
        for row in rows:
            halves = []
            for h in range(2):
                t = [u_ref[row + FIRST, 16 * k + 8 * h : 16 * k + 8 * h + 8, :] for k in range(3)]
                halves.append(swap_blocks(t + [t[2]], slot, 4))
            y.append(jnp.concatenate([halves[h][g] for g in range(4) for h in range(2)], axis=0))
        values = transform(inv_ref[...], jnp.concatenate(y, axis=1))
        out = []
        for e, row in enumerate(rows):
            v = permute_lanes(values[:, 128 * e : 128 * e + 128], natural)
            dir_ref[row] = v
            out.append(v)
        return out

    back([0, KEPT - 1])

    def back_body(i, _):
        for e, v in enumerate(back([i * BATCH + e + 1 for e in range(BATCH)])):
            for j in range(2):
                both = jnp.where(low_half, v[32 * j : 32 * j + 16], roll(v[32 * j + 16 : 32 * j + 32], 64))
                out_ref[pl.ds(i * BATCH + e + ROWS * j, NTM, stride=2 * ROWS), :] = both
        return 0

    lax.fori_loop(0, ROWS // BATCH, back_body, 0)


def solve(x, low, high, mob, ini):
    wide = pltpu.VMEM((PAD, 48, 128), F32)
    half = pltpu.VMEM((PAD, 24, 128), F32)
    return pl.pallas_call(
        solve_kernel,
        out_shape=(
            jax.ShapeDtypeStruct((NTM * 2 * ROWS, 128), F32),
            jax.ShapeDtypeStruct((KEPT, NT, 128), F32),
        ),
        scratch_shapes=[wide, wide, wide, half, half, half],
        compiler_params=pltpu.CompilerParams(vmem_limit_bytes=VMEM_LIMIT),
        name="solve",
    )(x, low, high, mob, ini, *time_tables())


def jacobian_kernel(dir_ref, traj_ref, x_ref, mob_ref, out_ref):
    first_row = lax.broadcasted_iota(jnp.int32, (NTM, 128), 0) == 0

    natural = natural_index(NT)
    slot = lanes(NTM) // 32

    def own(ref, row):
        slabs = [ref[pl.ds(row + ROWS * j, NTM, stride=2 * ROWS), :] for j in range(2)]
        return jnp.concatenate([roll(slabs[q // 2], 64 * (q % 2)) for q in range(4)], axis=0)

    def fold(values):
        return functools.reduce(jnp.add, [values[8 * i : 8 * i + 8] for i in range(8)])

    def one_row(r):
        v = dir_ref[r + 1]
        neighbours = (dir_ref[r] + dir_ref[r + 2]) + (roll(v, 1) + roll(v, -1))
        carried = jnp.where(first_row, 0.0, pltpu.roll(v[48:64], 1, 0))
        earlier = jnp.concatenate([carried, v[:48]], axis=0)
        mob = mob_ref[pl.ds(r + HALO, 1), :]
        traj = own(traj_ref, r)
        res = jnp.concatenate(halo_tiles(x_ref, r, ROWS, slot), axis=0)
        res = permute_lanes(res, natural)
        reaction = reaction_scale * (3.0 * traj * traj - 1.0)
        applied = (v - earlier) / time_step + mob * (4.0 * v - neighbours) + reaction * v
        return [fold(p) for p in (res * res, res * applied, applied * applied)]

    def body(i, sums):
        parts = [one_row(i * JBATCH + e) for e in range(JBATCH)]
        return tuple(s + functools.reduce(jnp.add, p) for s, p in zip(sums, zip(*parts)))

    zero = jnp.zeros((8, 128), F32)
    sums = lax.fori_loop(0, ROWS // JBATCH, body, (zero, zero, zero))
    totals = [jnp.sum(jnp.where(lanes() < 64, s, 0.0)) for s in sums]
    row = lax.broadcasted_iota(jnp.int32, (8, 128), 0)
    out_ref[...] = jnp.where(row == 0, totals[0], jnp.where(row == 1, totals[1], totals[2]))


def jacobian_sums(direction, traj, x, mob):
    return pl.pallas_call(
        jacobian_kernel,
        out_shape=jax.ShapeDtypeStruct((8, 128), F32),
        compiler_params=pltpu.CompilerParams(vmem_limit_bytes=VMEM_LIMIT),
        name="jacobian_sums",
    )(direction, traj, x, mob)


def finish_kernel(blocks_ref, sums_ref, out_ref):
    low_half = lanes() < 64
    row = lambda i: jnp.broadcast_to(sums_ref[i : i + 1, :], (8, 128))
    scale = row(1) / row(2)

    def body(i, _):
        rows = pl.ds(pl.multiple_of(i * 8, 8), 8)
        for k in range(8):
            for j in range(2):
                even = blocks_ref[2 * k, j, rows, :] * scale
                odd = blocks_ref[2 * k + 1, j, rows, :] * scale
                lane = slice(128 * k, 128 * k + 128)
                out_ref[2 * j, rows, lane] = jnp.where(low_half, even, roll(odd, 64))
                out_ref[2 * j + 1, rows, lane] = jnp.where(low_half, roll(even, 64), odd)
        return 0

    lax.fori_loop(0, ROWS // 8, body, 0)


def finish(blocks, sums):
    return pl.pallas_call(
        finish_kernel,
        out_shape=jax.ShapeDtypeStruct((STEPS, ROWS, COLS), F32),
        compiler_params=pltpu.CompilerParams(vmem_limit_bytes=VMEM_LIMIT),
        name="finish",
    )(blocks, sums)


def swap(blocks):
    return lax.all_to_all(blocks, TM, split_axis=0, concat_axis=0, tiled=True)


def shifted(array, axes, size, distance):
    return lax.ppermute(array, axes, [(i, (i + distance) % size) for i in range(size)])


def row_halos(array, dim):
    last = lax.slice_in_dim(array, ROWS - HALO, ROWS, axis=dim)
    first = lax.slice_in_dim(array, 0, HALO, axis=dim)
    return shifted(last, SPACE, NSP, 1), shifted(first, SPACE, NSP, -1)


def own_columns(array):
    block = lax.axis_index(TM)
    padded = jnp.concatenate([array[:, :, -HALO:], array, array[:, :, : HALO + 32]], axis=2)
    return lax.dynamic_slice_in_dim(padded, 64 * block, 128, axis=2)


def by_thirds(field):
    thirds = field[:, :96].reshape(WIDE, 32, 3).transpose(2, 0, 1)
    return jnp.concatenate([thirds] * GROUPS, axis=2)


def total(sums):
    sums = sums + shifted(sums, "space_1", 2, 1)
    for axis in ("space_0", "tm_1", "tm_0"):
        one, two, three = (shifted(sums, axis, 4, d) for d in (1, 2, 3))
        sums = (sums + two) + (one + three)
    return sums


def on_device(trajectory, initial_state, residual, mobility):
    x = swap(pack(residual, pack_halo_kernel, 3, "pack_halo"))
    low, high = row_halos(x, 2)
    fields = own_columns(jnp.stack([mobility, initial_state]))
    below, above = row_halos(fields, 1)
    mob, ini = jnp.concatenate([below, fields, above], axis=1)
    traj = swap(pack(trajectory, pack_kernel, 2, "pack"))
    flat = lambda a: a.reshape(-1, 128)
    packed, direction = solve(flat(x), flat(low), flat(high), by_thirds(mob), by_thirds(ini))
    blocks = swap(packed.reshape(NTM, 2, ROWS, 128))
    sums = total(jacobian_sums(direction, flat(traj), flat(x), jnp.roll(mob, -HALO, axis=1)))
    norm_square, cross_sum, squared_applied = sums[0, 0], sums[1, 0], sums[2, 0]
    projection = cross_sum / norm_square
    squared_sum = squared_applied / norm_square
    remainder = jnp.maximum(squared_sum - projection * projection, 0.0)
    return finish(blocks, sums), jnp.sqrt(remainder / squared_sum)


def solution(mesh):
    torus = Mesh(mesh.devices.reshape(4, 4, 4, 2), TM + SPACE)
    in_specs = (P(TM, SPACE, None), P(SPACE, None), P(TM, SPACE, None), P(SPACE, None))
    out_specs = (P(TM, SPACE, None), P())
    return jax.shard_map(
        on_device, mesh=torus, in_specs=in_specs, out_specs=out_specs, check_vma=False
    )
```

time: 186 us -> 132 us (0.71)
  Pallas kernels: 102 us -> 45 us
  waiting for transfers between devices: 36.6 us -> 33.2 us
  other arithmetic: 0.87 us -> 3.35 us
    pallas_call x1, Pallas kernels: 82.4 us -> 26 us  [solve(): pl.pallas_call(solve_kernel, out_shape=(jax.ShapeDtypeStruct((NTM * 2 * R...]
    ppermute x14, waiting for transfers between devices: 18.3 us -> 15.7 us  [shifted(): lax.ppermute(array, axes, [(i, (i + distance) % size) for i in range(size)])]
    pallas_call x1, Pallas kernels: 10.2 us -> 8.14 us  [jacobian_sums(): pl.pallas_call(jacobian_kernel, out_shape=jax.ShapeDtypeStruct((8, 128),...]
  transfers between devices with their start and end apart: 17 -> 17, of which waited for: 10 -> 10; matrix products, arithmetic and copies ran while one was open for 1% -> 5% of each run, Pallas kernels for 52% -> 28%
where the time goes in v2:
time: 132 us; the launch traced here: 131 us
  Pallas kernels  45 us (34%)
  starting transfers between devices  38.4 us (29%)
  waiting for transfers between devices  33.2 us (25%)
  between operations  5.85 us (4%)
  local copies, waits for them, and re-layouts  4.61 us (3%)
  other arithmetic  3.35 us (3%)
    pallas_call x1, Pallas kernels, solve(): pl.pallas_call(solve_kernel, out_shape=(jax.ShapeDtypeStruct((NTM * 2 * R...  26 us
    all_to_all x3, starting transfers between devices, swap(): return lax.all_to_all(blocks, TM, split_axis=0, concat_axis=0, tiled=True)  20.8 us
    ppermute x14, starting transfers between devices, shifted(): lax.ppermute(array, axes, [(i, (i + distance) % size) for i in range(size)])  17.6 us
    all_to_all x3, waiting for transfers between devices, swap(): return lax.all_to_all(blocks, TM, split_axis=0, concat_axis=0, tiled=True)  17.5 us
    ppermute x14, waiting for transfers between devices, shifted(): lax.ppermute(array, axes, [(i, (i + distance) % size) for i in range(size)])  15.7 us
    pallas_call x1, Pallas kernels, jacobian_sums(): pl.pallas_call(jacobian_kernel, out_shape=jax.ShapeDtypeStruct((8, 128),...  8.14 us
    pallas_call x2, Pallas kernels, pack(): pl.pallas_call(kernel, out_shape=jax.ShapeDtypeStruct((NTM, slabs, ROWS,...  7.91 us
    pallas_call x1, Pallas kernels, finish(): pl.pallas_call(finish_kernel, out_shape=jax.ShapeDtypeStruct((STEPS, ROWS...  3.02 us
  transfers between devices with their start and end apart: 17, of which 10 were waited for; matrix products, arithmetic and copies ran while one was open for 5% of the time, Pallas kernels for 28%

profile of v2, /device:TPU:6, one launch (start us, length us, event | category | flops | bytes accessed | tf_op | source)
XLA Modules:
  0.0 130.5 jit_solution(10264082979247118498)
XLA Ops:
  0.6 4.8 %pack_halo.1 = f32[16,3,64,128]{3,2,1,0:T(8,128)} custom-call(f32[4,64,1024]{2,1,0:T(8,128)} %in_ref.2), custom_call_target="tpu_custom_call" | custom-call | tf_op jit(solution)/shard_map/pack_halo/pallas_call | solution.py:134
  5.5 7.4 %all-to-all-start = ((f32[16,3,64,128]{3,2,1,0:T(8,128)}), f32[16,3,64,128]{3,2,1,0:T(8,128)S(1)}, u32[]{:S(2)}, u32[]{:S(2)}) async-start(f32[16,3,64,128]{3,2,1,0:T(8,128)} %pack_halo.1), calls=%async_computation | async-start | bytes 3145728 | tf_op jit(solution)/shard_map/all_to_all | solution.py:389
  12.9 3.1 %pack.1 = f32[16,2,64,128]{3,2,1,0:T(8,128)} custom-call(f32[4,64,1024]{2,1,0:T(8,128)} %in_ref.3), custom_call_target="tpu_custom_call" | custom-call | tf_op jit(solution)/shard_map/pack/pallas_call | solution.py:134
  16.9 17.5 %all-to-all-done = f32[16,3,64,128]{3,2,1,0:T(8,128)S(1)} async-done(((f32[16,3,64,128]{3,2,1,0:T(8,128)}), f32[16,3,64,128]{3,2,1,0:T(8,128)S(1)}, u32[]{:S(2)}, u32[]{:S(2)}) %all-to-all-start) | async-done | bytes 1572896 | tf_op jit(solution)/shard_map/all_to_all | solution.py:389
  34.4 6.1 %all-to-all-start.2 = ((f32[16,2,64,128]{3,2,1,0:T(8,128)}), f32[16,2,64,128]{3,2,1,0:T(8,128)S(1)}, u32[]{:S(2)}, u32[]{:S(2)}) async-start(f32[16,2,64,128]{3,2,1,0:T(8,128)} %pack.1), calls=%async_computation.2 | async-start | bytes 2097152 | tf_op jit(solution)/shard_map/all_to_all | solution.py:389
  40.6 1.4 %concatenate.16 = f32[2,64,1088]{2,1,0:T(8,128)S(1)} concatenate(f32[2,64,16]{2,1,0:T(8,128)S(1)} %fusion, f32[2,64,1024]{2,1,0:T(8,128)} %pad_maximum_fusion, f32[2,64,48]{2,1,0:T(8,128)S(1)} %fusion.1), dimensions={2} | concatenate | bytes 1114112 | tf_op jit(solution)/shard_map/concatenate | solution.py:404
  44.3 2.1 %collective-permute-start.1 = (f32[16,3,16,128]{3,2,1,0:T(8,128)S(1)}, f32[16,3,16,128]{3,2,1,0:T(8,128)S(1)}, u32[]{:S(2)}, u32[]{:S(2)}) collective-permute-start(f32[16,3,16,128]{3,2,1,0:T(8,128)S(1)} %get-tuple-element.6), channel_id=1, source_target_pairs={{0,7},{1,0},{2,1},{3,2},{4,3},{5,4},{6,5},{7,6},{8,15},{9,8},{10,9... | collective-permute-start | bytes 1179656 | tf_op jit(solution)/shard_map/ppermute | solution.py:393
  49.2 2.7 %collective-permute-done = f32[16,3,16,128]{3,2,1,0:T(8,128)S(1)} collective-permute-done((f32[16,3,16,128]{3,2,1,0:T(8,128)S(1)}, f32[16,3,16,128]{3,2,1,0:T(8,128)S(1)}, u32[]{:S(2)}, u32[]{:S(2)}) %collective-permute-start) | collective-permute-done | bytes 393248 | tf_op jit(solution)/shard_map/ppermute | solution.py:393
  52.8 26.0 %solve.1 = (f32[2048,128]{1,0:T(8,128)}, f32[66,64,128]{2,1,0:T(8,128)}) custom-call(f32[3072,128]{1,0:T(8,128)} %bitcast.23, f32[768,128]{1,0:T(8,128)} %bitcast.37, f32[768,128]{1,0:T(8,128)} %bitcast.38, f32[3,96,128]{2,1,0:T(8,128)} %get-tuple-element.15.mob_ref, f32[3,96,128]{2,1,0:T(8,128)} %get-tuple-element.16.ini_ref, ...), custom_call_target="tpu_custom_call" | custom-call | tf_op jit(solution)/shard_map/solve/pallas_call | solution.py:302
  78.8 7.2 %all-to-all-start.1 = ((f32[16,2,64,128]{3,2,1,0:T(8,128)}), f32[16,2,64,128]{3,2,1,0:T(8,128)S(1)}, u32[]{:S(2)}, u32[]{:S(2)}) async-start(f32[16,2,64,128]{3,2,1,0:T(8,128)} %bitcast.32), calls=%async_computation.1 | async-start | bytes 2097152 | tf_op jit(solution)/shard_map/all_to_all | solution.py:389
  86.8 8.1 %jacobian_sums.1 = f32[8,128]{1,0:T(8,128)} custom-call(f32[66,64,128]{2,1,0:T(8,128)} %get-tuple-element.5.dir_ref, f32[2048,128]{1,0:T(8,128)} %bitcast.25, f32[3072,128]{1,0:T(8,128)} %bitcast.24, f32[96,128]{1,0:T(8,128)} %pad_maximum_fusion.4.mob_ref), custom_call_target="tpu_custom_call" | custom-call | tf_op jit(solution)/shard_map/jacobian_sums/pallas_call | solution.py:352
  94.9 1.4 %collective-permute-done.4 = f32[8,128]{1,0:T(8,128)S(1)} collective-permute-done((f32[8,128]{1,0:T(8,128)}, f32[8,128]{1,0:T(8,128)S(1)}, u32[]{:S(2)}, u32[]{:S(2)}) %collective-permute-start.4) | collective-permute-done | bytes 4128 | tf_op jit(solution)/shard_map/ppermute | solution.py:393
  98.3 2.0 %collective-permute-start.7 = (f32[8,128]{1,0:T(8,128)S(1)}, f32[8,128]{1,0:T(8,128)S(1)}, u32[]{:S(2)}, u32[]{:S(2)}) collective-permute-start(f32[8,128]{1,0:T(8,128)S(1)} %add.38), channel_id=1, source_target_pairs={{0,6},{2,0},{4,2},{6,4},{1,7},{3,1},{5,3},{7,5},{8,14},{10,8},{12,... | collective-permute-start | bytes 12296 | tf_op jit(solution)/shard_map/ppermute | solution.py:393
  100.2 1.7 %collective-permute-start.5 = (f32[8,128]{1,0:T(8,128)S(1)}, f32[8,128]{1,0:T(8,128)S(1)}, u32[]{:S(2)}, u32[]{:S(2)}) collective-permute-start(f32[8,128]{1,0:T(8,128)S(1)} %add.38), channel_id=1, source_target_pairs={{0,4},{2,6},{4,0},{6,2},{1,5},{3,7},{5,1},{7,3},{8,12},{10,14},{12... | collective-permute-start | bytes 12296 | tf_op jit(solution)/shard_map/ppermute | solution.py:393
  101.9 3.4 %collective-permute-done.5 = f32[8,128]{1,0:T(8,128)S(1)} collective-permute-done((f32[8,128]{1,0:T(8,128)S(1)}, f32[8,128]{1,0:T(8,128)S(1)}, u32[]{:S(2)}, u32[]{:S(2)}) %collective-permute-start.5) | collective-permute-done | bytes 4128 | tf_op jit(solution)/shard_map/ppermute | solution.py:393
  105.4 1.5 %collective-permute-start.9 = (f32[8,128]{1,0:T(8,128)S(1)}, f32[8,128]{1,0:T(8,128)S(1)}, u32[]{:S(2)}, u32[]{:S(2)}) collective-permute-start(f32[8,128]{1,0:T(8,128)S(1)} %add_add_fusion.2), channel_id=1, source_target_pairs={{0,8},{8,16},{16,24},{24,0},{1,9},{9,17},{17,25},{25,1},{2,10},{10... | collective-permute-start | bytes 12296 | tf_op jit(solution)/shard_map/ppermute | solution.py:393
  106.8 1.8 %collective-permute-start.10 = (f32[8,128]{1,0:T(8,128)S(1)}, f32[8,128]{1,0:T(8,128)S(1)}, u32[]{:S(2)}, u32[]{:S(2)}) collective-permute-start(f32[8,128]{1,0:T(8,128)S(1)} %add_add_fusion.2), channel_id=1, source_target_pairs={{0,24},{8,0},{16,8},{24,16},{1,25},{9,1},{17,9},{25,17},{2,26},{10... | collective-permute-start | bytes 12296 | tf_op jit(solution)/shard_map/ppermute | solution.py:393
  108.6 1.8 %collective-permute-start.8 = (f32[8,128]{1,0:T(8,128)S(1)}, f32[8,128]{1,0:T(8,128)S(1)}, u32[]{:S(2)}, u32[]{:S(2)}) collective-permute-start(f32[8,128]{1,0:T(8,128)S(1)} %add_add_fusion.2), channel_id=1, source_target_pairs={{0,16},{8,24},{16,0},{24,8},{1,17},{9,25},{17,1},{25,9},{2,18},{10... | collective-permute-start | bytes 12296 | tf_op jit(solution)/shard_map/ppermute | solution.py:393
  110.4 3.3 %collective-permute-done.8 = f32[8,128]{1,0:T(8,128)S(1)} collective-permute-done((f32[8,128]{1,0:T(8,128)S(1)}, f32[8,128]{1,0:T(8,128)S(1)}, u32[]{:S(2)}, u32[]{:S(2)}) %collective-permute-start.8) | collective-permute-done | bytes 4128 | tf_op jit(solution)/shard_map/ppermute | solution.py:393
  113.8 1.9 %collective-permute-start.13 = (f32[8,128]{1,0:T(8,128)S(1)}, f32[8,128]{1,0:T(8,128)S(1)}, u32[]{:S(2)}, u32[]{:S(2)}) collective-permute-start(f32[8,128]{1,0:T(8,128)S(1)} %add_add_fusion.1), channel_id=1, source_target_pairs={{0,96},{32,0},{64,32},{96,64},{1,97},{33,1},{65,33},{97,65},{2,98}... | collective-permute-start | bytes 12296 | tf_op jit(solution)/shard_map/ppermute | solution.py:393
  115.7 1.5 %collective-permute-start.11 = (f32[8,128]{1,0:T(8,128)S(1)}, f32[8,128]{1,0:T(8,128)S(1)}, u32[]{:S(2)}, u32[]{:S(2)}) collective-permute-start(f32[8,128]{1,0:T(8,128)S(1)} %add_add_fusion.1), channel_id=1, source_target_pairs={{0,64},{32,96},{64,0},{96,32},{1,65},{33,97},{65,1},{97,33},{2,66}... | collective-permute-start | bytes 12296 | tf_op jit(solution)/shard_map/ppermute | solution.py:393
  117.3 1.3 %collective-permute-done.13 = f32[8,128]{1,0:T(8,128)S(1)} collective-permute-done((f32[8,128]{1,0:T(8,128)S(1)}, f32[8,128]{1,0:T(8,128)S(1)}, u32[]{:S(2)}, u32[]{:S(2)}) %collective-permute-start.13) | collective-permute-done | bytes 4128 | tf_op jit(solution)/shard_map/ppermute | solution.py:393
  118.6 2.2 %collective-permute-done.11 = f32[8,128]{1,0:T(8,128)S(1)} collective-permute-done((f32[8,128]{1,0:T(8,128)S(1)}, f32[8,128]{1,0:T(8,128)S(1)}, u32[]{:S(2)}, u32[]{:S(2)}) %collective-permute-start.11) | collective-permute-done | bytes 4128 | tf_op jit(solution)/shard_map/ppermute | solution.py:393
  126.4 3.0 %finish.1 = f32[4,64,1024]{2,1,0:T(8,128)} custom-call(f32[16,2,64,128]{3,2,1,0:T(8,128)} %copy-done.1, f32[8,128]{1,0:T(8,128)} %copy-done.7), custom_call_target="tpu_custom_call" | custom-call | tf_op jit(solution)/shard_map/finish/pallas_call | solution.py:380
  (54 shorter events, 11.4 us)
Async XLA Ops:
  5.5 28.9 %all-to-all-start = ((f32[16,3,64,128]{3,2,1,0:T(8,128)}), f32[16,3,64,128]{3,2,1,0:T(8,128)S(1)}, u32[]{:S(2)}, u32[]{:S(2)}) async-start(f32[16,3,64,128]{3,2,1,0:T(8,128)} %pack_halo.1), calls=%async_computation | async-start | bytes 3145728 | tf_op jit(solution)/shard_map/all_to_all | solution.py:389
  12.9 3.1 %copy-start.3 = (f32[64,1024]{1,0:T(8,128)S(1)}, f32[64,1024]{1,0:T(8,128)}, u32[]{:S(2)}) copy-start(f32[64,1024]{1,0:T(8,128)} %param.10) | copy-start | bytes 786436
  12.9 3.1 %copy-start.4 = (f32[64,1024]{1,0:T(8,128)S(1)}, f32[64,1024]{1,0:T(8,128)}, u32[]{:S(2)}) copy-start(f32[64,1024]{1,0:T(8,128)} %param.8) | copy-start | bytes 786436
  34.4 8.9 %copy-start = (f32[16,3,64,128]{3,2,1,0:T(8,128)}, f32[16,3,64,128]{3,2,1,0:T(8,128)S(1)}, u32[]{:S(2)}) copy-start(f32[16,3,64,128]{3,2,1,0:T(8,128)S(1)} %all-to-all-done) | copy-start | bytes 4718596
  34.4 44.3 %all-to-all-start.2 = ((f32[16,2,64,128]{3,2,1,0:T(8,128)}), f32[16,2,64,128]{3,2,1,0:T(8,128)S(1)}, u32[]{:S(2)}, u32[]{:S(2)}) async-start(f32[16,2,64,128]{3,2,1,0:T(8,128)} %pack.1), calls=%async_computation.2 | async-start | bytes 2097152 | tf_op jit(solution)/shard_map/all_to_all | solution.py:389
  42.1 4.4 %collective-permute-start.3 = (f32[2,16,128]{2,1,0:T(8,128)S(1)}, f32[2,16,128]{2,1,0:T(8,128)S(1)}, u32[]{:S(2)}, u32[]{:S(2)}) collective-permute-start(f32[2,16,128]{2,1,0:T(8,128)S(1)} %get-tuple-element.9), channel_id=1, source_target_pairs={{0,7},{1,0},{2,1},{3,2},{4,3},{5,4},{6,5},{7,6},{8,15},{9,8},{10,9... | collective-permute-start | bytes 49160 | tf_op jit(solution)/shard_map/ppermute | solution.py:393
  43.3 4.4 %collective-permute-start.2 = (f32[2,16,128]{2,1,0:T(8,128)S(1)}, f32[2,16,128]{2,1,0:T(8,128)S(1)}, u32[]{:S(2)}, u32[]{:S(2)}) collective-permute-start(f32[2,16,128]{2,1,0:T(8,128)S(1)} %get-tuple-element.8), channel_id=1, source_target_pairs={{0,1},{1,2},{2,3},{3,4},{4,5},{5,6},{6,7},{7,0},{8,9},{9,10},{10,1... | collective-permute-start | bytes 49160 | tf_op jit(solution)/shard_map/ppermute | solution.py:393
  43.4 8.4 %collective-permute-start = (f32[16,3,16,128]{3,2,1,0:T(8,128)S(1)}, f32[16,3,16,128]{3,2,1,0:T(8,128)S(1)}, u32[]{:S(2)}, u32[]{:S(2)}) collective-permute-start(f32[16,3,16,128]{3,2,1,0:T(8,128)S(1)} %get-tuple-element.7), channel_id=1, source_target_pairs={{0,1},{1,2},{2,3},{3,4},{4,5},{5,6},{6,7},{7,0},{8,9},{9,10},{10,1... | collective-permute-start | bytes 1179656 | tf_op jit(solution)/shard_map/ppermute | solution.py:393
  44.3 7.6 %collective-permute-start.1 = (f32[16,3,16,128]{3,2,1,0:T(8,128)S(1)}, f32[16,3,16,128]{3,2,1,0:T(8,128)S(1)}, u32[]{:S(2)}, u32[]{:S(2)}) collective-permute-start(f32[16,3,16,128]{3,2,1,0:T(8,128)S(1)} %get-tuple-element.6), channel_id=1, source_target_pairs={{0,7},{1,0},{2,1},{3,2},{4,3},{5,4},{6,5},{7,6},{8,15},{9,8},{10,9... | collective-permute-start | bytes 1179656 | tf_op jit(solution)/shard_map/ppermute | solution.py:393
  51.9 0.9 copy-start.6
  78.8 8.0 %copy-start.2 = (f32[16,2,64,128]{3,2,1,0:T(8,128)}, f32[16,2,64,128]{3,2,1,0:T(8,128)S(1)}, u32[]{:S(2)}) copy-start(f32[16,2,64,128]{3,2,1,0:T(8,128)S(1)} %all-to-all-done.2) | copy-start | bytes 3145732
  78.8 46.6 %all-to-all-start.1 = ((f32[16,2,64,128]{3,2,1,0:T(8,128)}), f32[16,2,64,128]{3,2,1,0:T(8,128)S(1)}, u32[]{:S(2)}, u32[]{:S(2)}) async-start(f32[16,2,64,128]{3,2,1,0:T(8,128)} %bitcast.32), calls=%async_computation.1 | async-start | bytes 2097152 | tf_op jit(solution)/shard_map/all_to_all | solution.py:389
  94.9 1.4 %collective-permute-start.4 = (f32[8,128]{1,0:T(8,128)}, f32[8,128]{1,0:T(8,128)S(1)}, u32[]{:S(2)}, u32[]{:S(2)}) collective-permute-start(f32[8,128]{1,0:T(8,128)} %jacobian_sums.1), channel_id=1, source_target_pairs={{0,1},{1,0},{2,3},{3,2},{4,5},{5,4},{6,7},{7,6},{8,9},{9,8},{10,11... | collective-permute-start | bytes 12296 | tf_op jit(solution)/shard_map/ppermute | solution.py:393
  97.0 4.9 %collective-permute-start.6 = (f32[8,128]{1,0:T(8,128)S(1)}, f32[8,128]{1,0:T(8,128)S(1)}, u32[]{:S(2)}, u32[]{:S(2)}) collective-permute-start(f32[8,128]{1,0:T(8,128)S(1)} %add.38), channel_id=1, source_target_pairs={{0,2},{2,4},{4,6},{6,0},{1,3},{3,5},{5,7},{7,1},{8,10},{10,12},{12... | collective-permute-start | bytes 12296 | tf_op jit(solution)/shard_map/ppermute | solution.py:393
  98.3 3.7 %collective-permute-start.7 = (f32[8,128]{1,0:T(8,128)S(1)}, f32[8,128]{1,0:T(8,128)S(1)}, u32[]{:S(2)}, u32[]{:S(2)}) collective-permute-start(f32[8,128]{1,0:T(8,128)S(1)} %add.38), channel_id=1, source_target_pairs={{0,6},{2,0},{4,2},{6,4},{1,7},{3,1},{5,3},{7,5},{8,14},{10,8},{12,... | collective-permute-start | bytes 12296 | tf_op jit(solution)/shard_map/ppermute | solution.py:393
  100.2 5.1 %collective-permute-start.5 = (f32[8,128]{1,0:T(8,128)S(1)}, f32[8,128]{1,0:T(8,128)S(1)}, u32[]{:S(2)}, u32[]{:S(2)}) collective-permute-start(f32[8,128]{1,0:T(8,128)S(1)} %add.38), channel_id=1, source_target_pairs={{0,4},{2,6},{4,0},{6,2},{1,5},{3,7},{5,1},{7,3},{8,12},{10,14},{12... | collective-permute-start | bytes 12296 | tf_op jit(solution)/shard_map/ppermute | solution.py:393
  105.4 5.0 %collective-permute-start.9 = (f32[8,128]{1,0:T(8,128)S(1)}, f32[8,128]{1,0:T(8,128)S(1)}, u32[]{:S(2)}, u32[]{:S(2)}) collective-permute-start(f32[8,128]{1,0:T(8,128)S(1)} %add_add_fusion.2), channel_id=1, source_target_pairs={{0,8},{8,16},{16,24},{24,0},{1,9},{9,17},{17,25},{25,1},{2,10},{10... | collective-permute-start | bytes 12296 | tf_op jit(solution)/shard_map/ppermute | solution.py:393
  106.8 3.6 %collective-permute-start.10 = (f32[8,128]{1,0:T(8,128)S(1)}, f32[8,128]{1,0:T(8,128)S(1)}, u32[]{:S(2)}, u32[]{:S(2)}) collective-permute-start(f32[8,128]{1,0:T(8,128)S(1)} %add_add_fusion.2), channel_id=1, source_target_pairs={{0,24},{8,0},{16,8},{24,16},{1,25},{9,1},{17,9},{25,17},{2,26},{10... | collective-permute-start | bytes 12296 | tf_op jit(solution)/shard_map/ppermute | solution.py:393
  108.6 5.1 %collective-permute-start.8 = (f32[8,128]{1,0:T(8,128)S(1)}, f32[8,128]{1,0:T(8,128)S(1)}, u32[]{:S(2)}, u32[]{:S(2)}) collective-permute-start(f32[8,128]{1,0:T(8,128)S(1)} %add_add_fusion.2), channel_id=1, source_target_pairs={{0,16},{8,24},{16,0},{24,8},{1,17},{9,25},{17,1},{25,9},{2,18},{10... | collective-permute-start | bytes 12296 | tf_op jit(solution)/shard_map/ppermute | solution.py:393
  113.7 3.6 %collective-permute-start.12 = (f32[8,128]{1,0:T(8,128)S(1)}, f32[8,128]{1,0:T(8,128)S(1)}, u32[]{:S(2)}, u32[]{:S(2)}) collective-permute-start(f32[8,128]{1,0:T(8,128)S(1)} %add_add_fusion.1), channel_id=1, source_target_pairs={{0,32},{32,64},{64,96},{96,0},{1,33},{33,65},{65,97},{97,1},{2,34}... | collective-permute-start | bytes 12296 | tf_op jit(solution)/shard_map/ppermute | solution.py:393
  113.8 4.8 %collective-permute-start.13 = (f32[8,128]{1,0:T(8,128)S(1)}, f32[8,128]{1,0:T(8,128)S(1)}, u32[]{:S(2)}, u32[]{:S(2)}) collective-permute-start(f32[8,128]{1,0:T(8,128)S(1)} %add_add_fusion.1), channel_id=1, source_target_pairs={{0,96},{32,0},{64,32},{96,64},{1,97},{33,1},{65,33},{97,65},{2,98}... | collective-permute-start | bytes 12296 | tf_op jit(solution)/shard_map/ppermute | solution.py:393
  115.7 5.1 %collective-permute-start.11 = (f32[8,128]{1,0:T(8,128)S(1)}, f32[8,128]{1,0:T(8,128)S(1)}, u32[]{:S(2)}, u32[]{:S(2)}) collective-permute-start(f32[8,128]{1,0:T(8,128)S(1)} %add_add_fusion.1), channel_id=1, source_target_pairs={{0,64},{32,96},{64,0},{96,32},{1,65},{33,97},{65,1},{97,33},{2,66}... | collective-permute-start | bytes 12296 | tf_op jit(solution)/shard_map/ppermute | solution.py:393
  120.9 4.5 %copy-start.7 = (f32[8,128]{1,0:T(8,128)}, f32[8,128]{1,0:T(8,128)S(1)}, u32[]{:S(2)}) copy-start(f32[8,128]{1,0:T(8,128)S(1)} %add_add_fusion.sums_ref) | copy-start | bytes 12292
  125.4 1.0 copy-start.1
  (1 other events, 0.8 us)

commit v3 on v2

--- a/solution.py
+++ b/solution.py
@@ -25,7 +25,9 @@
 KEPT = ROWS + 2
 GROUPS = 4
 BLOCK = 16
+LAST_BLOCK = 11
 BATCH = 8
+PACK_ROWS = 16
 JBATCH = 4
 
 circ_weight = 0.2
@@ -34,7 +36,7 @@
 
 F32 = jnp.float32
 BF16 = jnp.bfloat16
-VMEM_LIMIT = 56 * 1024 * 1024
+MIB = 1024 * 1024
 
 
 def time_tables():
@@ -88,26 +90,19 @@
 
 def pack_kernel(in_ref, out_ref):
     low_half = lanes() < 64
-
-    def rows_body(i, _):
-        rows = pl.ds(pl.multiple_of(i * 8, 8), 8)
+    for rows in (slice(i, i + 8) for i in range(0, PACK_ROWS, 8)):
         for k in range(8):
             for j in range(2):
                 lane = slice(128 * k, 128 * k + 128)
                 first, second = in_ref[2 * j, rows, lane], in_ref[2 * j + 1, rows, lane]
                 out_ref[2 * k, j, rows, :] = jnp.where(low_half, first, roll(second, 64))
                 out_ref[2 * k + 1, j, rows, :] = jnp.where(low_half, roll(first, 64), second)
-        return 0
-
-    lax.fori_loop(0, ROWS // 8, rows_body, 0)
 
 
 def pack_halo_kernel(in_ref, out_ref):
     lane = lanes()
     slot, q = lane // 32, lane % 32
-
-    def rows_body(i, _):
-        rows = pl.ds(pl.multiple_of(i * 8, 8), 8)
+    for rows in (slice(i, i + 8) for i in range(0, PACK_ROWS, 8)):
         for odd in range(2):
             base = 48 if odd else -16
             index = [(3 * q + jnp.where(slot < 3, slot, j) + base) & 127 for j in range(3)]
@@ -125,18 +120,22 @@
                     out_ref[b, j, rows, :] = jnp.where(
                         slot < 3, source, permute_lanes(both[3], index[j])
                     )
-        return 0
-
-    lax.fori_loop(0, ROWS // 8, rows_body, 0)
 
 
 def pack(array, kernel, slabs, name):
     return pl.pallas_call(
         kernel,
+        grid=(ROWS // PACK_ROWS,),
+        in_specs=[pl.BlockSpec((STEPS, PACK_ROWS, COLS), lambda i: (0, i, 0))],
+        out_specs=pl.BlockSpec((NTM, slabs, PACK_ROWS, 128), lambda i: (0, 0, i, 0)),
         out_shape=jax.ShapeDtypeStruct((NTM, slabs, ROWS, 128), F32),
-        compiler_params=pltpu.CompilerParams(vmem_limit_bytes=VMEM_LIMIT),
+        compiler_params=pltpu.CompilerParams(vmem_limit_bytes=8 * MIB),
         name=name,
     )(array)
+
+
+def vmem(*arrays):
+    return [pltpu.with_memory_space_constraint(a, pltpu.VMEM) for a in arrays]
 
 
 def halo_tiles(ref, row, rows, slot):
@@ -167,55 +166,60 @@
     return 32 * (column % 3) + column // 3
 
 
-def solve_kernel(
-    x_ref, low_ref, high_ref, mob_ref, ini_ref, fwd_ref, inv_ref, coef_ref,
-    out_ref, dir_ref, s_ref, u_ref, w_ref, pa_ref, pb_ref, q_ref,
-):
+def spectrum(source, rows, offset, mob_ref, ini_ref, fwd_ref, coef_ref, s_ref, pa_ref, pb_ref, q_ref):
     slot = lanes() // 32
     slot16 = lanes(NTM) // 32
 
-    def spectrum(source, rows, offset):
-        def body(i, _):
-            first = i * BATCH
-            x = [
-                jnp.concatenate(halo_tiles(source, first + e, rows, slot16), axis=0)
-                for e in range(BATCH)
+    def body(i, _):
+        first = i * BATCH
+        x = [
+            jnp.concatenate(halo_tiles(source, first + e, rows, slot16), axis=0)
+            for e in range(BATCH)
+        ]
+        coefs = transform(fwd_ref[...], jnp.concatenate(x, axis=1))
+        c = coef_ref[2]
+        for e in range(BATCH):
+            row = first + e + offset
+            here = coefs[:, 128 * e : 128 * e + 128]
+            parts = [
+                swap_blocks([here[16 * g + 8 * h : 16 * g + 8 * h + 8] for g in range(4)], slot, 3)
+                for h in range(2)
             ]
-            coefs = transform(fwd_ref[...], jnp.concatenate(x, axis=1))
-            c = coef_ref[2]
-            for e in range(BATCH):
-                row = first + e + offset
-                here = coefs[:, 128 * e : 128 * e + 128]
-                parts = [
-                    swap_blocks([here[16 * g + 8 * h : 16 * g + 8 * h + 8] for g in range(4)], slot, 3)
-                    for h in range(2)
-                ]
-                for k in range(3):
-                    mob = jnp.broadcast_to(mob_ref[k, pl.ds(row, 1), :], (8, 128))
-                    ini = jnp.broadcast_to(ini_ref[k, pl.ds(row, 1), :], (8, 128))
-                    frozen = reaction_scale * jnp.maximum(3.0 * ini * ini - 1.0, 0.0)
-                    base = frozen + 4.0 * mob
-                    diag_a = coef_ref[0] + base
-                    diag_b = coef_ref[1] + base
-                    scale = 0.8 / (diag_a * diag_b + c * c)
-                    k_a, k_b, k_c = diag_b * scale, diag_a * scale, c * scale
-                    s_a, s_b = parts[0][k], parts[1][k]
-                    s_ref[row, 16 * k : 16 * k + 8, :] = k_a * s_a - k_c * s_b
-                    s_ref[row, 16 * k + 8 : 16 * k + 16, :] = k_b * s_b + k_c * s_a
-                    mob5 = 5.0 * mob
-                    tile = slice(8 * k, 8 * k + 8)
-                    pa_ref[row, tile, :] = mob5 * k_a
-                    pb_ref[row, tile, :] = mob5 * k_b
-                    q_ref[row, tile, :] = mob5 * k_c
-            return 0
-
-        lax.fori_loop(0, rows // BATCH, body, 0)
-
-    spectrum(low_ref, HALO, 0)
-    spectrum(x_ref, ROWS, HALO)
-    spectrum(high_ref, HALO, HALO + ROWS)
-
-    def apply(k, source, target, join=None, old=None):
+            for k in range(3):
+                mob = jnp.broadcast_to(mob_ref[k, pl.ds(row, 1), :], (8, 128))
+                ini = jnp.broadcast_to(ini_ref[k, pl.ds(row, 1), :], (8, 128))
+                frozen = reaction_scale * jnp.maximum(3.0 * ini * ini - 1.0, 0.0)
+                base = frozen + 4.0 * mob
+                diag_a = coef_ref[0] + base
+                diag_b = coef_ref[1] + base
+                scale = 0.8 / (diag_a * diag_b + c * c)
+                k_a, k_b, k_c = diag_b * scale, diag_a * scale, c * scale
+                s_a, s_b = parts[0][k], parts[1][k]
+                s_ref[row, 16 * k : 16 * k + 8, :] = k_a * s_a - k_c * s_b
+                s_ref[row, 16 * k + 8 : 16 * k + 16, :] = k_b * s_b + k_c * s_a
+                mob5 = 5.0 * mob
+                tile = slice(8 * k, 8 * k + 8)
+                pa_ref[row, tile, :] = mob5 * k_a
+                pb_ref[row, tile, :] = mob5 * k_b
+                q_ref[row, tile, :] = mob5 * k_c
+        return 0
+
+    lax.fori_loop(0, rows // BATCH, body, 0)
+
+
+def transform_kernel(x_ref, mob_ref, ini_ref, fwd_ref, coef_ref, *outs):
+    spectrum(x_ref, ROWS, HALO, mob_ref, ini_ref, fwd_ref, coef_ref, *outs)
+
+
+def sweep_kernel(
+    low_ref, high_ref, mob_ref, ini_ref, fwd_ref, coef_ref, s_in, pa_in, pb_in, q_in,
+    solved_ref, s_ref, pa_ref, pb_ref, q_ref, u_ref, w_ref,
+):
+    del s_in, pa_in, pb_in, q_in
+    for source, offset in ((low_ref, 0), (high_ref, HALO + ROWS)):
+        spectrum(source, HALO, offset, mob_ref, ini_ref, fwd_ref, coef_ref, s_ref, pa_ref, pb_ref, q_ref)
+
+    def apply(k, source, target, join=None, old=None, block=BLOCK, shift=0):
         count = WIDE - 2 * k
 
         def load(row):
@@ -223,8 +227,8 @@
 
         def body(i, carry):
             above, here = carry
-            start = k + i * BLOCK
-            for e in range(BLOCK):
+            start = k + i * block
+            for e in range(block):
                 row = start + e
                 below = load(row + 1)
                 n = [a + b for a, b in zip(above, below)]
@@ -247,11 +251,11 @@
                         if join is not None:
                             kept = here[2 * j + h] if old is source else old[row, m, :]
                             value = kept + join * value
-                        target[row, m, :] = value
+                        target[row - shift, m, :] = value
                 above, here = here, below
             return above, here
 
-        lax.fori_loop(0, -(-count // BLOCK), body, (load(k - 1), load(k)))
+        lax.fori_loop(0, -(-count // block), body, (load(k - 1), load(k)))
 
     apply(1, s_ref, u_ref, 0.2, s_ref)
     k = 1
@@ -263,8 +267,40 @@
             apply(k, source, target)
             source = target
         k += 1
-        apply(k, source, u_ref, 0.2**power, u_ref)
-
+        if power < 8:
+            apply(k, source, u_ref, 0.2**power, u_ref)
+        else:
+            apply(k, source, solved_ref, 0.2**power, u_ref, LAST_BLOCK, FIRST)
+
+
+WIDE_BUFFER = pltpu.VMEM((PAD, 48, 128), F32)
+SOLVED = pltpu.VMEM((KEPT, 48, 128), F32)
+HALF_BUFFER = pltpu.VMEM((PAD, 24, 128), F32)
+
+
+def transform_rows(x, mob, ini, forward, coefs):
+    return pl.pallas_call(
+        transform_kernel,
+        out_shape=(WIDE_BUFFER, HALF_BUFFER, HALF_BUFFER, HALF_BUFFER),
+        compiler_params=pltpu.CompilerParams(vmem_limit_bytes=16 * MIB),
+        name="transform_rows",
+    )(*vmem(x, mob, ini), forward, coefs)
+
+
+def sweep(low, high, mob, ini, forward, coefs, buffers):
+    return pl.pallas_call(
+        sweep_kernel,
+        out_shape=(SOLVED, WIDE_BUFFER, HALF_BUFFER, HALF_BUFFER, HALF_BUFFER),
+        scratch_shapes=[WIDE_BUFFER, WIDE_BUFFER],
+        input_output_aliases={6: 1, 7: 2, 8: 3, 9: 4},
+        compiler_params=pltpu.CompilerParams(vmem_limit_bytes=24 * MIB),
+        name="sweep",
+    )(*vmem(low, high, mob, ini), forward, coefs, *vmem(*buffers))[0]
+
+
+def back_kernel(u_ref, traj_ref, x_ref, mob_ref, inv_ref, out_ref, sums_ref, dir_ref, packed_ref, sem):
+    slot = lanes() // 32
+    slot16 = lanes(NTM) // 32
     natural = natural_index(NT)
     low_half = lanes(NTM) < 64
 
@@ -273,7 +309,7 @@
         for row in rows:
             halves = []
             for h in range(2):
-                t = [u_ref[row + FIRST, 16 * k + 8 * h : 16 * k + 8 * h + 8, :] for k in range(3)]
+                t = [u_ref[row, 16 * k + 8 * h : 16 * k + 8 * h + 8, :] for k in range(3)]
                 halves.append(swap_blocks(t + [t[2]], slot, 4))
             y.append(jnp.concatenate([halves[h][g] for g in range(4) for h in range(2)], axis=0))
         values = transform(inv_ref[...], jnp.concatenate(y, axis=1))
@@ -290,32 +326,34 @@
         for e, v in enumerate(back([i * BATCH + e + 1 for e in range(BATCH)])):
             for j in range(2):
                 both = jnp.where(low_half, v[32 * j : 32 * j + 16], roll(v[32 * j + 16 : 32 * j + 32], 64))
-                out_ref[pl.ds(i * BATCH + e + ROWS * j, NTM, stride=2 * ROWS), :] = both
+                packed_ref[pl.ds(i * BATCH + e + ROWS * j, NTM, stride=2 * ROWS), :] = both
         return 0
 
     lax.fori_loop(0, ROWS // BATCH, back_body, 0)
-
-
-def solve(x, low, high, mob, ini):
-    wide = pltpu.VMEM((PAD, 48, 128), F32)
-    half = pltpu.VMEM((PAD, 24, 128), F32)
+    copy = pltpu.make_async_copy(packed_ref, out_ref, sem)
+    copy.start()
+    jacobian_sums(dir_ref, traj_ref, x_ref, mob_ref, sums_ref, natural, slot16)
+    copy.wait()
+
+
+def back(u, traj, x, mob, inverse):
     return pl.pallas_call(
-        solve_kernel,
-        out_shape=(
-            jax.ShapeDtypeStruct((NTM * 2 * ROWS, 128), F32),
-            jax.ShapeDtypeStruct((KEPT, NT, 128), F32),
-        ),
-        scratch_shapes=[wide, wide, wide, half, half, half],
-        compiler_params=pltpu.CompilerParams(vmem_limit_bytes=VMEM_LIMIT),
-        name="solve",
-    )(x, low, high, mob, ini, *time_tables())
-
-
-def jacobian_kernel(dir_ref, traj_ref, x_ref, mob_ref, out_ref):
+        back_kernel,
+        in_specs=[pl.BlockSpec(memory_space=pltpu.VMEM)] * 5,
+        out_specs=(pl.BlockSpec(memory_space=pltpu.HBM), pl.BlockSpec(memory_space=pltpu.VMEM)),
+        out_shape=(pltpu.HBM((NTM * 2 * ROWS, 128), F32), pltpu.VMEM((8, 128), F32)),
+        scratch_shapes=[
+            pltpu.VMEM((KEPT, NT, 128), F32),
+            pltpu.VMEM((NTM * 2 * ROWS, 128), F32),
+            pltpu.SemaphoreType.DMA,
+        ],
+        compiler_params=pltpu.CompilerParams(vmem_limit_bytes=16 * MIB),
+        name="back",
+    )(*vmem(u, traj, x, mob), inverse)
+
+
+def jacobian_sums(dir_ref, traj_ref, x_ref, mob_ref, out_ref, natural, slot):
     first_row = lax.broadcasted_iota(jnp.int32, (NTM, 128), 0) == 0
-
-    natural = natural_index(NT)
-    slot = lanes(NTM) // 32
 
     def own(ref, row):
         slabs = [ref[pl.ds(row + ROWS * j, NTM, stride=2 * ROWS), :] for j in range(2)]
@@ -348,41 +386,48 @@
     out_ref[...] = jnp.where(row == 0, totals[0], jnp.where(row == 1, totals[1], totals[2]))
 
 
-def jacobian_sums(direction, traj, x, mob):
-    return pl.pallas_call(
-        jacobian_kernel,
-        out_shape=jax.ShapeDtypeStruct((8, 128), F32),
-        compiler_params=pltpu.CompilerParams(vmem_limit_bytes=VMEM_LIMIT),
-        name="jacobian_sums",
-    )(direction, traj, x, mob)
-
-
-def finish_kernel(blocks_ref, sums_ref, out_ref):
+def finish_kernel(blocks_ref, sums_ref, out_ref, reduction_ref):
     low_half = lanes() < 64
-    row = lambda i: jnp.broadcast_to(sums_ref[i : i + 1, :], (8, 128))
-    scale = row(1) / row(2)
-
-    def body(i, _):
-        rows = pl.ds(pl.multiple_of(i * 8, 8), 8)
+    norm_square, cross_sum, squared_applied = (
+        jnp.broadcast_to(sums_ref[i : i + 1, :], (8, 128)) for i in range(3)
+    )
+    scale = cross_sum / squared_applied
+    first = pl.program_id(0) * PACK_ROWS
+
+    @pl.when(first == 0)
+    def _():
+        projection = cross_sum / norm_square
+        squared_sum = squared_applied / norm_square
+        remainder = jnp.maximum(squared_sum - projection * projection, 0.0)
+        reduction_ref[...] = jnp.sqrt(remainder / squared_sum)[:1, :1]
+
+    for i in range(0, PACK_ROWS, 8):
+        rows = pl.ds(pl.multiple_of(first + i, 8), 8)
         for k in range(8):
             for j in range(2):
                 even = blocks_ref[2 * k, j, rows, :] * scale
                 odd = blocks_ref[2 * k + 1, j, rows, :] * scale
                 lane = slice(128 * k, 128 * k + 128)
-                out_ref[2 * j, rows, lane] = jnp.where(low_half, even, roll(odd, 64))
-                out_ref[2 * j + 1, rows, lane] = jnp.where(low_half, roll(even, 64), odd)
-        return 0
-
-    lax.fori_loop(0, ROWS // 8, body, 0)
+                out_ref[2 * j, i : i + 8, lane] = jnp.where(low_half, even, roll(odd, 64))
+                out_ref[2 * j + 1, i : i + 8, lane] = jnp.where(low_half, roll(even, 64), odd)
 
 
 def finish(blocks, sums):
     return pl.pallas_call(
         finish_kernel,
-        out_shape=jax.ShapeDtypeStruct((STEPS, ROWS, COLS), F32),
-        compiler_params=pltpu.CompilerParams(vmem_limit_bytes=VMEM_LIMIT),
+        grid=(ROWS // PACK_ROWS,),
+        in_specs=[pl.BlockSpec(memory_space=pltpu.VMEM)] * 2,
+        out_specs=(
+            pl.BlockSpec((STEPS, PACK_ROWS, COLS), lambda i: (0, i, 0)),
+            pl.BlockSpec((1, 1), lambda i: (0, 0)),
+        ),
+        out_shape=(
+            jax.ShapeDtypeStruct((STEPS, ROWS, COLS), F32),
+            jax.ShapeDtypeStruct((1, 1), F32),
+        ),
+        compiler_params=pltpu.CompilerParams(vmem_limit_bytes=8 * MIB),
         name="finish",
-    )(blocks, sums)
+    )(*vmem(blocks, sums))
 
 
 def swap(blocks):
@@ -410,30 +455,33 @@
     return jnp.concatenate([thirds] * GROUPS, axis=2)
 
 
-def total(sums):
-    sums = sums + shifted(sums, "space_1", 2, 1)
-    for axis in ("space_0", "tm_1", "tm_0"):
-        one, two, three = (shifted(sums, axis, 4, d) for d in (1, 2, 3))
-        sums = (sums + two) + (one + three)
-    return sums
+def around(sums, axis):
+    return [shifted(sums, axis, 4, distance) for distance in (1, 2, 3)]
 
 
 def on_device(trajectory, initial_state, residual, mobility):
+    forward, inverse, coefs = time_tables()
+    flat = lambda a: a.reshape(-1, 128)
     x = swap(pack(residual, pack_halo_kernel, 3, "pack_halo"))
-    low, high = row_halos(x, 2)
     fields = own_columns(jnp.stack([mobility, initial_state]))
     below, above = row_halos(fields, 1)
     mob, ini = jnp.concatenate([below, fields, above], axis=1)
-    traj = swap(pack(trajectory, pack_kernel, 2, "pack"))
-    flat = lambda a: a.reshape(-1, 128)
-    packed, direction = solve(flat(x), flat(low), flat(high), by_thirds(mob), by_thirds(ini))
+    thirds = by_thirds(mob), by_thirds(ini)
+    trajectory, thirds = lax.optimization_barrier((trajectory, thirds))
+    traj = pack(trajectory, pack_kernel, 2, "pack")
+    low, high = row_halos(x, 2)
+    buffers = transform_rows(flat(x), *thirds, forward, coefs)
+    traj = swap(traj)
+    solved = sweep(flat(low), flat(high), *thirds, forward, coefs, buffers)
+    packed, sums = back(solved, flat(traj), flat(x), jnp.roll(mob, -HALO, axis=1), inverse)
+    sums = sums + shifted(sums, "space_1", 2, 1)
+    packed, sums = lax.optimization_barrier((packed, sums))
     blocks = swap(packed.reshape(NTM, 2, ROWS, 128))
-    sums = total(jacobian_sums(direction, flat(traj), flat(x), jnp.roll(mob, -HALO, axis=1)))
-    norm_square, cross_sum, squared_applied = sums[0, 0], sums[1, 0], sums[2, 0]
-    projection = cross_sum / norm_square
-    squared_sum = squared_applied / norm_square
-    remainder = jnp.maximum(squared_sum - projection * projection, 0.0)
-    return finish(blocks, sums), jnp.sqrt(remainder / squared_sum)
+    for axis in ("space_0", "tm_1", "tm_0"):
+        one, two, three = around(sums, axis)
+        sums = (sums + two) + (one + three)
+    update, reduction = finish(blocks, sums)
+    return update, reduction.reshape(())
 
 
 def solution(mesh):

time: 132 us -> 112 us (0.85)
  Pallas kernels: 45 us -> 35 us
  waiting for transfers between devices: 33.2 us -> 25.1 us
  between operations: 5.85 us -> 0.83 us
  starting transfers between devices: 38.4 us -> 42.8 us
  other arithmetic: 3.35 us -> 0.54 us
  local copies, waits for them, and re-layouts: 4.61 us -> 7.32 us
    pallas_call x5 -> x6, Pallas kernels: 45 us -> 35 us  [the longest x1 13.6 us: sweep(): pl.pallas_call(sweep_kernel, out_shape=(SOLVED, WIDE_BUFFER, HALF_BUFFER,...]
    all_to_all x3, waiting for transfers between devices: 17.5 us -> 12.3 us  [swap(): return lax.all_to_all(blocks, TM, split_axis=0, concat_axis=0, tiled=True)]
    ppermute x14, starting transfers between devices: 17.6 us -> 21.9 us  [shifted(): lax.ppermute(array, axes, [(i, (i + distance) % size) for i in range(size)])]
    ppermute x14, waiting for transfers between devices: 15.7 us -> 12.8 us  [shifted(): lax.ppermute(array, axes, [(i, (i + distance) % size) for i in range(size)])]
    unnamed x16 -> x18, local copies, waits for them, and re-layouts: 1.9 us -> 3.87 us
  transfers between devices with their start and end apart: 17 -> 17, of which waited for: 10 -> 10; matrix products, arithmetic and copies ran while one was open for 5% -> 4% of each run, Pallas kernels for 28% -> 18%
where the time goes in v3:
time: 112 us
  starting transfers between devices  42.8 us (38%)
  Pallas kernels  35 us (31%)
  waiting for transfers between devices  25.1 us (22%)
  local copies, waits for them, and re-layouts  7.32 us (7%)
    ppermute x14, starting transfers between devices, shifted(): lax.ppermute(array, axes, [(i, (i + distance) % size) for i in range(size)])  21.9 us
    all_to_all x3, starting transfers between devices, swap(): return lax.all_to_all(blocks, TM, split_axis=0, concat_axis=0, tiled=True)  20.9 us
    pallas_call x1, Pallas kernels, sweep(): pl.pallas_call(sweep_kernel, out_shape=(SOLVED, WIDE_BUFFER, HALF_BUFFER,...  13.6 us
    ppermute x14, waiting for transfers between devices, shifted(): lax.ppermute(array, axes, [(i, (i + distance) % size) for i in range(size)])  12.8 us
    all_to_all x3, waiting for transfers between devices, swap(): return lax.all_to_all(blocks, TM, split_axis=0, concat_axis=0, tiled=True)  12.3 us
    pallas_call x1, Pallas kernels, back(): pl.pallas_call(back_kernel, in_specs=[pl.BlockSpec(memory_space=pltpu.VME...  10.2 us
    pallas_call x2, Pallas kernels, pack(): pl.pallas_call(kernel, grid=(ROWS // PACK_ROWS,), in_specs=[pl.BlockSpec(...  5.18 us
    pallas_call x1, Pallas kernels, transform_rows(): pl.pallas_call(transform_kernel, out_shape=(WIDE_BUFFER, HALF_BUFFER, HAL...  4.11 us
  transfers between devices with their start and end apart: 17, of which 10 were waited for; matrix products, arithmetic and copies ran while one was open for 4% of the time, Pallas kernels for 18%

profile of v3, /device:TPU:6, one launch (start us, length us, event | category | flops | bytes accessed | tf_op | source)
XLA Modules:
  0.0 111.6 jit_solution(15603640947607953234)
XLA Ops:
  0.6 1.2 %copy-done.2 = f32[4,64,1024]{2,1,0:T(8,128)S(1)} copy-done((f32[4,64,1024]{2,1,0:T(8,128)S(1)}, f32[4,64,1024]{2,1,0:T(8,128)}, u32[]{:S(2)}) %copy-start.2) | copy-done | bytes 1048600
  1.9 3.3 %pack_halo.1 = f32[16,3,64,128]{3,2,1,0:T(8,128)} custom-call(f32[4,64,1024]{2,1,0:T(8,128)S(1)} %copy-done.2), custom_call_target="tpu_custom_call" | custom-call | tf_op jit(solution)/shard_map/pack_halo/pallas_call | solution.py:126
  5.1 7.6 %all-to-all-start = ((f32[16,3,64,128]{3,2,1,0:T(8,128)}), f32[16,3,64,128]{3,2,1,0:T(8,128)S(1)}, u32[]{:S(2)}, u32[]{:S(2)}) async-start(f32[16,3,64,128]{3,2,1,0:T(8,128)} %pack_halo.1), calls=%async_computation | async-start | bytes 3145728 | tf_op jit(solution)/shard_map/all_to_all | solution.py:434
  14.8 3.0 %collective-permute-start.3 = (f32[2,16,128]{2,1,0:T(8,128)S(1)}, f32[2,16,128]{2,1,0:T(8,128)S(1)}, u32[]{:S(2)}, u32[]{:S(2)}) collective-permute-start(f32[2,16,128]{2,1,0:T(8,128)S(1)} %get-tuple-element.33), channel_id=1, source_target_pairs={{0,7},{1,0},{2,1},{3,2},{4,3},{5,4},{6,5},{7,6},{8,15},{9,8},{10,9... | collective-permute-start | bytes 49160 | tf_op jit(solution)/shard_map/ppermute | solution.py:438
  20.0 1.9 %pack.1 = f32[16,2,64,128]{3,2,1,0:T(8,128)} custom-call(f32[4,64,1024]{2,1,0:T(8,128)S(1)} %copy-done.3), custom_call_target="tpu_custom_call" | custom-call | tf_op jit(solution)/shard_map/pack/pallas_call | solution.py:126
  21.9 12.3 %all-to-all-done = f32[16,3,64,128]{3,2,1,0:T(8,128)S(1)} async-done(((f32[16,3,64,128]{3,2,1,0:T(8,128)}), f32[16,3,64,128]{3,2,1,0:T(8,128)S(1)}, u32[]{:S(2)}, u32[]{:S(2)}) %all-to-all-start) | async-done | bytes 1572896 | tf_op jit(solution)/shard_map/all_to_all | solution.py:434
  34.2 6.1 %all-to-all-start.1 = ((f32[16,2,64,128]{3,2,1,0:T(8,128)}), f32[16,2,64,128]{3,2,1,0:T(8,128)S(1)}, u32[]{:S(2)}, u32[]{:S(2)}) async-start(f32[16,2,64,128]{3,2,1,0:T(8,128)} %pack.1), calls=%async_computation.1 | async-start | bytes 2097152 | tf_op jit(solution)/shard_map/all_to_all | solution.py:434
  40.5 2.9 %collective-permute-start.1 = (f32[16,3,16,128]{3,2,1,0:T(8,128)S(1)}, f32[16,3,16,128]{3,2,1,0:T(8,128)S(1)}, u32[]{:S(2)}, u32[]{:S(2)}) collective-permute-start(f32[16,3,16,128]{3,2,1,0:T(8,128)S(1)} %get-tuple-element.30), channel_id=1, source_target_pairs={{0,7},{1,0},{2,1},{3,2},{4,3},{5,4},{6,5},{7,6},{8,15},{9,8},{10,9... | collective-permute-start | bytes 1179656 | tf_op jit(solution)/shard_map/ppermute | solution.py:438
  43.6 4.1 %transform_rows.1 = (f32[112,48,128]{2,1,0:T(8,128)S(1)}, f32[112,24,128]{2,1,0:T(8,128)S(1)}, f32[112,24,128]{2,1,0:T(8,128)S(1)}, f32[112,24,128]{2,1,0:T(8,128)S(1)}) custom-call(f32[3072,128]{1,0:T(8,128)S(1)} %bitcast.21, f32[3,96,128]{2,1,0:T(8,128)S(1)} %get-tuple-element.16.mob_ref, f32[3,96,128]{2,1,0:T(8,128)S(1)} %get-tuple-element.17.ini_ref, ...), custom_call_target="tpu_custom_call" | custom-call | tf_op jit(solution)/shard_map/transform_rows/pallas_call | solution.py:282
  48.9 13.6 %sweep.1 = (f32[66,48,128]{2,1,0:T(8,128)S(1)}, f32[112,48,128]{2,1,0:T(8,128)S(1)}, f32[112,24,128]{2,1,0:T(8,128)S(1)}, f32[112,24,128]{2,1,0:T(8,128)S(1)}, f32[112,24,128]{2,1,0:T(8,128)S(1)}) custom-call(f32[768,128]{1,0:T(8,128)S(1)} %bitcast.24, ...), custom_call_target="tpu_custom_call", output_to_operand_aliasing={{1}: (6, {}), {2}: (7, {}), {3}: (8, {}), {4}: (9, {})} | custom-call | tf_op jit(solution)/shard_map/sweep/pallas_call | solution.py:291
  62.5 1.2 %copy-done = f32[66,48,128]{2,1,0:T(8,128)} copy-done((f32[66,48,128]{2,1,0:T(8,128)}, f32[66,48,128]{2,1,0:T(8,128)S(1)}, u32[]{:S(2)}) %copy-start) | copy-done | bytes 1622040
  63.7 1.4 %copy-done.1 = f32[66,48,128]{2,1,0:T(8,128)S(1)} copy-done((f32[66,48,128]{2,1,0:T(8,128)S(1)}, f32[66,48,128]{2,1,0:T(8,128)}, u32[]{:S(2)}) %copy-start.1) | copy-done | bytes 1622040
  65.1 10.2 %back.1 = (f32[2048,128]{1,0:T(8,128)}, f32[8,128]{1,0:T(8,128)S(1)}) custom-call(f32[66,48,128]{2,1,0:T(8,128)S(1)} %copy-done.1, f32[2048,128]{1,0:T(8,128)S(1)} %bitcast.23, f32[3072,128]{1,0:T(8,128)S(1)} %bitcast.22, f32[96,128]{1,0:T(8,128)S(1)} %pad_maximum_fusion.4.mob_ref, bf16[64,256]{1,0:T(8,128)(2,1)S(1)} %copy-done.6), custom_call_target="tpu_custom_call" | custom-call | tf_op jit(solution)/shard_map/back/pallas_call | solution.py:340
  77.3 7.2 %all-to-all-start.2 = ((f32[16,2,64,128]{3,2,1,0:T(8,128)}), f32[16,2,64,128]{3,2,1,0:T(8,128)S(1)}, u32[]{:S(2)}, u32[]{:S(2)}) async-start(f32[16,2,64,128]{3,2,1,0:T(8,128)} %bitcast.32), calls=%async_computation.2 | async-start | bytes 2097152 | tf_op jit(solution)/shard_map/all_to_all | solution.py:434
  84.5 3.6 %collective-permute-start.5 = (f32[8,128]{1,0:T(8,128)S(1)}, f32[8,128]{1,0:T(8,128)S(1)}, u32[]{:S(2)}, u32[]{:S(2)}) collective-permute-start(f32[8,128]{1,0:T(8,128)S(1)} %add.38), channel_id=1, source_target_pairs={{0,4},{2,6},{4,0},{6,2},{1,5},{3,7},{5,1},{7,3},{8,12},{10,14},{12... | collective-permute-start | bytes 12296 | tf_op jit(solution)/shard_map/ppermute | solution.py:438
  88.1 3.2 %collective-permute-start.7 = (f32[8,128]{1,0:T(8,128)S(1)}, f32[8,128]{1,0:T(8,128)S(1)}, u32[]{:S(2)}, u32[]{:S(2)}) collective-permute-start(f32[8,128]{1,0:T(8,128)S(1)} %add.38), channel_id=1, source_target_pairs={{0,6},{2,0},{4,2},{6,4},{1,7},{3,1},{5,3},{7,5},{8,14},{10,8},{12,... | collective-permute-start | bytes 12296 | tf_op jit(solution)/shard_map/ppermute | solution.py:438
  91.4 1.6 %collective-permute-done.6 = f32[8,128]{1,0:T(8,128)S(1)} collective-permute-done((f32[8,128]{1,0:T(8,128)S(1)}, f32[8,128]{1,0:T(8,128)S(1)}, u32[]{:S(2)}, u32[]{:S(2)}) %collective-permute-start.6) | collective-permute-done | bytes 4128 | tf_op jit(solution)/shard_map/ppermute | solution.py:438
  92.9 2.7 %collective-permute-start.10 = (f32[8,128]{1,0:T(8,128)S(1)}, f32[8,128]{1,0:T(8,128)S(1)}, u32[]{:S(2)}, u32[]{:S(2)}) collective-permute-start(f32[8,128]{1,0:T(8,128)S(1)} %add_add_fusion.2), channel_id=1, source_target_pairs={{0,24},{8,0},{16,8},{24,16},{1,25},{9,1},{17,9},{25,17},{2,26},{10... | collective-permute-start | bytes 12296 | tf_op jit(solution)/shard_map/ppermute | solution.py:438
  98.2 2.6 %collective-permute-done.8 = f32[8,128]{1,0:T(8,128)S(1)} collective-permute-done((f32[8,128]{1,0:T(8,128)S(1)}, f32[8,128]{1,0:T(8,128)S(1)}, u32[]{:S(2)}, u32[]{:S(2)}) %collective-permute-start.8) | collective-permute-done | bytes 4128 | tf_op jit(solution)/shard_map/ppermute | solution.py:438
  101.4 1.5 %collective-permute-start.11 = (f32[8,128]{1,0:T(8,128)S(1)}, f32[8,128]{1,0:T(8,128)S(1)}, u32[]{:S(2)}, u32[]{:S(2)}) collective-permute-start(f32[8,128]{1,0:T(8,128)S(1)} %add_add_fusion.1), channel_id=1, source_target_pairs={{0,64},{32,96},{64,0},{96,32},{1,65},{33,97},{65,1},{97,33},{2,66}... | collective-permute-start | bytes 12296 | tf_op jit(solution)/shard_map/ppermute | solution.py:438
  102.8 2.1 %collective-permute-start.12 = (f32[8,128]{1,0:T(8,128)S(1)}, f32[8,128]{1,0:T(8,128)S(1)}, u32[]{:S(2)}, u32[]{:S(2)}) collective-permute-start(f32[8,128]{1,0:T(8,128)S(1)} %add_add_fusion.1), channel_id=1, source_target_pairs={{0,32},{32,64},{64,96},{96,0},{1,33},{33,65},{65,97},{97,1},{2,34}... | collective-permute-start | bytes 12296 | tf_op jit(solution)/shard_map/ppermute | solution.py:438
  104.9 1.6 %collective-permute-done.11 = f32[8,128]{1,0:T(8,128)S(1)} collective-permute-done((f32[8,128]{1,0:T(8,128)S(1)}, f32[8,128]{1,0:T(8,128)S(1)}, u32[]{:S(2)}, u32[]{:S(2)}) %collective-permute-start.11) | collective-permute-done | bytes 4128 | tf_op jit(solution)/shard_map/ppermute | solution.py:438
  106.5 3.2 %collective-permute-done.13 = f32[8,128]{1,0:T(8,128)S(1)} collective-permute-done((f32[8,128]{1,0:T(8,128)S(1)}, f32[8,128]{1,0:T(8,128)S(1)}, u32[]{:S(2)}, u32[]{:S(2)}) %collective-permute-start.13) | collective-permute-done | bytes 4128 | tf_op jit(solution)/shard_map/ppermute | solution.py:438
  109.7 1.9 %finish.1 = (f32[4,64,1024]{2,1,0:T(8,128)}, f32[1,1]{1,0:T(1,128)}) custom-call(f32[16,2,64,128]{3,2,1,0:T(8,128)S(1)} %all-to-all-done.2.blocks_ref, f32[8,128]{1,0:T(8,128)S(1)} %add_add_fusion.sums_ref), custom_call_target="tpu_custom_call" | custom-call | tf_op jit(solution)/shard_map/finish/pallas_call | solution.py:416
  (56 shorter events, 10.8 us)
Async XLA Ops:
  5.1 7.6 %copy-start.7 = (f32[64,1024]{1,0:T(8,128)S(1)}, f32[64,1024]{1,0:T(8,128)}, u32[]{:S(2)}) copy-start(f32[64,1024]{1,0:T(8,128)} %param.10) | copy-start | bytes 786436
  5.1 7.6 %copy-start.8 = (f32[64,1024]{1,0:T(8,128)S(1)}, f32[64,1024]{1,0:T(8,128)}, u32[]{:S(2)}) copy-start(f32[64,1024]{1,0:T(8,128)} %param.8) | copy-start | bytes 786436
  5.1 29.1 %all-to-all-start = ((f32[16,3,64,128]{3,2,1,0:T(8,128)}), f32[16,3,64,128]{3,2,1,0:T(8,128)S(1)}, u32[]{:S(2)}, u32[]{:S(2)}) async-start(f32[16,3,64,128]{3,2,1,0:T(8,128)} %pack_halo.1), calls=%async_computation | async-start | bytes 3145728 | tf_op jit(solution)/shard_map/all_to_all | solution.py:434
  12.9 7.1 %copy-start.3 = (f32[4,64,1024]{2,1,0:T(8,128)S(1)}, f32[4,64,1024]{2,1,0:T(8,128)}, u32[]{:S(2)}) copy-start(f32[4,64,1024]{2,1,0:T(8,128)} %in_ref.2) | copy-start | bytes 3145732
  14.8 4.4 %collective-permute-start.2 = (f32[2,16,128]{2,1,0:T(8,128)S(1)}, f32[2,16,128]{2,1,0:T(8,128)S(1)}, u32[]{:S(2)}, u32[]{:S(2)}) collective-permute-start(f32[2,16,128]{2,1,0:T(8,128)S(1)} %get-tuple-element.32), channel_id=1, source_target_pairs={{0,1},{1,2},{2,3},{3,4},{4,5},{5,6},{6,7},{7,0},{8,9},{9,10},{10,1... | collective-permute-start | bytes 49160 | tf_op jit(solution)/shard_map/ppermute | solution.py:438
  14.8 4.4 %collective-permute-start.3 = (f32[2,16,128]{2,1,0:T(8,128)S(1)}, f32[2,16,128]{2,1,0:T(8,128)S(1)}, u32[]{:S(2)}, u32[]{:S(2)}) collective-permute-start(f32[2,16,128]{2,1,0:T(8,128)S(1)} %get-tuple-element.33), channel_id=1, source_target_pairs={{0,7},{1,0},{2,1},{3,2},{4,3},{5,4},{6,5},{7,6},{8,15},{9,8},{10,9... | collective-permute-start | bytes 49160 | tf_op jit(solution)/shard_map/ppermute | solution.py:438
  21.9 21.7 %copy-start.4 = (bf16[64,256]{1,0:T(8,128)(2,1)S(1)}, bf16[64,256]{1,0:T(8,128)(2,1)}, u32[]{:S(2)}) copy-start(bf16[64,256]{1,0:T(8,128)(2,1)} %constant.23.clone.fwd_ref) | copy-start | bytes 98308
  21.9 21.7 %copy-start.5 = (f32[3,8,128]{2,1,0:T(8,128)S(1)}, f32[3,8,128]{2,1,0:T(8,128)}, u32[]{:S(2)}) copy-start(f32[3,8,128]{2,1,0:T(8,128)} %constant.24.clone.coef_ref) | copy-start | bytes 36868
  34.2 29.5 %all-to-all-start.1 = ((f32[16,2,64,128]{3,2,1,0:T(8,128)}), f32[16,2,64,128]{3,2,1,0:T(8,128)S(1)}, u32[]{:S(2)}, u32[]{:S(2)}) async-start(f32[16,2,64,128]{3,2,1,0:T(8,128)} %pack.1), calls=%async_computation.1 | async-start | bytes 2097152 | tf_op jit(solution)/shard_map/all_to_all | solution.py:434
  40.4 8.4 %collective-permute-start = (f32[16,3,16,128]{3,2,1,0:T(8,128)S(1)}, f32[16,3,16,128]{3,2,1,0:T(8,128)S(1)}, u32[]{:S(2)}, u32[]{:S(2)}) collective-permute-start(f32[16,3,16,128]{3,2,1,0:T(8,128)S(1)} %get-tuple-element.31), channel_id=1, source_target_pairs={{0,1},{1,2},{2,3},{3,4},{4,5},{5,6},{6,7},{7,0},{8,9},{9,10},{10,1... | collective-permute-start | bytes 1179656 | tf_op jit(solution)/shard_map/ppermute | solution.py:438
  40.5 8.4 %collective-permute-start.1 = (f32[16,3,16,128]{3,2,1,0:T(8,128)S(1)}, f32[16,3,16,128]{3,2,1,0:T(8,128)S(1)}, u32[]{:S(2)}, u32[]{:S(2)}) collective-permute-start(f32[16,3,16,128]{3,2,1,0:T(8,128)S(1)} %get-tuple-element.30), channel_id=1, source_target_pairs={{0,7},{1,0},{2,1},{3,2},{4,3},{5,4},{6,5},{7,6},{8,15},{9,8},{10,9... | collective-permute-start | bytes 1179656 | tf_op jit(solution)/shard_map/ppermute | solution.py:438
  48.9 14.8 %copy-start.6 = (bf16[64,256]{1,0:T(8,128)(2,1)S(1)}, bf16[64,256]{1,0:T(8,128)(2,1)}, u32[]{:S(2)}) copy-start(bf16[64,256]{1,0:T(8,128)(2,1)} %constant.25.clone.inv_ref) | copy-start | bytes 98308
  63.7 1.4 %copy-start.1 = (f32[66,48,128]{2,1,0:T(8,128)S(1)}, f32[66,48,128]{2,1,0:T(8,128)}, u32[]{:S(2)}) copy-start(f32[66,48,128]{2,1,0:T(8,128)} %copy-done) | copy-start | bytes 4866052
  75.3 2.0 %collective-permute-start.4 = (f32[8,128]{1,0:T(8,128)S(1)}, f32[8,128]{1,0:T(8,128)S(1)}, u32[]{:S(2)}, u32[]{:S(2)}) collective-permute-start(f32[8,128]{1,0:T(8,128)S(1)} %get-tuple-element.25), channel_id=1, source_target_pairs={{0,1},{1,0},{2,3},{3,2},{4,5},{5,4},{6,7},{7,6},{8,9},{9,8},{10,11... | collective-permute-start | bytes 12296 | tf_op jit(solution)/shard_map/ppermute | solution.py:438
  77.3 32.4 %all-to-all-start.2 = ((f32[16,2,64,128]{3,2,1,0:T(8,128)}), f32[16,2,64,128]{3,2,1,0:T(8,128)S(1)}, u32[]{:S(2)}, u32[]{:S(2)}) async-start(f32[16,2,64,128]{3,2,1,0:T(8,128)} %bitcast.32), calls=%async_computation.2 | async-start | bytes 2097152 | tf_op jit(solution)/shard_map/all_to_all | solution.py:434
  84.5 6.8 %collective-permute-start.5 = (f32[8,128]{1,0:T(8,128)S(1)}, f32[8,128]{1,0:T(8,128)S(1)}, u32[]{:S(2)}, u32[]{:S(2)}) collective-permute-start(f32[8,128]{1,0:T(8,128)S(1)} %add.38), channel_id=1, source_target_pairs={{0,4},{2,6},{4,0},{6,2},{1,5},{3,7},{5,1},{7,3},{8,12},{10,14},{12... | collective-permute-start | bytes 12296 | tf_op jit(solution)/shard_map/ppermute | solution.py:438
  88.1 4.8 %collective-permute-start.6 = (f32[8,128]{1,0:T(8,128)S(1)}, f32[8,128]{1,0:T(8,128)S(1)}, u32[]{:S(2)}, u32[]{:S(2)}) collective-permute-start(f32[8,128]{1,0:T(8,128)S(1)} %add.38), channel_id=1, source_target_pairs={{0,2},{2,4},{4,6},{6,0},{1,3},{3,5},{5,7},{7,1},{8,10},{10,12},{12... | collective-permute-start | bytes 12296 | tf_op jit(solution)/shard_map/ppermute | solution.py:438
  88.1 4.8 %collective-permute-start.7 = (f32[8,128]{1,0:T(8,128)S(1)}, f32[8,128]{1,0:T(8,128)S(1)}, u32[]{:S(2)}, u32[]{:S(2)}) collective-permute-start(f32[8,128]{1,0:T(8,128)S(1)} %add.38), channel_id=1, source_target_pairs={{0,6},{2,0},{4,2},{6,4},{1,7},{3,1},{5,3},{7,5},{8,14},{10,8},{12,... | collective-permute-start | bytes 12296 | tf_op jit(solution)/shard_map/ppermute | solution.py:438
  92.9 5.3 %collective-permute-start.10 = (f32[8,128]{1,0:T(8,128)S(1)}, f32[8,128]{1,0:T(8,128)S(1)}, u32[]{:S(2)}, u32[]{:S(2)}) collective-permute-start(f32[8,128]{1,0:T(8,128)S(1)} %add_add_fusion.2), channel_id=1, source_target_pairs={{0,24},{8,0},{16,8},{24,16},{1,25},{9,1},{17,9},{25,17},{2,26},{10... | collective-permute-start | bytes 12296 | tf_op jit(solution)/shard_map/ppermute | solution.py:438
  95.7 5.1 %collective-permute-start.8 = (f32[8,128]{1,0:T(8,128)S(1)}, f32[8,128]{1,0:T(8,128)S(1)}, u32[]{:S(2)}, u32[]{:S(2)}) collective-permute-start(f32[8,128]{1,0:T(8,128)S(1)} %add_add_fusion.2), channel_id=1, source_target_pairs={{0,16},{8,24},{16,0},{24,8},{1,17},{9,25},{17,1},{25,9},{2,18},{10... | collective-permute-start | bytes 12296 | tf_op jit(solution)/shard_map/ppermute | solution.py:438
  96.5 4.8 %collective-permute-start.9 = (f32[8,128]{1,0:T(8,128)S(1)}, f32[8,128]{1,0:T(8,128)S(1)}, u32[]{:S(2)}, u32[]{:S(2)}) collective-permute-start(f32[8,128]{1,0:T(8,128)S(1)} %add_add_fusion.2), channel_id=1, source_target_pairs={{0,8},{8,16},{16,24},{24,0},{1,9},{9,17},{17,25},{25,1},{2,10},{10... | collective-permute-start | bytes 12296 | tf_op jit(solution)/shard_map/ppermute | solution.py:438
  101.4 5.1 %collective-permute-start.11 = (f32[8,128]{1,0:T(8,128)S(1)}, f32[8,128]{1,0:T(8,128)S(1)}, u32[]{:S(2)}, u32[]{:S(2)}) collective-permute-start(f32[8,128]{1,0:T(8,128)S(1)} %add_add_fusion.1), channel_id=1, source_target_pairs={{0,64},{32,96},{64,0},{96,32},{1,65},{33,97},{65,1},{97,33},{2,66}... | collective-permute-start | bytes 12296 | tf_op jit(solution)/shard_map/ppermute | solution.py:438
  102.8 3.7 %collective-permute-start.12 = (f32[8,128]{1,0:T(8,128)S(1)}, f32[8,128]{1,0:T(8,128)S(1)}, u32[]{:S(2)}, u32[]{:S(2)}) collective-permute-start(f32[8,128]{1,0:T(8,128)S(1)} %add_add_fusion.1), channel_id=1, source_target_pairs={{0,32},{32,64},{64,96},{96,0},{1,33},{33,65},{65,97},{97,1},{2,34}... | collective-permute-start | bytes 12296 | tf_op jit(solution)/shard_map/ppermute | solution.py:438
  104.9 4.8 %collective-permute-start.13 = (f32[8,128]{1,0:T(8,128)S(1)}, f32[8,128]{1,0:T(8,128)S(1)}, u32[]{:S(2)}, u32[]{:S(2)}) collective-permute-start(f32[8,128]{1,0:T(8,128)S(1)} %add_add_fusion.1), channel_id=1, source_target_pairs={{0,96},{32,0},{64,32},{96,64},{1,97},{33,1},{65,33},{97,65},{2,98}... | collective-permute-start | bytes 12296 | tf_op jit(solution)/shard_map/ppermute | solution.py:438
  (2 other events, 2.4 us)

commit v4 on v3

--- a/solution.py
+++ b/solution.py
@@ -20,14 +20,16 @@
 COLS = 1024
 HALO = 16
 WIDE = ROWS + 2 * HALO
-PAD = WIDE + 16
+PAD = WIDE + 8
 FIRST = HALO - 1
 KEPT = ROWS + 2
+SOLVED_ROWS = 68
+PACKED_ROWS = 80
 GROUPS = 4
-BLOCK = 16
-LAST_BLOCK = 11
-BATCH = 8
-PACK_ROWS = 16
+BLOCKS = 2
+LAST_BLOCK = 22
+BATCH = 4
+PACK_ROWS = 32
 JBATCH = 4
 
 circ_weight = 0.2
@@ -65,14 +67,31 @@
 def split_matrix(matrix):
     high = matrix.astype(ml_dtypes.bfloat16)
     low = (matrix - high.astype(np.float64)).astype(ml_dtypes.bfloat16)
-    return np.concatenate([high, high, low, low], axis=1)
-
-
-def transform(matrix, values):
-    high = values.astype(BF16)
-    low = (values - high.astype(F32)).astype(BF16)
-    stacked = jnp.concatenate([high, low, high, low], axis=0)
-    return jnp.dot(matrix, stacked, preferred_element_type=F32)
+    return np.concatenate([np.concatenate([m, m], axis=1) for m in (high, low)], axis=0)
+
+
+def transform(matrix_ref, count, take, give, stage_ref, result_ref):
+    def stage(i):
+        for e, values in enumerate(take(i)):
+            high = values.astype(BF16)
+            stage_ref[:NT, 128 * e : 128 * e + 128] = high
+            stage_ref[NT:, 128 * e : 128 * e + 128] = (values - high.astype(F32)).astype(BF16)
+
+    def step(i, _):
+        give(jnp.maximum(i - 1, 0), result_ref)
+        both = jnp.dot(matrix_ref[...], stage_ref[...], preferred_element_type=F32)
+        result_ref[...] = both[:NT] + both[NT:]
+        stage(jnp.minimum(i + 1, count - 1))
+        return 0
+
+    stage(0)
+    lax.fori_loop(0, count + 1, step, 0)
+
+
+TRANSFORM_SCRATCH = [
+    pltpu.VMEM((2 * NT, 128 * BATCH), BF16),
+    pltpu.VMEM((NT, 128 * BATCH), F32),
+]
 
 
 def lanes(rows=8):
@@ -166,23 +185,28 @@
     return 32 * (column % 3) + column // 3
 
 
-def spectrum(source, rows, offset, mob_ref, ini_ref, fwd_ref, coef_ref, s_ref, pa_ref, pb_ref, q_ref):
+def spectrum(sources, mob_ref, ini_ref, fwd_ref, coef_ref, s_ref, pa_ref, pb_ref, q_ref, *scratch):
     slot = lanes() // 32
     slot16 = lanes(NTM) // 32
-
-    def body(i, _):
-        first = i * BATCH
-        x = [
-            jnp.concatenate(halo_tiles(source, first + e, rows, slot16), axis=0)
-            for e in range(BATCH)
+    each = BATCH // len(sources)
+    rows = sources[0][1]
+
+    def take(i):
+        return [
+            jnp.concatenate(halo_tiles(source, i * each + e, rows, slot16), axis=0)
+            for source, _, _ in sources
+            for e in range(each)
         ]
-        coefs = transform(fwd_ref[...], jnp.concatenate(x, axis=1))
+
+    def give(i, coefs):
         c = coef_ref[2]
-        for e in range(BATCH):
-            row = first + e + offset
-            here = coefs[:, 128 * e : 128 * e + 128]
+        places = [i * each + e + offset for _, _, offset in sources for e in range(each)]
+        for e, row in enumerate(places):
+            lane = slice(128 * e, 128 * e + 128)
             parts = [
-                swap_blocks([here[16 * g + 8 * h : 16 * g + 8 * h + 8] for g in range(4)], slot, 3)
+                swap_blocks(
+                    [coefs[16 * g + 8 * h : 16 * g + 8 * h + 8, lane] for g in range(4)], slot, 3
+                )
                 for h in range(2)
             ]
             for k in range(3):
@@ -202,25 +226,25 @@
                 pa_ref[row, tile, :] = mob5 * k_a
                 pb_ref[row, tile, :] = mob5 * k_b
                 q_ref[row, tile, :] = mob5 * k_c
-        return 0
-
-    lax.fori_loop(0, rows // BATCH, body, 0)
-
-
-def transform_kernel(x_ref, mob_ref, ini_ref, fwd_ref, coef_ref, *outs):
-    spectrum(x_ref, ROWS, HALO, mob_ref, ini_ref, fwd_ref, coef_ref, *outs)
+
+    transform(fwd_ref, rows // each, take, give, *scratch)
+
+
+def transform_kernel(x_ref, *refs):
+    spectrum([(x_ref, ROWS, HALO)], *refs)
 
 
 def sweep_kernel(
     low_ref, high_ref, mob_ref, ini_ref, fwd_ref, coef_ref, s_in, pa_in, pb_in, q_in,
-    solved_ref, s_ref, pa_ref, pb_ref, q_ref, u_ref, w_ref,
+    solved_ref, s_ref, pa_ref, pb_ref, q_ref, u_ref, w_ref, *scratch,
 ):
     del s_in, pa_in, pb_in, q_in
-    for source, offset in ((low_ref, 0), (high_ref, HALO + ROWS)):
-        spectrum(source, HALO, offset, mob_ref, ini_ref, fwd_ref, coef_ref, s_ref, pa_ref, pb_ref, q_ref)
-
-    def apply(k, source, target, join=None, old=None, block=BLOCK, shift=0):
+    sources = [(low_ref, HALO, 0), (high_ref, HALO, HALO + ROWS)]
+    spectrum(sources, mob_ref, ini_ref, fwd_ref, coef_ref, s_ref, pa_ref, pb_ref, q_ref, *scratch)
+
+    def apply(k, source, target, join=None, old=None, shift=0):
         count = WIDE - 2 * k
+        block = -(-count // BLOCKS) if shift == 0 else LAST_BLOCK
 
         def load(row):
             return [source[row, 8 * m : 8 * m + 8, :] for m in range(6)]
@@ -270,11 +294,11 @@
         if power < 8:
             apply(k, source, u_ref, 0.2**power, u_ref)
         else:
-            apply(k, source, solved_ref, 0.2**power, u_ref, LAST_BLOCK, FIRST)
+            apply(k, source, solved_ref, 0.2**power, u_ref, FIRST)
 
 
 WIDE_BUFFER = pltpu.VMEM((PAD, 48, 128), F32)
-SOLVED = pltpu.VMEM((KEPT, 48, 128), F32)
+SOLVED = pltpu.VMEM((SOLVED_ROWS, 48, 128), F32)
 HALF_BUFFER = pltpu.VMEM((PAD, 24, 128), F32)
 
 
@@ -282,6 +306,7 @@
     return pl.pallas_call(
         transform_kernel,
         out_shape=(WIDE_BUFFER, HALF_BUFFER, HALF_BUFFER, HALF_BUFFER),
+        scratch_shapes=TRANSFORM_SCRATCH,
         compiler_params=pltpu.CompilerParams(vmem_limit_bytes=16 * MIB),
         name="transform_rows",
     )(*vmem(x, mob, ini), forward, coefs)
@@ -291,46 +316,42 @@
     return pl.pallas_call(
         sweep_kernel,
         out_shape=(SOLVED, WIDE_BUFFER, HALF_BUFFER, HALF_BUFFER, HALF_BUFFER),
-        scratch_shapes=[WIDE_BUFFER, WIDE_BUFFER],
+        scratch_shapes=[WIDE_BUFFER, WIDE_BUFFER, *TRANSFORM_SCRATCH],
         input_output_aliases={6: 1, 7: 2, 8: 3, 9: 4},
         compiler_params=pltpu.CompilerParams(vmem_limit_bytes=24 * MIB),
         name="sweep",
     )(*vmem(low, high, mob, ini), forward, coefs, *vmem(*buffers))[0]
 
 
-def back_kernel(u_ref, traj_ref, x_ref, mob_ref, inv_ref, out_ref, sums_ref, dir_ref, packed_ref, sem):
+def back_kernel(u_ref, traj_ref, x_ref, mob_ref, inv_ref, out_ref, sums_ref, dir_ref, packed_ref, sem, *scratch):
     slot = lanes() // 32
     slot16 = lanes(NTM) // 32
     natural = natural_index(NT)
     low_half = lanes(NTM) < 64
 
-    def back(rows):
+    flat_ref = packed_ref.reshape(NTM * 2 * PACKED_ROWS, 128)
+
+    def take(i):
         y = []
-        for row in rows:
+        for row in (i * BATCH + e for e in range(BATCH)):
             halves = []
             for h in range(2):
                 t = [u_ref[row, 16 * k + 8 * h : 16 * k + 8 * h + 8, :] for k in range(3)]
                 halves.append(swap_blocks(t + [t[2]], slot, 4))
             y.append(jnp.concatenate([halves[h][g] for g in range(4) for h in range(2)], axis=0))
-        values = transform(inv_ref[...], jnp.concatenate(y, axis=1))
-        out = []
-        for e, row in enumerate(rows):
-            v = permute_lanes(values[:, 128 * e : 128 * e + 128], natural)
+        return y
+
+    def give(i, result):
+        for e in range(BATCH):
+            row = i * BATCH + e
+            v = permute_lanes(result[:, 128 * e : 128 * e + 128], natural)
             dir_ref[row] = v
-            out.append(v)
-        return out
-
-    back([0, KEPT - 1])
-
-    def back_body(i, _):
-        for e, v in enumerate(back([i * BATCH + e + 1 for e in range(BATCH)])):
             for j in range(2):
                 both = jnp.where(low_half, v[32 * j : 32 * j + 16], roll(v[32 * j + 16 : 32 * j + 32], 64))
-                packed_ref[pl.ds(i * BATCH + e + ROWS * j, NTM, stride=2 * ROWS), :] = both
-        return 0
-
-    lax.fori_loop(0, ROWS // BATCH, back_body, 0)
-    copy = pltpu.make_async_copy(packed_ref, out_ref, sem)
+                flat_ref[pl.ds(row + 7 + PACKED_ROWS * j, NTM, stride=2 * PACKED_ROWS), :] = both
+
+    transform(inv_ref, -(-KEPT // BATCH), take, give, *scratch)
+    copy = pltpu.make_async_copy(packed_ref.at[:, pl.ds(8, ROWS), :], out_ref, sem)
     copy.start()
     jacobian_sums(dir_ref, traj_ref, x_ref, mob_ref, sums_ref, natural, slot16)
     copy.wait()
@@ -341,11 +362,12 @@
         back_kernel,
         in_specs=[pl.BlockSpec(memory_space=pltpu.VMEM)] * 5,
         out_specs=(pl.BlockSpec(memory_space=pltpu.HBM), pl.BlockSpec(memory_space=pltpu.VMEM)),
-        out_shape=(pltpu.HBM((NTM * 2 * ROWS, 128), F32), pltpu.VMEM((8, 128), F32)),
+        out_shape=(pltpu.HBM((NTM * 2, ROWS, 128), F32), pltpu.VMEM((8, 128), F32)),
         scratch_shapes=[
-            pltpu.VMEM((KEPT, NT, 128), F32),
-            pltpu.VMEM((NTM * 2 * ROWS, 128), F32),
+            pltpu.VMEM((SOLVED_ROWS, NT, 128), F32),
+            pltpu.VMEM((NTM * 2, PACKED_ROWS, 128), F32),
             pltpu.SemaphoreType.DMA,
+            *TRANSFORM_SCRATCH,
         ],
         compiler_params=pltpu.CompilerParams(vmem_limit_bytes=16 * MIB),
         name="back",
@@ -371,8 +393,8 @@
         traj = own(traj_ref, r)
         res = jnp.concatenate(halo_tiles(x_ref, r, ROWS, slot), axis=0)
         res = permute_lanes(res, natural)
-        reaction = reaction_scale * (3.0 * traj * traj - 1.0)
-        applied = (v - earlier) / time_step + mob * (4.0 * v - neighbours) + reaction * v
+        own_factor = (1.0 / time_step - reaction_scale + 4.0 * mob) + (3.0 * reaction_scale) * (traj * traj)
+        applied = own_factor * v - (1.0 / time_step) * earlier - mob * neighbours
         return [fold(p) for p in (res * res, res * applied, applied * applied)]
 
     def body(i, sums):

time: 112 us -> 109 us (0.973)
  Pallas kernels: 35 us -> 30.6 us
  waiting for transfers between devices: 25.1 us -> 26.3 us
    pallas_call x1, Pallas kernels: 13.6 us -> 11.7 us  [sweep(): pl.pallas_call(sweep_kernel, out_shape=(SOLVED, WIDE_BUFFER, HALF_BUFFER,...]
  transfers between devices with their start and end apart: 17 -> 17, of which waited for: 10 -> 10; matrix products, arithmetic and copies ran while one was open for 4% -> 4% of each run, Pallas kernels for 18% -> 15%
where the time goes in v4:
time: 109 us; the launch traced here: 108 us
  starting transfers between devices  42.8 us (39%)
  Pallas kernels  30.6 us (28%)
  waiting for transfers between devices  26.3 us (24%)
  local copies, waits for them, and re-layouts  7.34 us (7%)
    ppermute x14, starting transfers between devices, shifted(): lax.ppermute(array, axes, [(i, (i + distance) % size) for i in range(size)])  21.9 us
    all_to_all x3, starting transfers between devices, swap(): return lax.all_to_all(blocks, TM, split_axis=0, concat_axis=0, tiled=True)  20.9 us
    ppermute x14, waiting for transfers between devices, shifted(): lax.ppermute(array, axes, [(i, (i + distance) % size) for i in range(size)])  13.4 us
    all_to_all x3, waiting for transfers between devices, swap(): return lax.all_to_all(blocks, TM, split_axis=0, concat_axis=0, tiled=True)  12.9 us
    pallas_call x1, Pallas kernels, sweep(): pl.pallas_call(sweep_kernel, out_shape=(SOLVED, WIDE_BUFFER, HALF_BUFFER,...  11.7 us
    pallas_call x1, Pallas kernels, back(): pl.pallas_call(back_kernel, in_specs=[pl.BlockSpec(memory_space=pltpu.VME...  9.81 us
    pallas_call x2, Pallas kernels, pack(): pl.pallas_call(kernel, grid=(ROWS // PACK_ROWS,), in_specs=[pl.BlockSpec(...  4.32 us
    unnamed x18, local copies, waits for them, and re-layouts  3.89 us
  transfers between devices with their start and end apart: 17, of which 10 were waited for; matrix products, arithmetic and copies ran while one was open for 4% of the time, Pallas kernels for 15%

profile of v4, /device:TPU:6, one launch (start us, length us, event | category | flops | bytes accessed | tf_op | source)
XLA Modules:
  0.0 108.4 jit_solution(1479523797752404459)
XLA Ops:
  0.6 1.2 %copy-done.2 = f32[4,64,1024]{2,1,0:T(8,128)S(1)} copy-done((f32[4,64,1024]{2,1,0:T(8,128)S(1)}, f32[4,64,1024]{2,1,0:T(8,128)}, u32[]{:S(2)}) %copy-start.2) | copy-done | bytes 1048600
  1.9 3.0 %pack_halo.1 = f32[16,3,64,128]{3,2,1,0:T(8,128)} custom-call(f32[4,64,1024]{2,1,0:T(8,128)S(1)} %copy-done.2), custom_call_target="tpu_custom_call" | custom-call | tf_op jit(solution)/shard_map/pack_halo/pallas_call | solution.py:145
  4.9 7.6 %all-to-all-start = ((f32[16,3,64,128]{3,2,1,0:T(8,128)}), f32[16,3,64,128]{3,2,1,0:T(8,128)S(1)}, u32[]{:S(2)}, u32[]{:S(2)}) async-start(f32[16,3,64,128]{3,2,1,0:T(8,128)} %pack_halo.1), calls=%async_computation | async-start | bytes 3145728 | tf_op jit(solution)/shard_map/all_to_all | solution.py:456
  14.5 3.0 %collective-permute-start.3 = (f32[2,16,128]{2,1,0:T(8,128)S(1)}, f32[2,16,128]{2,1,0:T(8,128)S(1)}, u32[]{:S(2)}, u32[]{:S(2)}) collective-permute-start(f32[2,16,128]{2,1,0:T(8,128)S(1)} %get-tuple-element.33), channel_id=1, source_target_pairs={{0,7},{1,0},{2,1},{3,2},{4,3},{5,4},{6,5},{7,6},{8,15},{9,8},{10,9... | collective-permute-start | bytes 49160 | tf_op jit(solution)/shard_map/ppermute | solution.py:460
  19.7 1.3 %pack.1 = f32[16,2,64,128]{3,2,1,0:T(8,128)} custom-call(f32[4,64,1024]{2,1,0:T(8,128)S(1)} %copy-done.3), custom_call_target="tpu_custom_call" | custom-call | tf_op jit(solution)/shard_map/pack/pallas_call | solution.py:145
  21.0 12.9 %all-to-all-done = f32[16,3,64,128]{3,2,1,0:T(8,128)S(1)} async-done(((f32[16,3,64,128]{3,2,1,0:T(8,128)}), f32[16,3,64,128]{3,2,1,0:T(8,128)S(1)}, u32[]{:S(2)}, u32[]{:S(2)}) %all-to-all-start) | async-done | bytes 1572896 | tf_op jit(solution)/shard_map/all_to_all | solution.py:456
  33.9 6.1 %all-to-all-start.1 = ((f32[16,2,64,128]{3,2,1,0:T(8,128)}), f32[16,2,64,128]{3,2,1,0:T(8,128)S(1)}, u32[]{:S(2)}, u32[]{:S(2)}) async-start(f32[16,2,64,128]{3,2,1,0:T(8,128)} %pack.1), calls=%async_computation.1 | async-start | bytes 2097152 | tf_op jit(solution)/shard_map/all_to_all | solution.py:456
  40.2 2.9 %collective-permute-start.1 = (f32[16,3,16,128]{3,2,1,0:T(8,128)S(1)}, f32[16,3,16,128]{3,2,1,0:T(8,128)S(1)}, u32[]{:S(2)}, u32[]{:S(2)}) collective-permute-start(f32[16,3,16,128]{3,2,1,0:T(8,128)S(1)} %get-tuple-element.30), channel_id=1, source_target_pairs={{0,7},{1,0},{2,1},{3,2},{4,3},{5,4},{6,5},{7,6},{8,15},{9,8},{10,9... | collective-permute-start | bytes 1179656 | tf_op jit(solution)/shard_map/ppermute | solution.py:460
  43.3 3.5 %transform_rows.1 = (f32[104,48,128]{2,1,0:T(8,128)S(1)}, f32[104,24,128]{2,1,0:T(8,128)S(1)}, f32[104,24,128]{2,1,0:T(8,128)S(1)}, f32[104,24,128]{2,1,0:T(8,128)S(1)}) custom-call(f32[3072,128]{1,0:T(8,128)S(1)} %bitcast.21, f32[3,96,128]{2,1,0:T(8,128)S(1)} %get-tuple-element.16.refs_0_.mob_ref, f32[3,96,128]{2,1,0:T(8,128)S(1)} %get-tuple-element.17.refs_1_.ini_ref, ...), custom_call_target="tpu_custom_call" | custom-call | tf_op jit(solution)/shard_map/transform_rows/pallas_call | solution.py:306
  46.9 1.7 %collective-permute-done = f32[16,3,16,128]{3,2,1,0:T(8,128)S(1)} collective-permute-done((f32[16,3,16,128]{3,2,1,0:T(8,128)S(1)}, f32[16,3,16,128]{3,2,1,0:T(8,128)S(1)}, u32[]{:S(2)}, u32[]{:S(2)}) %collective-permute-start) | collective-permute-done | bytes 393248 | tf_op jit(solution)/shard_map/ppermute | solution.py:460
  48.6 11.7 %sweep.1 = (f32[68,48,128]{2,1,0:T(8,128)S(1)}, f32[104,48,128]{2,1,0:T(8,128)S(1)}, f32[104,24,128]{2,1,0:T(8,128)S(1)}, f32[104,24,128]{2,1,0:T(8,128)S(1)}, f32[104,24,128]{2,1,0:T(8,128)S(1)}) custom-call(f32[768,128]{1,0:T(8,128)S(1)} %bitcast.24, ...), custom_call_target="tpu_custom_call", output_to_operand_aliasing={{1}: (6, {}), {2}: (7, {}), {3}: (8, {}), {4}: (9, {})} | custom-call | tf_op jit(solution)/shard_map/sweep/pallas_call | solution.py:316
  61.5 1.4 %copy-done.1 = f32[68,48,128]{2,1,0:T(8,128)S(1)} copy-done((f32[68,48,128]{2,1,0:T(8,128)S(1)}, f32[68,48,128]{2,1,0:T(8,128)}, u32[]{:S(2)}) %copy-start.1) | copy-done | bytes 1671192
  62.9 9.8 %back.1 = (f32[32,64,128]{2,1,0:T(8,128)}, f32[8,128]{1,0:T(8,128)S(1)}) custom-call(f32[68,48,128]{2,1,0:T(8,128)S(1)} %copy-done.1, f32[2048,128]{1,0:T(8,128)S(1)} %bitcast.23, f32[3072,128]{1,0:T(8,128)S(1)} %bitcast.22, f32[96,128]{1,0:T(8,128)S(1)} %pad_maximum_fusion.4.mob_ref, bf16[128,128]{1,0:T(8,128)(2,1)S(1)} %copy-done.6), custom_call_target="tpu_custom_call" | custom-call | tf_op jit(solution)/shard_map/back/pallas_call | solution.py:361
  74.7 7.2 %all-to-all-start.2 = ((f32[16,2,64,128]{3,2,1,0:T(8,128)}), f32[16,2,64,128]{3,2,1,0:T(8,128)S(1)}, u32[]{:S(2)}, u32[]{:S(2)}) async-start(f32[16,2,64,128]{3,2,1,0:T(8,128)} %bitcast.32), calls=%async_computation.2 | async-start | bytes 2097152 | tf_op jit(solution)/shard_map/all_to_all | solution.py:456
  82.0 3.6 %collective-permute-start.5 = (f32[8,128]{1,0:T(8,128)S(1)}, f32[8,128]{1,0:T(8,128)S(1)}, u32[]{:S(2)}, u32[]{:S(2)}) collective-permute-start(f32[8,128]{1,0:T(8,128)S(1)} %add.38), channel_id=1, source_target_pairs={{0,4},{2,6},{4,0},{6,2},{1,5},{3,7},{5,1},{7,3},{8,12},{10,14},{12... | collective-permute-start | bytes 12296 | tf_op jit(solution)/shard_map/ppermute | solution.py:460
  85.6 3.2 %collective-permute-start.7 = (f32[8,128]{1,0:T(8,128)S(1)}, f32[8,128]{1,0:T(8,128)S(1)}, u32[]{:S(2)}, u32[]{:S(2)}) collective-permute-start(f32[8,128]{1,0:T(8,128)S(1)} %add.38), channel_id=1, source_target_pairs={{0,6},{2,0},{4,2},{6,4},{1,7},{3,1},{5,3},{7,5},{8,14},{10,8},{12,... | collective-permute-start | bytes 12296 | tf_op jit(solution)/shard_map/ppermute | solution.py:460
  88.8 1.6 %collective-permute-done.6 = f32[8,128]{1,0:T(8,128)S(1)} collective-permute-done((f32[8,128]{1,0:T(8,128)S(1)}, f32[8,128]{1,0:T(8,128)S(1)}, u32[]{:S(2)}, u32[]{:S(2)}) %collective-permute-start.6) | collective-permute-done | bytes 4128 | tf_op jit(solution)/shard_map/ppermute | solution.py:460
  90.4 2.7 %collective-permute-start.10 = (f32[8,128]{1,0:T(8,128)S(1)}, f32[8,128]{1,0:T(8,128)S(1)}, u32[]{:S(2)}, u32[]{:S(2)}) collective-permute-start(f32[8,128]{1,0:T(8,128)S(1)} %add_add_fusion.2), channel_id=1, source_target_pairs={{0,24},{8,0},{16,8},{24,16},{1,25},{9,1},{17,9},{25,17},{2,26},{10... | collective-permute-start | bytes 12296 | tf_op jit(solution)/shard_map/ppermute | solution.py:460
  95.6 2.6 %collective-permute-done.8 = f32[8,128]{1,0:T(8,128)S(1)} collective-permute-done((f32[8,128]{1,0:T(8,128)S(1)}, f32[8,128]{1,0:T(8,128)S(1)}, u32[]{:S(2)}, u32[]{:S(2)}) %collective-permute-start.8) | collective-permute-done | bytes 4128 | tf_op jit(solution)/shard_map/ppermute | solution.py:460
  98.8 1.5 %collective-permute-start.11 = (f32[8,128]{1,0:T(8,128)S(1)}, f32[8,128]{1,0:T(8,128)S(1)}, u32[]{:S(2)}, u32[]{:S(2)}) collective-permute-start(f32[8,128]{1,0:T(8,128)S(1)} %add_add_fusion.1), channel_id=1, source_target_pairs={{0,64},{32,96},{64,0},{96,32},{1,65},{33,97},{65,1},{97,33},{2,66}... | collective-permute-start | bytes 12296 | tf_op jit(solution)/shard_map/ppermute | solution.py:460
  100.3 2.1 %collective-permute-start.12 = (f32[8,128]{1,0:T(8,128)S(1)}, f32[8,128]{1,0:T(8,128)S(1)}, u32[]{:S(2)}, u32[]{:S(2)}) collective-permute-start(f32[8,128]{1,0:T(8,128)S(1)} %add_add_fusion.1), channel_id=1, source_target_pairs={{0,32},{32,64},{64,96},{96,0},{1,33},{33,65},{65,97},{97,1},{2,34}... | collective-permute-start | bytes 12296 | tf_op jit(solution)/shard_map/ppermute | solution.py:460
  102.3 1.6 %collective-permute-done.11 = f32[8,128]{1,0:T(8,128)S(1)} collective-permute-done((f32[8,128]{1,0:T(8,128)S(1)}, f32[8,128]{1,0:T(8,128)S(1)}, u32[]{:S(2)}, u32[]{:S(2)}) %collective-permute-start.11) | collective-permute-done | bytes 4128 | tf_op jit(solution)/shard_map/ppermute | solution.py:460
  103.9 3.2 %collective-permute-done.13 = f32[8,128]{1,0:T(8,128)S(1)} collective-permute-done((f32[8,128]{1,0:T(8,128)S(1)}, f32[8,128]{1,0:T(8,128)S(1)}, u32[]{:S(2)}, u32[]{:S(2)}) %collective-permute-start.13) | collective-permute-done | bytes 4128 | tf_op jit(solution)/shard_map/ppermute | solution.py:460
  107.2 1.3 %finish.1 = (f32[4,64,1024]{2,1,0:T(8,128)}, f32[1,1]{1,0:T(1,128)}) custom-call(f32[16,2,64,128]{3,2,1,0:T(8,128)S(1)} %all-to-all-done.2.blocks_ref, f32[8,128]{1,0:T(8,128)S(1)} %add_add_fusion.sums_ref), custom_call_target="tpu_custom_call" | custom-call | tf_op jit(solution)/shard_map/finish/pallas_call | solution.py:438
  (56 shorter events, 10.8 us)
Async XLA Ops:
  4.9 7.6 %copy-start.7 = (f32[64,1024]{1,0:T(8,128)S(1)}, f32[64,1024]{1,0:T(8,128)}, u32[]{:S(2)}) copy-start(f32[64,1024]{1,0:T(8,128)} %param.10) | copy-start | bytes 786436
  4.9 7.6 %copy-start.8 = (f32[64,1024]{1,0:T(8,128)S(1)}, f32[64,1024]{1,0:T(8,128)}, u32[]{:S(2)}) copy-start(f32[64,1024]{1,0:T(8,128)} %param.8) | copy-start | bytes 786436
  4.9 29.1 %all-to-all-start = ((f32[16,3,64,128]{3,2,1,0:T(8,128)}), f32[16,3,64,128]{3,2,1,0:T(8,128)S(1)}, u32[]{:S(2)}, u32[]{:S(2)}) async-start(f32[16,3,64,128]{3,2,1,0:T(8,128)} %pack_halo.1), calls=%async_computation | async-start | bytes 3145728 | tf_op jit(solution)/shard_map/all_to_all | solution.py:456
  12.6 7.1 %copy-start.3 = (f32[4,64,1024]{2,1,0:T(8,128)S(1)}, f32[4,64,1024]{2,1,0:T(8,128)}, u32[]{:S(2)}) copy-start(f32[4,64,1024]{2,1,0:T(8,128)} %in_ref.2) | copy-start | bytes 3145732
  14.5 4.4 %collective-permute-start.2 = (f32[2,16,128]{2,1,0:T(8,128)S(1)}, f32[2,16,128]{2,1,0:T(8,128)S(1)}, u32[]{:S(2)}, u32[]{:S(2)}) collective-permute-start(f32[2,16,128]{2,1,0:T(8,128)S(1)} %get-tuple-element.32), channel_id=1, source_target_pairs={{0,1},{1,2},{2,3},{3,4},{4,5},{5,6},{6,7},{7,0},{8,9},{9,10},{10,1... | collective-permute-start | bytes 49160 | tf_op jit(solution)/shard_map/ppermute | solution.py:460
  14.5 4.4 %collective-permute-start.3 = (f32[2,16,128]{2,1,0:T(8,128)S(1)}, f32[2,16,128]{2,1,0:T(8,128)S(1)}, u32[]{:S(2)}, u32[]{:S(2)}) collective-permute-start(f32[2,16,128]{2,1,0:T(8,128)S(1)} %get-tuple-element.33), channel_id=1, source_target_pairs={{0,7},{1,0},{2,1},{3,2},{4,3},{5,4},{6,5},{7,6},{8,15},{9,8},{10,9... | collective-permute-start | bytes 49160 | tf_op jit(solution)/shard_map/ppermute | solution.py:460
  21.0 22.3 %copy-start.4 = (bf16[128,128]{1,0:T(8,128)(2,1)S(1)}, bf16[128,128]{1,0:T(8,128)(2,1)}, u32[]{:S(2)}) copy-start(bf16[128,128]{1,0:T(8,128)(2,1)} %constant.23.clone.refs_2_.fwd_ref) | copy-start | bytes 98308
  21.0 22.3 %copy-start.5 = (f32[3,8,128]{2,1,0:T(8,128)S(1)}, f32[3,8,128]{2,1,0:T(8,128)}, u32[]{:S(2)}) copy-start(f32[3,8,128]{2,1,0:T(8,128)} %constant.24.clone.refs_3_.coef_ref) | copy-start | bytes 36868
  33.9 27.5 %all-to-all-start.1 = ((f32[16,2,64,128]{3,2,1,0:T(8,128)}), f32[16,2,64,128]{3,2,1,0:T(8,128)S(1)}, u32[]{:S(2)}, u32[]{:S(2)}) async-start(f32[16,2,64,128]{3,2,1,0:T(8,128)} %pack.1), calls=%async_computation.1 | async-start | bytes 2097152 | tf_op jit(solution)/shard_map/all_to_all | solution.py:456
  40.2 8.4 %collective-permute-start = (f32[16,3,16,128]{3,2,1,0:T(8,128)S(1)}, f32[16,3,16,128]{3,2,1,0:T(8,128)S(1)}, u32[]{:S(2)}, u32[]{:S(2)}) collective-permute-start(f32[16,3,16,128]{3,2,1,0:T(8,128)S(1)} %get-tuple-element.31), channel_id=1, source_target_pairs={{0,1},{1,2},{2,3},{3,4},{4,5},{5,6},{6,7},{7,0},{8,9},{9,10},{10,1... | collective-permute-start | bytes 1179656 | tf_op jit(solution)/shard_map/ppermute | solution.py:460
  40.2 8.4 %collective-permute-start.1 = (f32[16,3,16,128]{3,2,1,0:T(8,128)S(1)}, f32[16,3,16,128]{3,2,1,0:T(8,128)S(1)}, u32[]{:S(2)}, u32[]{:S(2)}) collective-permute-start(f32[16,3,16,128]{3,2,1,0:T(8,128)S(1)} %get-tuple-element.30), channel_id=1, source_target_pairs={{0,7},{1,0},{2,1},{3,2},{4,3},{5,4},{6,5},{7,6},{8,15},{9,8},{10,9... | collective-permute-start | bytes 1179656 | tf_op jit(solution)/shard_map/ppermute | solution.py:460
  48.6 12.9 %copy-start.6 = (bf16[128,128]{1,0:T(8,128)(2,1)S(1)}, bf16[128,128]{1,0:T(8,128)(2,1)}, u32[]{:S(2)}) copy-start(bf16[128,128]{1,0:T(8,128)(2,1)} %constant.25.clone.inv_ref) | copy-start | bytes 98308
  61.5 1.4 %copy-start.1 = (f32[68,48,128]{2,1,0:T(8,128)S(1)}, f32[68,48,128]{2,1,0:T(8,128)}, u32[]{:S(2)}) copy-start(f32[68,48,128]{2,1,0:T(8,128)} %copy-done) | copy-start | bytes 5013508
  72.7 2.0 %collective-permute-start.4 = (f32[8,128]{1,0:T(8,128)S(1)}, f32[8,128]{1,0:T(8,128)S(1)}, u32[]{:S(2)}, u32[]{:S(2)}) collective-permute-start(f32[8,128]{1,0:T(8,128)S(1)} %get-tuple-element.25), channel_id=1, source_target_pairs={{0,1},{1,0},{2,3},{3,2},{4,5},{5,4},{6,7},{7,6},{8,9},{9,8},{10,11... | collective-permute-start | bytes 12296 | tf_op jit(solution)/shard_map/ppermute | solution.py:460
  74.7 32.4 %all-to-all-start.2 = ((f32[16,2,64,128]{3,2,1,0:T(8,128)}), f32[16,2,64,128]{3,2,1,0:T(8,128)S(1)}, u32[]{:S(2)}, u32[]{:S(2)}) async-start(f32[16,2,64,128]{3,2,1,0:T(8,128)} %bitcast.32), calls=%async_computation.2 | async-start | bytes 2097152 | tf_op jit(solution)/shard_map/all_to_all | solution.py:456
  82.0 6.8 %collective-permute-start.5 = (f32[8,128]{1,0:T(8,128)S(1)}, f32[8,128]{1,0:T(8,128)S(1)}, u32[]{:S(2)}, u32[]{:S(2)}) collective-permute-start(f32[8,128]{1,0:T(8,128)S(1)} %add.38), channel_id=1, source_target_pairs={{0,4},{2,6},{4,0},{6,2},{1,5},{3,7},{5,1},{7,3},{8,12},{10,14},{12... | collective-permute-start | bytes 12296 | tf_op jit(solution)/shard_map/ppermute | solution.py:460
  85.6 4.8 %collective-permute-start.6 = (f32[8,128]{1,0:T(8,128)S(1)}, f32[8,128]{1,0:T(8,128)S(1)}, u32[]{:S(2)}, u32[]{:S(2)}) collective-permute-start(f32[8,128]{1,0:T(8,128)S(1)} %add.38), channel_id=1, source_target_pairs={{0,2},{2,4},{4,6},{6,0},{1,3},{3,5},{5,7},{7,1},{8,10},{10,12},{12... | collective-permute-start | bytes 12296 | tf_op jit(solution)/shard_map/ppermute | solution.py:460
  85.6 4.8 %collective-permute-start.7 = (f32[8,128]{1,0:T(8,128)S(1)}, f32[8,128]{1,0:T(8,128)S(1)}, u32[]{:S(2)}, u32[]{:S(2)}) collective-permute-start(f32[8,128]{1,0:T(8,128)S(1)} %add.38), channel_id=1, source_target_pairs={{0,6},{2,0},{4,2},{6,4},{1,7},{3,1},{5,3},{7,5},{8,14},{10,8},{12,... | collective-permute-start | bytes 12296 | tf_op jit(solution)/shard_map/ppermute | solution.py:460
  90.4 5.3 %collective-permute-start.10 = (f32[8,128]{1,0:T(8,128)S(1)}, f32[8,128]{1,0:T(8,128)S(1)}, u32[]{:S(2)}, u32[]{:S(2)}) collective-permute-start(f32[8,128]{1,0:T(8,128)S(1)} %add_add_fusion.2), channel_id=1, source_target_pairs={{0,24},{8,0},{16,8},{24,16},{1,25},{9,1},{17,9},{25,17},{2,26},{10... | collective-permute-start | bytes 12296 | tf_op jit(solution)/shard_map/ppermute | solution.py:460
  93.1 5.1 %collective-permute-start.8 = (f32[8,128]{1,0:T(8,128)S(1)}, f32[8,128]{1,0:T(8,128)S(1)}, u32[]{:S(2)}, u32[]{:S(2)}) collective-permute-start(f32[8,128]{1,0:T(8,128)S(1)} %add_add_fusion.2), channel_id=1, source_target_pairs={{0,16},{8,24},{16,0},{24,8},{1,17},{9,25},{17,1},{25,9},{2,18},{10... | collective-permute-start | bytes 12296 | tf_op jit(solution)/shard_map/ppermute | solution.py:460
  94.0 4.8 %collective-permute-start.9 = (f32[8,128]{1,0:T(8,128)S(1)}, f32[8,128]{1,0:T(8,128)S(1)}, u32[]{:S(2)}, u32[]{:S(2)}) collective-permute-start(f32[8,128]{1,0:T(8,128)S(1)} %add_add_fusion.2), channel_id=1, source_target_pairs={{0,8},{8,16},{16,24},{24,0},{1,9},{9,17},{17,25},{25,1},{2,10},{10... | collective-permute-start | bytes 12296 | tf_op jit(solution)/shard_map/ppermute | solution.py:460
  98.8 5.1 %collective-permute-start.11 = (f32[8,128]{1,0:T(8,128)S(1)}, f32[8,128]{1,0:T(8,128)S(1)}, u32[]{:S(2)}, u32[]{:S(2)}) collective-permute-start(f32[8,128]{1,0:T(8,128)S(1)} %add_add_fusion.1), channel_id=1, source_target_pairs={{0,64},{32,96},{64,0},{96,32},{1,65},{33,97},{65,1},{97,33},{2,66}... | collective-permute-start | bytes 12296 | tf_op jit(solution)/shard_map/ppermute | solution.py:460
  100.3 3.7 %collective-permute-start.12 = (f32[8,128]{1,0:T(8,128)S(1)}, f32[8,128]{1,0:T(8,128)S(1)}, u32[]{:S(2)}, u32[]{:S(2)}) collective-permute-start(f32[8,128]{1,0:T(8,128)S(1)} %add_add_fusion.1), channel_id=1, source_target_pairs={{0,32},{32,64},{64,96},{96,0},{1,33},{33,65},{65,97},{97,1},{2,34}... | collective-permute-start | bytes 12296 | tf_op jit(solution)/shard_map/ppermute | solution.py:460
  102.3 4.8 %collective-permute-start.13 = (f32[8,128]{1,0:T(8,128)S(1)}, f32[8,128]{1,0:T(8,128)S(1)}, u32[]{:S(2)}, u32[]{:S(2)}) collective-permute-start(f32[8,128]{1,0:T(8,128)S(1)} %add_add_fusion.1), channel_id=1, source_target_pairs={{0,96},{32,0},{64,32},{96,64},{1,97},{33,1},{65,33},{97,65},{2,98}... | collective-permute-start | bytes 12296 | tf_op jit(solution)/shard_map/ppermute | solution.py:460
  (2 other events, 2.4 us)

commit v5 on v4

--- a/solution.py
+++ b/solution.py
@@ -26,8 +26,8 @@
 SOLVED_ROWS = 68
 PACKED_ROWS = 80
 GROUPS = 4
-BLOCKS = 2
-LAST_BLOCK = 22
+BLOCKS = 1
+LAST_BLOCK = 66
 BATCH = 4
 PACK_ROWS = 32
 JBATCH = 4

time: 109 us -> 107 us (0.982)
  Pallas kernels: 30.6 us -> 29 us
    pallas_call x1, Pallas kernels: 11.7 us -> 10 us  [sweep(): pl.pallas_call(sweep_kernel, out_shape=(SOLVED, WIDE_BUFFER, HALF_BUFFER,...]
  transfers between devices with their start and end apart: 17 -> 17, of which waited for: 10 -> 10; matrix products, arithmetic and copies ran while one was open for 4% -> 4% of each run, Pallas kernels for 15% -> 14%
where the time goes in v5:
time: 107 us
  starting transfers between devices  42.9 us (40%)
  Pallas kernels  29 us (27%)
  waiting for transfers between devices  26.3 us (25%)
  local copies, waits for them, and re-layouts  7.34 us (7%)
    ppermute x14, starting transfers between devices, shifted(): lax.ppermute(array, axes, [(i, (i + distance) % size) for i in range(size)])  21.9 us
    all_to_all x3, starting transfers between devices, swap(): return lax.all_to_all(blocks, TM, split_axis=0, concat_axis=0, tiled=True)  20.9 us
    ppermute x14, waiting for transfers between devices, shifted(): lax.ppermute(array, axes, [(i, (i + distance) % size) for i in range(size)])  13.4 us
    all_to_all x3, waiting for transfers between devices, swap(): return lax.all_to_all(blocks, TM, split_axis=0, concat_axis=0, tiled=True)  12.9 us
    pallas_call x1, Pallas kernels, sweep(): pl.pallas_call(sweep_kernel, out_shape=(SOLVED, WIDE_BUFFER, HALF_BUFFER,...  10 us
    pallas_call x1, Pallas kernels, back(): pl.pallas_call(back_kernel, in_specs=[pl.BlockSpec(memory_space=pltpu.VME...  9.81 us
    pallas_call x2, Pallas kernels, pack(): pl.pallas_call(kernel, grid=(ROWS // PACK_ROWS,), in_specs=[pl.BlockSpec(...  4.32 us
    unnamed x18, local copies, waits for them, and re-layouts  3.89 us
  transfers between devices with their start and end apart: 17, of which 10 were waited for; matrix products, arithmetic and copies ran while one was open for 4% of the time, Pallas kernels for 14%

profile of v5, /device:TPU:6, one launch (start us, length us, event | category | flops | bytes accessed | tf_op | source)
XLA Modules:
  0.0 106.8 jit_solution(10262839170228016159)
XLA Ops:
  0.6 1.2 %copy-done.2 = f32[4,64,1024]{2,1,0:T(8,128)S(1)} copy-done((f32[4,64,1024]{2,1,0:T(8,128)S(1)}, f32[4,64,1024]{2,1,0:T(8,128)}, u32[]{:S(2)}) %copy-start.2) | copy-done | bytes 1048600
  1.9 3.0 %pack_halo.1 = f32[16,3,64,128]{3,2,1,0:T(8,128)} custom-call(f32[4,64,1024]{2,1,0:T(8,128)S(1)} %copy-done.2), custom_call_target="tpu_custom_call" | custom-call | tf_op jit(solution)/shard_map/pack_halo/pallas_call | solution.py:145
  4.9 7.6 %all-to-all-start = ((f32[16,3,64,128]{3,2,1,0:T(8,128)}), f32[16,3,64,128]{3,2,1,0:T(8,128)S(1)}, u32[]{:S(2)}, u32[]{:S(2)}) async-start(f32[16,3,64,128]{3,2,1,0:T(8,128)} %pack_halo.1), calls=%async_computation | async-start | bytes 3145728 | tf_op jit(solution)/shard_map/all_to_all | solution.py:456
  14.5 3.0 %collective-permute-start.3 = (f32[2,16,128]{2,1,0:T(8,128)S(1)}, f32[2,16,128]{2,1,0:T(8,128)S(1)}, u32[]{:S(2)}, u32[]{:S(2)}) collective-permute-start(f32[2,16,128]{2,1,0:T(8,128)S(1)} %get-tuple-element.33), channel_id=1, source_target_pairs={{0,7},{1,0},{2,1},{3,2},{4,3},{5,4},{6,5},{7,6},{8,15},{9,8},{10,9... | collective-permute-start | bytes 49160 | tf_op jit(solution)/shard_map/ppermute | solution.py:460
  19.7 1.3 %pack.1 = f32[16,2,64,128]{3,2,1,0:T(8,128)} custom-call(f32[4,64,1024]{2,1,0:T(8,128)S(1)} %copy-done.3), custom_call_target="tpu_custom_call" | custom-call | tf_op jit(solution)/shard_map/pack/pallas_call | solution.py:145
  21.0 12.9 %all-to-all-done = f32[16,3,64,128]{3,2,1,0:T(8,128)S(1)} async-done(((f32[16,3,64,128]{3,2,1,0:T(8,128)}), f32[16,3,64,128]{3,2,1,0:T(8,128)S(1)}, u32[]{:S(2)}, u32[]{:S(2)}) %all-to-all-start) | async-done | bytes 1572896 | tf_op jit(solution)/shard_map/all_to_all | solution.py:456
  33.9 6.1 %all-to-all-start.1 = ((f32[16,2,64,128]{3,2,1,0:T(8,128)}), f32[16,2,64,128]{3,2,1,0:T(8,128)S(1)}, u32[]{:S(2)}, u32[]{:S(2)}) async-start(f32[16,2,64,128]{3,2,1,0:T(8,128)} %pack.1), calls=%async_computation.1 | async-start | bytes 2097152 | tf_op jit(solution)/shard_map/all_to_all | solution.py:456
  40.2 2.9 %collective-permute-start.1 = (f32[16,3,16,128]{3,2,1,0:T(8,128)S(1)}, f32[16,3,16,128]{3,2,1,0:T(8,128)S(1)}, u32[]{:S(2)}, u32[]{:S(2)}) collective-permute-start(f32[16,3,16,128]{3,2,1,0:T(8,128)S(1)} %get-tuple-element.30), channel_id=1, source_target_pairs={{0,7},{1,0},{2,1},{3,2},{4,3},{5,4},{6,5},{7,6},{8,15},{9,8},{10,9... | collective-permute-start | bytes 1179656 | tf_op jit(solution)/shard_map/ppermute | solution.py:460
  43.3 3.5 %transform_rows.1 = (f32[104,48,128]{2,1,0:T(8,128)S(1)}, f32[104,24,128]{2,1,0:T(8,128)S(1)}, f32[104,24,128]{2,1,0:T(8,128)S(1)}, f32[104,24,128]{2,1,0:T(8,128)S(1)}) custom-call(f32[3072,128]{1,0:T(8,128)S(1)} %bitcast.21, f32[3,96,128]{2,1,0:T(8,128)S(1)} %get-tuple-element.16.refs_0_.mob_ref, f32[3,96,128]{2,1,0:T(8,128)S(1)} %get-tuple-element.17.refs_1_.ini_ref, ...), custom_call_target="tpu_custom_call" | custom-call | tf_op jit(solution)/shard_map/transform_rows/pallas_call | solution.py:306
  46.8 1.7 %collective-permute-done = f32[16,3,16,128]{3,2,1,0:T(8,128)S(1)} collective-permute-done((f32[16,3,16,128]{3,2,1,0:T(8,128)S(1)}, f32[16,3,16,128]{3,2,1,0:T(8,128)S(1)}, u32[]{:S(2)}, u32[]{:S(2)}) %collective-permute-start) | collective-permute-done | bytes 393248 | tf_op jit(solution)/shard_map/ppermute | solution.py:460
  48.6 10.0 %sweep.1 = (f32[68,48,128]{2,1,0:T(8,128)S(1)}, f32[104,48,128]{2,1,0:T(8,128)S(1)}, f32[104,24,128]{2,1,0:T(8,128)S(1)}, f32[104,24,128]{2,1,0:T(8,128)S(1)}, f32[104,24,128]{2,1,0:T(8,128)S(1)}) custom-call(f32[768,128]{1,0:T(8,128)S(1)} %bitcast.24, ...), custom_call_target="tpu_custom_call", output_to_operand_aliasing={{1}: (6, {}), {2}: (7, {}), {3}: (8, {}), {4}: (9, {})} | custom-call | tf_op jit(solution)/shard_map/sweep/pallas_call | solution.py:316
  59.8 1.4 %copy-done.1 = f32[68,48,128]{2,1,0:T(8,128)S(1)} copy-done((f32[68,48,128]{2,1,0:T(8,128)S(1)}, f32[68,48,128]{2,1,0:T(8,128)}, u32[]{:S(2)}) %copy-start.1) | copy-done | bytes 1671192
  61.3 9.8 %back.1 = (f32[32,64,128]{2,1,0:T(8,128)}, f32[8,128]{1,0:T(8,128)S(1)}) custom-call(f32[68,48,128]{2,1,0:T(8,128)S(1)} %copy-done.1, f32[2048,128]{1,0:T(8,128)S(1)} %bitcast.23, f32[3072,128]{1,0:T(8,128)S(1)} %bitcast.22, f32[96,128]{1,0:T(8,128)S(1)} %pad_maximum_fusion.4.mob_ref, bf16[128,128]{1,0:T(8,128)(2,1)S(1)} %copy-done.6), custom_call_target="tpu_custom_call" | custom-call | tf_op jit(solution)/shard_map/back/pallas_call | solution.py:361
  73.1 7.2 %all-to-all-start.2 = ((f32[16,2,64,128]{3,2,1,0:T(8,128)}), f32[16,2,64,128]{3,2,1,0:T(8,128)S(1)}, u32[]{:S(2)}, u32[]{:S(2)}) async-start(f32[16,2,64,128]{3,2,1,0:T(8,128)} %bitcast.32), calls=%async_computation.2 | async-start | bytes 2097152 | tf_op jit(solution)/shard_map/all_to_all | solution.py:456
  80.4 3.6 %collective-permute-start.5 = (f32[8,128]{1,0:T(8,128)S(1)}, f32[8,128]{1,0:T(8,128)S(1)}, u32[]{:S(2)}, u32[]{:S(2)}) collective-permute-start(f32[8,128]{1,0:T(8,128)S(1)} %add.38), channel_id=1, source_target_pairs={{0,4},{2,6},{4,0},{6,2},{1,5},{3,7},{5,1},{7,3},{8,12},{10,14},{12... | collective-permute-start | bytes 12296 | tf_op jit(solution)/shard_map/ppermute | solution.py:460
  83.9 3.2 %collective-permute-start.7 = (f32[8,128]{1,0:T(8,128)S(1)}, f32[8,128]{1,0:T(8,128)S(1)}, u32[]{:S(2)}, u32[]{:S(2)}) collective-permute-start(f32[8,128]{1,0:T(8,128)S(1)} %add.38), channel_id=1, source_target_pairs={{0,6},{2,0},{4,2},{6,4},{1,7},{3,1},{5,3},{7,5},{8,14},{10,8},{12,... | collective-permute-start | bytes 12296 | tf_op jit(solution)/shard_map/ppermute | solution.py:460
  87.2 1.6 %collective-permute-done.6 = f32[8,128]{1,0:T(8,128)S(1)} collective-permute-done((f32[8,128]{1,0:T(8,128)S(1)}, f32[8,128]{1,0:T(8,128)S(1)}, u32[]{:S(2)}, u32[]{:S(2)}) %collective-permute-start.6) | collective-permute-done | bytes 4128 | tf_op jit(solution)/shard_map/ppermute | solution.py:460
  88.8 2.7 %collective-permute-start.10 = (f32[8,128]{1,0:T(8,128)S(1)}, f32[8,128]{1,0:T(8,128)S(1)}, u32[]{:S(2)}, u32[]{:S(2)}) collective-permute-start(f32[8,128]{1,0:T(8,128)S(1)} %add_add_fusion.2), channel_id=1, source_target_pairs={{0,24},{8,0},{16,8},{24,16},{1,25},{9,1},{17,9},{25,17},{2,26},{10... | collective-permute-start | bytes 12296 | tf_op jit(solution)/shard_map/ppermute | solution.py:460
  94.0 2.6 %collective-permute-done.8 = f32[8,128]{1,0:T(8,128)S(1)} collective-permute-done((f32[8,128]{1,0:T(8,128)S(1)}, f32[8,128]{1,0:T(8,128)S(1)}, u32[]{:S(2)}, u32[]{:S(2)}) %collective-permute-start.8) | collective-permute-done | bytes 4128 | tf_op jit(solution)/shard_map/ppermute | solution.py:460
  97.2 1.5 %collective-permute-start.11 = (f32[8,128]{1,0:T(8,128)S(1)}, f32[8,128]{1,0:T(8,128)S(1)}, u32[]{:S(2)}, u32[]{:S(2)}) collective-permute-start(f32[8,128]{1,0:T(8,128)S(1)} %add_add_fusion.1), channel_id=1, source_target_pairs={{0,64},{32,96},{64,0},{96,32},{1,65},{33,97},{65,1},{97,33},{2,66}... | collective-permute-start | bytes 12296 | tf_op jit(solution)/shard_map/ppermute | solution.py:460
  98.6 2.1 %collective-permute-start.12 = (f32[8,128]{1,0:T(8,128)S(1)}, f32[8,128]{1,0:T(8,128)S(1)}, u32[]{:S(2)}, u32[]{:S(2)}) collective-permute-start(f32[8,128]{1,0:T(8,128)S(1)} %add_add_fusion.1), channel_id=1, source_target_pairs={{0,32},{32,64},{64,96},{96,0},{1,33},{33,65},{65,97},{97,1},{2,34}... | collective-permute-start | bytes 12296 | tf_op jit(solution)/shard_map/ppermute | solution.py:460
  100.7 1.6 %collective-permute-done.11 = f32[8,128]{1,0:T(8,128)S(1)} collective-permute-done((f32[8,128]{1,0:T(8,128)S(1)}, f32[8,128]{1,0:T(8,128)S(1)}, u32[]{:S(2)}, u32[]{:S(2)}) %collective-permute-start.11) | collective-permute-done | bytes 4128 | tf_op jit(solution)/shard_map/ppermute | solution.py:460
  102.3 3.2 %collective-permute-done.13 = f32[8,128]{1,0:T(8,128)S(1)} collective-permute-done((f32[8,128]{1,0:T(8,128)S(1)}, f32[8,128]{1,0:T(8,128)S(1)}, u32[]{:S(2)}, u32[]{:S(2)}) %collective-permute-start.13) | collective-permute-done | bytes 4128 | tf_op jit(solution)/shard_map/ppermute | solution.py:460
  105.5 1.3 %finish.1 = (f32[4,64,1024]{2,1,0:T(8,128)}, f32[1,1]{1,0:T(1,128)}) custom-call(f32[16,2,64,128]{3,2,1,0:T(8,128)S(1)} %all-to-all-done.2.blocks_ref, f32[8,128]{1,0:T(8,128)S(1)} %add_add_fusion.sums_ref), custom_call_target="tpu_custom_call" | custom-call | tf_op jit(solution)/shard_map/finish/pallas_call | solution.py:438
  (56 shorter events, 10.8 us)
Async XLA Ops:
  4.9 7.6 %copy-start.7 = (f32[64,1024]{1,0:T(8,128)S(1)}, f32[64,1024]{1,0:T(8,128)}, u32[]{:S(2)}) copy-start(f32[64,1024]{1,0:T(8,128)} %param.10) | copy-start | bytes 786436
  4.9 7.6 %copy-start.8 = (f32[64,1024]{1,0:T(8,128)S(1)}, f32[64,1024]{1,0:T(8,128)}, u32[]{:S(2)}) copy-start(f32[64,1024]{1,0:T(8,128)} %param.8) | copy-start | bytes 786436
  4.9 29.1 %all-to-all-start = ((f32[16,3,64,128]{3,2,1,0:T(8,128)}), f32[16,3,64,128]{3,2,1,0:T(8,128)S(1)}, u32[]{:S(2)}, u32[]{:S(2)}) async-start(f32[16,3,64,128]{3,2,1,0:T(8,128)} %pack_halo.1), calls=%async_computation | async-start | bytes 3145728 | tf_op jit(solution)/shard_map/all_to_all | solution.py:456
  12.6 7.1 %copy-start.3 = (f32[4,64,1024]{2,1,0:T(8,128)S(1)}, f32[4,64,1024]{2,1,0:T(8,128)}, u32[]{:S(2)}) copy-start(f32[4,64,1024]{2,1,0:T(8,128)} %in_ref.2) | copy-start | bytes 3145732
  14.5 4.4 %collective-permute-start.2 = (f32[2,16,128]{2,1,0:T(8,128)S(1)}, f32[2,16,128]{2,1,0:T(8,128)S(1)}, u32[]{:S(2)}, u32[]{:S(2)}) collective-permute-start(f32[2,16,128]{2,1,0:T(8,128)S(1)} %get-tuple-element.32), channel_id=1, source_target_pairs={{0,1},{1,2},{2,3},{3,4},{4,5},{5,6},{6,7},{7,0},{8,9},{9,10},{10,1... | collective-permute-start | bytes 49160 | tf_op jit(solution)/shard_map/ppermute | solution.py:460
  14.5 4.4 %collective-permute-start.3 = (f32[2,16,128]{2,1,0:T(8,128)S(1)}, f32[2,16,128]{2,1,0:T(8,128)S(1)}, u32[]{:S(2)}, u32[]{:S(2)}) collective-permute-start(f32[2,16,128]{2,1,0:T(8,128)S(1)} %get-tuple-element.33), channel_id=1, source_target_pairs={{0,7},{1,0},{2,1},{3,2},{4,3},{5,4},{6,5},{7,6},{8,15},{9,8},{10,9... | collective-permute-start | bytes 49160 | tf_op jit(solution)/shard_map/ppermute | solution.py:460
  21.0 22.3 %copy-start.4 = (bf16[128,128]{1,0:T(8,128)(2,1)S(1)}, bf16[128,128]{1,0:T(8,128)(2,1)}, u32[]{:S(2)}) copy-start(bf16[128,128]{1,0:T(8,128)(2,1)} %constant.23.clone.refs_2_.fwd_ref) | copy-start | bytes 98308
  21.0 22.3 %copy-start.5 = (f32[3,8,128]{2,1,0:T(8,128)S(1)}, f32[3,8,128]{2,1,0:T(8,128)}, u32[]{:S(2)}) copy-start(f32[3,8,128]{2,1,0:T(8,128)} %constant.24.clone.refs_3_.coef_ref) | copy-start | bytes 36868
  33.9 25.9 %all-to-all-start.1 = ((f32[16,2,64,128]{3,2,1,0:T(8,128)}), f32[16,2,64,128]{3,2,1,0:T(8,128)S(1)}, u32[]{:S(2)}, u32[]{:S(2)}) async-start(f32[16,2,64,128]{3,2,1,0:T(8,128)} %pack.1), calls=%async_computation.1 | async-start | bytes 2097152 | tf_op jit(solution)/shard_map/all_to_all | solution.py:456
  40.2 8.4 %collective-permute-start = (f32[16,3,16,128]{3,2,1,0:T(8,128)S(1)}, f32[16,3,16,128]{3,2,1,0:T(8,128)S(1)}, u32[]{:S(2)}, u32[]{:S(2)}) collective-permute-start(f32[16,3,16,128]{3,2,1,0:T(8,128)S(1)} %get-tuple-element.31), channel_id=1, source_target_pairs={{0,1},{1,2},{2,3},{3,4},{4,5},{5,6},{6,7},{7,0},{8,9},{9,10},{10,1... | collective-permute-start | bytes 1179656 | tf_op jit(solution)/shard_map/ppermute | solution.py:460
  40.2 8.4 %collective-permute-start.1 = (f32[16,3,16,128]{3,2,1,0:T(8,128)S(1)}, f32[16,3,16,128]{3,2,1,0:T(8,128)S(1)}, u32[]{:S(2)}, u32[]{:S(2)}) collective-permute-start(f32[16,3,16,128]{3,2,1,0:T(8,128)S(1)} %get-tuple-element.30), channel_id=1, source_target_pairs={{0,7},{1,0},{2,1},{3,2},{4,3},{5,4},{6,5},{7,6},{8,15},{9,8},{10,9... | collective-permute-start | bytes 1179656 | tf_op jit(solution)/shard_map/ppermute | solution.py:460
  48.6 11.3 %copy-start.6 = (bf16[128,128]{1,0:T(8,128)(2,1)S(1)}, bf16[128,128]{1,0:T(8,128)(2,1)}, u32[]{:S(2)}) copy-start(bf16[128,128]{1,0:T(8,128)(2,1)} %constant.25.clone.inv_ref) | copy-start | bytes 98308
  59.8 1.4 %copy-start.1 = (f32[68,48,128]{2,1,0:T(8,128)S(1)}, f32[68,48,128]{2,1,0:T(8,128)}, u32[]{:S(2)}) copy-start(f32[68,48,128]{2,1,0:T(8,128)} %copy-done) | copy-start | bytes 5013508
  71.1 2.0 %collective-permute-start.4 = (f32[8,128]{1,0:T(8,128)S(1)}, f32[8,128]{1,0:T(8,128)S(1)}, u32[]{:S(2)}, u32[]{:S(2)}) collective-permute-start(f32[8,128]{1,0:T(8,128)S(1)} %get-tuple-element.25), channel_id=1, source_target_pairs={{0,1},{1,0},{2,3},{3,2},{4,5},{5,4},{6,7},{7,6},{8,9},{9,8},{10,11... | collective-permute-start | bytes 12296 | tf_op jit(solution)/shard_map/ppermute | solution.py:460
  73.1 32.4 %all-to-all-start.2 = ((f32[16,2,64,128]{3,2,1,0:T(8,128)}), f32[16,2,64,128]{3,2,1,0:T(8,128)S(1)}, u32[]{:S(2)}, u32[]{:S(2)}) async-start(f32[16,2,64,128]{3,2,1,0:T(8,128)} %bitcast.32), calls=%async_computation.2 | async-start | bytes 2097152 | tf_op jit(solution)/shard_map/all_to_all | solution.py:456
  80.4 6.8 %collective-permute-start.5 = (f32[8,128]{1,0:T(8,128)S(1)}, f32[8,128]{1,0:T(8,128)S(1)}, u32[]{:S(2)}, u32[]{:S(2)}) collective-permute-start(f32[8,128]{1,0:T(8,128)S(1)} %add.38), channel_id=1, source_target_pairs={{0,4},{2,6},{4,0},{6,2},{1,5},{3,7},{5,1},{7,3},{8,12},{10,14},{12... | collective-permute-start | bytes 12296 | tf_op jit(solution)/shard_map/ppermute | solution.py:460
  83.9 4.8 %collective-permute-start.6 = (f32[8,128]{1,0:T(8,128)S(1)}, f32[8,128]{1,0:T(8,128)S(1)}, u32[]{:S(2)}, u32[]{:S(2)}) collective-permute-start(f32[8,128]{1,0:T(8,128)S(1)} %add.38), channel_id=1, source_target_pairs={{0,2},{2,4},{4,6},{6,0},{1,3},{3,5},{5,7},{7,1},{8,10},{10,12},{12... | collective-permute-start | bytes 12296 | tf_op jit(solution)/shard_map/ppermute | solution.py:460
  83.9 4.8 %collective-permute-start.7 = (f32[8,128]{1,0:T(8,128)S(1)}, f32[8,128]{1,0:T(8,128)S(1)}, u32[]{:S(2)}, u32[]{:S(2)}) collective-permute-start(f32[8,128]{1,0:T(8,128)S(1)} %add.38), channel_id=1, source_target_pairs={{0,6},{2,0},{4,2},{6,4},{1,7},{3,1},{5,3},{7,5},{8,14},{10,8},{12,... | collective-permute-start | bytes 12296 | tf_op jit(solution)/shard_map/ppermute | solution.py:460
  88.8 5.3 %collective-permute-start.10 = (f32[8,128]{1,0:T(8,128)S(1)}, f32[8,128]{1,0:T(8,128)S(1)}, u32[]{:S(2)}, u32[]{:S(2)}) collective-permute-start(f32[8,128]{1,0:T(8,128)S(1)} %add_add_fusion.2), channel_id=1, source_target_pairs={{0,24},{8,0},{16,8},{24,16},{1,25},{9,1},{17,9},{25,17},{2,26},{10... | collective-permute-start | bytes 12296 | tf_op jit(solution)/shard_map/ppermute | solution.py:460
  91.5 5.1 %collective-permute-start.8 = (f32[8,128]{1,0:T(8,128)S(1)}, f32[8,128]{1,0:T(8,128)S(1)}, u32[]{:S(2)}, u32[]{:S(2)}) collective-permute-start(f32[8,128]{1,0:T(8,128)S(1)} %add_add_fusion.2), channel_id=1, source_target_pairs={{0,16},{8,24},{16,0},{24,8},{1,17},{9,25},{17,1},{25,9},{2,18},{10... | collective-permute-start | bytes 12296 | tf_op jit(solution)/shard_map/ppermute | solution.py:460
  92.4 4.8 %collective-permute-start.9 = (f32[8,128]{1,0:T(8,128)S(1)}, f32[8,128]{1,0:T(8,128)S(1)}, u32[]{:S(2)}, u32[]{:S(2)}) collective-permute-start(f32[8,128]{1,0:T(8,128)S(1)} %add_add_fusion.2), channel_id=1, source_target_pairs={{0,8},{8,16},{16,24},{24,0},{1,9},{9,17},{17,25},{25,1},{2,10},{10... | collective-permute-start | bytes 12296 | tf_op jit(solution)/shard_map/ppermute | solution.py:460
  97.2 5.1 %collective-permute-start.11 = (f32[8,128]{1,0:T(8,128)S(1)}, f32[8,128]{1,0:T(8,128)S(1)}, u32[]{:S(2)}, u32[]{:S(2)}) collective-permute-start(f32[8,128]{1,0:T(8,128)S(1)} %add_add_fusion.1), channel_id=1, source_target_pairs={{0,64},{32,96},{64,0},{96,32},{1,65},{33,97},{65,1},{97,33},{2,66}... | collective-permute-start | bytes 12296 | tf_op jit(solution)/shard_map/ppermute | solution.py:460
  98.6 3.7 %collective-permute-start.12 = (f32[8,128]{1,0:T(8,128)S(1)}, f32[8,128]{1,0:T(8,128)S(1)}, u32[]{:S(2)}, u32[]{:S(2)}) collective-permute-start(f32[8,128]{1,0:T(8,128)S(1)} %add_add_fusion.1), channel_id=1, source_target_pairs={{0,32},{32,64},{64,96},{96,0},{1,33},{33,65},{65,97},{97,1},{2,34}... | collective-permute-start | bytes 12296 | tf_op jit(solution)/shard_map/ppermute | solution.py:460
  100.7 4.8 %collective-permute-start.13 = (f32[8,128]{1,0:T(8,128)S(1)}, f32[8,128]{1,0:T(8,128)S(1)}, u32[]{:S(2)}, u32[]{:S(2)}) collective-permute-start(f32[8,128]{1,0:T(8,128)S(1)} %add_add_fusion.1), channel_id=1, source_target_pairs={{0,96},{32,0},{64,32},{96,64},{1,97},{33,1},{65,33},{97,65},{2,98}... | collective-permute-start | bytes 12296 | tf_op jit(solution)/shard_map/ppermute | solution.py:460
  (2 other events, 2.4 us)

commit v6 on v5

--- a/solution.py
+++ b/solution.py
@@ -23,11 +23,12 @@
 PAD = WIDE + 8
 FIRST = HALO - 1
 KEPT = ROWS + 2
-SOLVED_ROWS = 68
+SOLVED_ROWS = 72
 PACKED_ROWS = 80
+ARRIVING = 3
 GROUPS = 4
 BLOCKS = 1
-LAST_BLOCK = 66
+LAST_BLOCK = 22
 BATCH = 4
 PACK_ROWS = 32
 JBATCH = 4
@@ -70,7 +71,7 @@
     return np.concatenate([np.concatenate([m, m], axis=1) for m in (high, low)], axis=0)
 
 
-def transform(matrix_ref, count, take, give, stage_ref, result_ref):
+def transform(matrix_ref, count, take, give, stage_ref, result_ref, ready=lambda i: None):
     def stage(i):
         for e, values in enumerate(take(i)):
             high = values.astype(BF16)
@@ -78,12 +79,14 @@
             stage_ref[NT:, 128 * e : 128 * e + 128] = (values - high.astype(F32)).astype(BF16)
 
     def step(i, _):
+        ready(i + 1)
         give(jnp.maximum(i - 1, 0), result_ref)
         both = jnp.dot(matrix_ref[...], stage_ref[...], preferred_element_type=F32)
         result_ref[...] = both[:NT] + both[NT:]
         stage(jnp.minimum(i + 1, count - 1))
         return 0
 
+    ready(0)
     stage(0)
     lax.fori_loop(0, count + 1, step, 0)
 
@@ -236,7 +239,7 @@
 
 def sweep_kernel(
     low_ref, high_ref, mob_ref, ini_ref, fwd_ref, coef_ref, s_in, pa_in, pb_in, q_in,
-    solved_ref, s_ref, pa_ref, pb_ref, q_ref, u_ref, w_ref, *scratch,
+    solved_out, s_ref, pa_ref, pb_ref, q_ref, u_ref, w_ref, solved_ref, sems, *scratch,
 ):
     del s_in, pa_in, pb_in, q_in
     sources = [(low_ref, HALO, 0), (high_ref, HALO, HALO + ROWS)]
@@ -277,9 +280,15 @@
                             value = kept + join * value
                         target[row - shift, m, :] = value
                 above, here = here, below
+            if shift:
+                solved_copy(i).start()
             return above, here
 
         lax.fori_loop(0, -(-count // block), body, (load(k - 1), load(k)))
+
+    def solved_copy(i):
+        rows = pl.ds(i * LAST_BLOCK, LAST_BLOCK)
+        return pltpu.make_async_copy(solved_ref.at[rows], solved_out.at[rows], sems.at[i])
 
     apply(1, s_ref, u_ref, 0.2, s_ref)
     k = 1
@@ -295,10 +304,11 @@
             apply(k, source, u_ref, 0.2**power, u_ref)
         else:
             apply(k, source, solved_ref, 0.2**power, u_ref, FIRST)
+            for i in range(KEPT // LAST_BLOCK):
+                solved_copy(i).wait()
 
 
 WIDE_BUFFER = pltpu.VMEM((PAD, 48, 128), F32)
-SOLVED = pltpu.VMEM((SOLVED_ROWS, 48, 128), F32)
 HALF_BUFFER = pltpu.VMEM((PAD, 24, 128), F32)
 
 
@@ -315,15 +325,37 @@
 def sweep(low, high, mob, ini, forward, coefs, buffers):
     return pl.pallas_call(
         sweep_kernel,
-        out_shape=(SOLVED, WIDE_BUFFER, HALF_BUFFER, HALF_BUFFER, HALF_BUFFER),
-        scratch_shapes=[WIDE_BUFFER, WIDE_BUFFER, *TRANSFORM_SCRATCH],
+        in_specs=[pl.BlockSpec(memory_space=pltpu.VMEM)] * 10,
+        out_specs=[pl.BlockSpec(memory_space=pltpu.HBM)] + [pl.BlockSpec(memory_space=pltpu.VMEM)] * 4,
+        out_shape=(pltpu.HBM((SOLVED_ROWS, 48, 128), F32), WIDE_BUFFER, HALF_BUFFER, HALF_BUFFER, HALF_BUFFER),
+        scratch_shapes=[
+            WIDE_BUFFER,
+            WIDE_BUFFER,
+            pltpu.VMEM((KEPT, 48, 128), F32),
+            pltpu.SemaphoreType.DMA((KEPT // LAST_BLOCK,)),
+            *TRANSFORM_SCRATCH,
+        ],
         input_output_aliases={6: 1, 7: 2, 8: 3, 9: 4},
         compiler_params=pltpu.CompilerParams(vmem_limit_bytes=24 * MIB),
         name="sweep",
     )(*vmem(low, high, mob, ini), forward, coefs, *vmem(*buffers))[0]
 
 
-def back_kernel(u_ref, traj_ref, x_ref, mob_ref, inv_ref, out_ref, sums_ref, dir_ref, packed_ref, sem, *scratch):
+def back_kernel(
+    solved_ref, traj_ref, x_ref, mob_ref, inv_ref, out_ref, sums_ref, dir_ref, packed_ref, sem, u_ref, sems, *scratch
+):
+    def arriving(i):
+        rows = pl.ds(i * ARRIVING * BATCH, ARRIVING * BATCH)
+        return pltpu.make_async_copy(solved_ref.at[rows], u_ref.at[rows], sems.at[i])
+
+    for i in range(SOLVED_ROWS // (ARRIVING * BATCH)):
+        arriving(i).start()
+
+    def ready(i):
+        @pl.when((i % ARRIVING == 0) & (i * BATCH < SOLVED_ROWS))
+        def _():
+            arriving(i // ARRIVING).wait()
+
     slot = lanes() // 32
     slot16 = lanes(NTM) // 32
     natural = natural_index(NT)
@@ -350,28 +382,30 @@
                 both = jnp.where(low_half, v[32 * j : 32 * j + 16], roll(v[32 * j + 16 : 32 * j + 32], 64))
                 flat_ref[pl.ds(row + 7 + PACKED_ROWS * j, NTM, stride=2 * PACKED_ROWS), :] = both
 
-    transform(inv_ref, -(-KEPT // BATCH), take, give, *scratch)
+    transform(inv_ref, SOLVED_ROWS // BATCH, take, give, *scratch, ready=ready)
     copy = pltpu.make_async_copy(packed_ref.at[:, pl.ds(8, ROWS), :], out_ref, sem)
     copy.start()
     jacobian_sums(dir_ref, traj_ref, x_ref, mob_ref, sums_ref, natural, slot16)
     copy.wait()
 
 
-def back(u, traj, x, mob, inverse):
+def back(solved, traj, x, mob, inverse):
     return pl.pallas_call(
         back_kernel,
-        in_specs=[pl.BlockSpec(memory_space=pltpu.VMEM)] * 5,
+        in_specs=[pl.BlockSpec(memory_space=pltpu.HBM)] + [pl.BlockSpec(memory_space=pltpu.VMEM)] * 4,
         out_specs=(pl.BlockSpec(memory_space=pltpu.HBM), pl.BlockSpec(memory_space=pltpu.VMEM)),
         out_shape=(pltpu.HBM((NTM * 2, ROWS, 128), F32), pltpu.VMEM((8, 128), F32)),
         scratch_shapes=[
             pltpu.VMEM((SOLVED_ROWS, NT, 128), F32),
             pltpu.VMEM((NTM * 2, PACKED_ROWS, 128), F32),
             pltpu.SemaphoreType.DMA,
+            pltpu.VMEM((SOLVED_ROWS, 48, 128), F32),
+            pltpu.SemaphoreType.DMA((SOLVED_ROWS // (ARRIVING * BATCH),)),
             *TRANSFORM_SCRATCH,
         ],
         compiler_params=pltpu.CompilerParams(vmem_limit_bytes=16 * MIB),
         name="back",
-    )(*vmem(u, traj, x, mob), inverse)
+    )(pltpu.with_memory_space_constraint(solved, pltpu.HBM), *vmem(traj, x, mob), inverse)
 
 
 def jacobian_sums(dir_ref, traj_ref, x_ref, mob_ref, out_ref, natural, slot):

time: 107 us -> 107 us (level)
  local copies, waits for them, and re-layouts: 7.34 us -> 5.66 us
  Pallas kernels: 29 us -> 30.6 us
    pallas_call x2, Pallas kernels: 19.8 us -> 22.2 us  [the longest x1 11.2 us: back(): pl.pallas_call(back_kernel, in_specs=[pl.BlockSpec(memory_space=pltpu.HBM...]
    unnamed x18 -> x16, local copies, waits for them, and re-layouts: 3.89 us -> 2.21 us
where the time goes in v6:
time: 107 us
  starting transfers between devices  42.8 us (40%)
  Pallas kernels  30.6 us (29%)
  waiting for transfers between devices  26 us (24%)
  local copies, waits for them, and re-layouts  5.66 us (5%)
    ppermute x14, starting transfers between devices, shifted(): lax.ppermute(array, axes, [(i, (i + distance) % size) for i in range(size)])  21.9 us
    all_to_all x3, starting transfers between devices, swap(): return lax.all_to_all(blocks, TM, split_axis=0, concat_axis=0, tiled=True)  20.9 us
    ppermute x14, waiting for transfers between devices, shifted(): lax.ppermute(array, axes, [(i, (i + distance) % size) for i in range(size)])  13.4 us
    all_to_all x3, waiting for transfers between devices, swap(): return lax.all_to_all(blocks, TM, split_axis=0, concat_axis=0, tiled=True)  12.7 us
    pallas_call x1, Pallas kernels, back(): pl.pallas_call(back_kernel, in_specs=[pl.BlockSpec(memory_space=pltpu.HBM...  11.2 us
    pallas_call x1, Pallas kernels, sweep(): pl.pallas_call(sweep_kernel, in_specs=[pl.BlockSpec(memory_space=pltpu.VM...  11 us
    pallas_call x2, Pallas kernels, pack(): pl.pallas_call(kernel, grid=(ROWS // PACK_ROWS,), in_specs=[pl.BlockSpec(...  3.59 us
    pallas_call x1, Pallas kernels, transform_rows(): pl.pallas_call(transform_kernel, out_shape=(WIDE_BUFFER, HALF_BUFFER, HAL...  3.53 us
  transfers between devices with their start and end apart: 17, of which 10 were waited for; matrix products, arithmetic and copies ran while one was open for 4% of the time, Pallas kernels for 14%

profile of v6, /device:TPU:6, one launch (start us, length us, event | category | flops | bytes accessed | tf_op | source)
XLA Modules:
  0.0 106.6 jit_solution(1471216839645663401)
XLA Ops:
  0.6 1.2 %copy-done.1 = f32[4,64,1024]{2,1,0:T(8,128)S(1)} copy-done((f32[4,64,1024]{2,1,0:T(8,128)S(1)}, f32[4,64,1024]{2,1,0:T(8,128)}, u32[]{:S(2)}) %copy-start.1) | copy-done | bytes 1048600
  1.9 3.0 %pack_halo.1 = f32[16,3,64,128]{3,2,1,0:T(8,128)} custom-call(f32[4,64,1024]{2,1,0:T(8,128)S(1)} %copy-done.1), custom_call_target="tpu_custom_call" | custom-call | tf_op jit(solution)/shard_map/pack_halo/pallas_call | solution.py:148
  4.9 7.6 %all-to-all-start = ((f32[16,3,64,128]{3,2,1,0:T(8,128)}), f32[16,3,64,128]{3,2,1,0:T(8,128)S(1)}, u32[]{:S(2)}, u32[]{:S(2)}) async-start(f32[16,3,64,128]{3,2,1,0:T(8,128)} %pack_halo.1), calls=%async_computation | async-start | bytes 3145728 | tf_op jit(solution)/shard_map/all_to_all | solution.py:490
  12.6 1.0 concatenate.16
  14.5 3.0 %collective-permute-start.3 = (f32[2,16,128]{2,1,0:T(8,128)S(1)}, f32[2,16,128]{2,1,0:T(8,128)S(1)}, u32[]{:S(2)}, u32[]{:S(2)}) collective-permute-start(f32[2,16,128]{2,1,0:T(8,128)S(1)} %get-tuple-element.33), channel_id=1, source_target_pairs={{0,7},{1,0},{2,1},{3,2},{4,3},{5,4},{6,5},{7,6},{8,15},{9,8},{10,9... | collective-permute-start | bytes 49160 | tf_op jit(solution)/shard_map/ppermute | solution.py:494
  21.3 12.7 %all-to-all-done = f32[16,3,64,128]{3,2,1,0:T(8,128)S(1)} async-done(((f32[16,3,64,128]{3,2,1,0:T(8,128)}), f32[16,3,64,128]{3,2,1,0:T(8,128)S(1)}, u32[]{:S(2)}, u32[]{:S(2)}) %all-to-all-start) | async-done | bytes 1572896 | tf_op jit(solution)/shard_map/all_to_all | solution.py:490
  34.0 6.1 %all-to-all-start.1 = ((f32[16,2,64,128]{3,2,1,0:T(8,128)}), f32[16,2,64,128]{3,2,1,0:T(8,128)S(1)}, u32[]{:S(2)}, u32[]{:S(2)}) async-start(f32[16,2,64,128]{3,2,1,0:T(8,128)} %copy-done), calls=%async_computation.1 | async-start | bytes 2097152 | tf_op jit(solution)/shard_map/all_to_all | solution.py:490
  40.2 2.9 %collective-permute-start.1 = (f32[16,3,16,128]{3,2,1,0:T(8,128)S(1)}, f32[16,3,16,128]{3,2,1,0:T(8,128)S(1)}, u32[]{:S(2)}, u32[]{:S(2)}) collective-permute-start(f32[16,3,16,128]{3,2,1,0:T(8,128)S(1)} %get-tuple-element.30), channel_id=1, source_target_pairs={{0,7},{1,0},{2,1},{3,2},{4,3},{5,4},{6,5},{7,6},{8,15},{9,8},{10,9... | collective-permute-start | bytes 1179656 | tf_op jit(solution)/shard_map/ppermute | solution.py:494
  43.3 3.5 %transform_rows.1 = (f32[104,48,128]{2,1,0:T(8,128)S(1)}, f32[104,24,128]{2,1,0:T(8,128)S(1)}, f32[104,24,128]{2,1,0:T(8,128)S(1)}, f32[104,24,128]{2,1,0:T(8,128)S(1)}) custom-call(f32[3072,128]{1,0:T(8,128)S(1)} %bitcast.21, f32[3,96,128]{2,1,0:T(8,128)S(1)} %get-tuple-element.16.refs_0_.mob_ref, f32[3,96,128]{2,1,0:T(8,128)S(1)} %get-tuple-element.17.refs_1_.ini_ref, ...), custom_call_target="tpu_custom_call" | custom-call | tf_op jit(solution)/shard_map/transform_rows/pallas_call | solution.py:316
  46.9 1.7 %collective-permute-done = f32[16,3,16,128]{3,2,1,0:T(8,128)S(1)} collective-permute-done((f32[16,3,16,128]{3,2,1,0:T(8,128)S(1)}, f32[16,3,16,128]{3,2,1,0:T(8,128)S(1)}, u32[]{:S(2)}, u32[]{:S(2)}) %collective-permute-start) | collective-permute-done | bytes 393248 | tf_op jit(solution)/shard_map/ppermute | solution.py:494
  48.6 11.0 %sweep.1 = (f32[72,48,128]{2,1,0:T(8,128)}, f32[104,48,128]{2,1,0:T(8,128)S(1)}, f32[104,24,128]{2,1,0:T(8,128)S(1)}, f32[104,24,128]{2,1,0:T(8,128)S(1)}, f32[104,24,128]{2,1,0:T(8,128)S(1)}) custom-call(f32[768,128]{1,0:T(8,128)S(1)} %bitcast.24, f32[768,128]{1,0:T(8,128)S(1)} %bitcast.25, ...), custom_call_target="tpu_custom_call", output_to_operand_aliasing={{1}: (6, {}), {2}: (7, {}), {3}: (8, {}), {4}: (9, {})} | custom-call | tf_op jit(solution)/shard_map/sweep/pallas_call | solution.py:326
  59.7 11.2 %back.1 = (f32[32,64,128]{2,1,0:T(8,128)}, f32[8,128]{1,0:T(8,128)S(1)}) custom-call(f32[72,48,128]{2,1,0:T(8,128)} %get-tuple-element.22.solved_ref, f32[2048,128]{1,0:T(8,128)S(1)} %bitcast.23, f32[3072,128]{1,0:T(8,128)S(1)} %bitcast.22, f32[96,128]{1,0:T(8,128)S(1)} %pad_maximum_fusion.4.mob_ref, bf16[128,128]{1,0:T(8,128)(2,1)S(1)} %copy-done.5), custom_call_target="tpu_custom_call" | custom-call | tf_op jit(solution)/shard_map/back/pallas_call | solution.py:393
  70.9 1.2 %collective-permute-start.4 = (f32[8,128]{1,0:T(8,128)S(1)}, f32[8,128]{1,0:T(8,128)S(1)}, u32[]{:S(2)}, u32[]{:S(2)}) collective-permute-start(f32[8,128]{1,0:T(8,128)S(1)} %get-tuple-element.25), channel_id=1, source_target_pairs={{0,1},{1,0},{2,3},{3,2},{4,5},{5,4},{6,7},{7,6},{8,9},{9,8},{10,11... | collective-permute-start | bytes 12296 | tf_op jit(solution)/shard_map/ppermute | solution.py:494
  72.9 7.2 %all-to-all-start.2 = ((f32[16,2,64,128]{3,2,1,0:T(8,128)}), f32[16,2,64,128]{3,2,1,0:T(8,128)S(1)}, u32[]{:S(2)}, u32[]{:S(2)}) async-start(f32[16,2,64,128]{3,2,1,0:T(8,128)} %bitcast.32), calls=%async_computation.2 | async-start | bytes 2097152 | tf_op jit(solution)/shard_map/all_to_all | solution.py:490
  80.1 3.6 %collective-permute-start.5 = (f32[8,128]{1,0:T(8,128)S(1)}, f32[8,128]{1,0:T(8,128)S(1)}, u32[]{:S(2)}, u32[]{:S(2)}) collective-permute-start(f32[8,128]{1,0:T(8,128)S(1)} %add.38), channel_id=1, source_target_pairs={{0,4},{2,6},{4,0},{6,2},{1,5},{3,7},{5,1},{7,3},{8,12},{10,14},{12... | collective-permute-start | bytes 12296 | tf_op jit(solution)/shard_map/ppermute | solution.py:494
  83.7 3.2 %collective-permute-start.7 = (f32[8,128]{1,0:T(8,128)S(1)}, f32[8,128]{1,0:T(8,128)S(1)}, u32[]{:S(2)}, u32[]{:S(2)}) collective-permute-start(f32[8,128]{1,0:T(8,128)S(1)} %add.38), channel_id=1, source_target_pairs={{0,6},{2,0},{4,2},{6,4},{1,7},{3,1},{5,3},{7,5},{8,14},{10,8},{12,... | collective-permute-start | bytes 12296 | tf_op jit(solution)/shard_map/ppermute | solution.py:494
  86.9 1.6 %collective-permute-done.6 = f32[8,128]{1,0:T(8,128)S(1)} collective-permute-done((f32[8,128]{1,0:T(8,128)S(1)}, f32[8,128]{1,0:T(8,128)S(1)}, u32[]{:S(2)}, u32[]{:S(2)}) %collective-permute-start.6) | collective-permute-done | bytes 4128 | tf_op jit(solution)/shard_map/ppermute | solution.py:494
  88.5 2.7 %collective-permute-start.10 = (f32[8,128]{1,0:T(8,128)S(1)}, f32[8,128]{1,0:T(8,128)S(1)}, u32[]{:S(2)}, u32[]{:S(2)}) collective-permute-start(f32[8,128]{1,0:T(8,128)S(1)} %add_add_fusion.2), channel_id=1, source_target_pairs={{0,24},{8,0},{16,8},{24,16},{1,25},{9,1},{17,9},{25,17},{2,26},{10... | collective-permute-start | bytes 12296 | tf_op jit(solution)/shard_map/ppermute | solution.py:494
  93.8 2.6 %collective-permute-done.8 = f32[8,128]{1,0:T(8,128)S(1)} collective-permute-done((f32[8,128]{1,0:T(8,128)S(1)}, f32[8,128]{1,0:T(8,128)S(1)}, u32[]{:S(2)}, u32[]{:S(2)}) %collective-permute-start.8) | collective-permute-done | bytes 4128 | tf_op jit(solution)/shard_map/ppermute | solution.py:494
  96.9 1.5 %collective-permute-start.11 = (f32[8,128]{1,0:T(8,128)S(1)}, f32[8,128]{1,0:T(8,128)S(1)}, u32[]{:S(2)}, u32[]{:S(2)}) collective-permute-start(f32[8,128]{1,0:T(8,128)S(1)} %add_add_fusion.1), channel_id=1, source_target_pairs={{0,64},{32,96},{64,0},{96,32},{1,65},{33,97},{65,1},{97,33},{2,66}... | collective-permute-start | bytes 12296 | tf_op jit(solution)/shard_map/ppermute | solution.py:494
  98.4 2.1 %collective-permute-start.12 = (f32[8,128]{1,0:T(8,128)S(1)}, f32[8,128]{1,0:T(8,128)S(1)}, u32[]{:S(2)}, u32[]{:S(2)}) collective-permute-start(f32[8,128]{1,0:T(8,128)S(1)} %add_add_fusion.1), channel_id=1, source_target_pairs={{0,32},{32,64},{64,96},{96,0},{1,33},{33,65},{65,97},{97,1},{2,34}... | collective-permute-start | bytes 12296 | tf_op jit(solution)/shard_map/ppermute | solution.py:494
  100.5 1.6 %collective-permute-done.11 = f32[8,128]{1,0:T(8,128)S(1)} collective-permute-done((f32[8,128]{1,0:T(8,128)S(1)}, f32[8,128]{1,0:T(8,128)S(1)}, u32[]{:S(2)}, u32[]{:S(2)}) %collective-permute-start.11) | collective-permute-done | bytes 4128 | tf_op jit(solution)/shard_map/ppermute | solution.py:494
  102.1 3.2 %collective-permute-done.13 = f32[8,128]{1,0:T(8,128)S(1)} collective-permute-done((f32[8,128]{1,0:T(8,128)S(1)}, f32[8,128]{1,0:T(8,128)S(1)}, u32[]{:S(2)}, u32[]{:S(2)}) %collective-permute-start.13) | collective-permute-done | bytes 4128 | tf_op jit(solution)/shard_map/ppermute | solution.py:494
  105.3 1.3 %finish.1 = (f32[4,64,1024]{2,1,0:T(8,128)}, f32[1,1]{1,0:T(1,128)}) custom-call(f32[16,2,64,128]{3,2,1,0:T(8,128)S(1)} %all-to-all-done.2.blocks_ref, f32[8,128]{1,0:T(8,128)S(1)} %add_add_fusion.sums_ref), custom_call_target="tpu_custom_call" | custom-call | tf_op jit(solution)/shard_map/finish/pallas_call | solution.py:472
  (54 shorter events, 8.9 us)
Async XLA Ops:
  0.6 1.2 %copy-start.1 = (f32[4,64,1024]{2,1,0:T(8,128)S(1)}, f32[4,64,1024]{2,1,0:T(8,128)}, u32[]{:S(2)}) copy-start(f32[4,64,1024]{2,1,0:T(8,128)} %in_ref.1) | copy-start | bytes 3145732
  4.9 7.6 %copy-start.6 = (f32[64,1024]{1,0:T(8,128)S(1)}, f32[64,1024]{1,0:T(8,128)}, u32[]{:S(2)}) copy-start(f32[64,1024]{1,0:T(8,128)} %param.10) | copy-start | bytes 786436
  4.9 7.6 %copy-start.7 = (f32[64,1024]{1,0:T(8,128)S(1)}, f32[64,1024]{1,0:T(8,128)}, u32[]{:S(2)}) copy-start(f32[64,1024]{1,0:T(8,128)} %param.8) | copy-start | bytes 786436
  4.9 29.1 %all-to-all-start = ((f32[16,3,64,128]{3,2,1,0:T(8,128)}), f32[16,3,64,128]{3,2,1,0:T(8,128)S(1)}, u32[]{:S(2)}, u32[]{:S(2)}) async-start(f32[16,3,64,128]{3,2,1,0:T(8,128)} %pack_halo.1), calls=%async_computation | async-start | bytes 3145728 | tf_op jit(solution)/shard_map/all_to_all | solution.py:490
  12.6 7.1 %copy-start.2 = (f32[4,64,1024]{2,1,0:T(8,128)S(1)}, f32[4,64,1024]{2,1,0:T(8,128)}, u32[]{:S(2)}) copy-start(f32[4,64,1024]{2,1,0:T(8,128)} %in_ref.2) | copy-start | bytes 3145732
  14.5 4.4 %collective-permute-start.2 = (f32[2,16,128]{2,1,0:T(8,128)S(1)}, f32[2,16,128]{2,1,0:T(8,128)S(1)}, u32[]{:S(2)}, u32[]{:S(2)}) collective-permute-start(f32[2,16,128]{2,1,0:T(8,128)S(1)} %get-tuple-element.32), channel_id=1, source_target_pairs={{0,1},{1,2},{2,3},{3,4},{4,5},{5,6},{6,7},{7,0},{8,9},{9,10},{10,1... | collective-permute-start | bytes 49160 | tf_op jit(solution)/shard_map/ppermute | solution.py:494
  14.5 4.4 %collective-permute-start.3 = (f32[2,16,128]{2,1,0:T(8,128)S(1)}, f32[2,16,128]{2,1,0:T(8,128)S(1)}, u32[]{:S(2)}, u32[]{:S(2)}) collective-permute-start(f32[2,16,128]{2,1,0:T(8,128)S(1)} %get-tuple-element.33), channel_id=1, source_target_pairs={{0,7},{1,0},{2,1},{3,2},{4,3},{5,4},{6,5},{7,6},{8,15},{9,8},{10,9... | collective-permute-start | bytes 49160 | tf_op jit(solution)/shard_map/ppermute | solution.py:494
  21.3 22.0 %copy-start.3 = (bf16[128,128]{1,0:T(8,128)(2,1)S(1)}, bf16[128,128]{1,0:T(8,128)(2,1)}, u32[]{:S(2)}) copy-start(bf16[128,128]{1,0:T(8,128)(2,1)} %constant.23.clone.refs_2_.fwd_ref) | copy-start | bytes 98308
  21.3 22.0 %copy-start.4 = (f32[3,8,128]{2,1,0:T(8,128)S(1)}, f32[3,8,128]{2,1,0:T(8,128)}, u32[]{:S(2)}) copy-start(f32[3,8,128]{2,1,0:T(8,128)} %constant.24.clone.refs_3_.coef_ref) | copy-start | bytes 36868
  34.0 25.7 %all-to-all-start.1 = ((f32[16,2,64,128]{3,2,1,0:T(8,128)}), f32[16,2,64,128]{3,2,1,0:T(8,128)S(1)}, u32[]{:S(2)}, u32[]{:S(2)}) async-start(f32[16,2,64,128]{3,2,1,0:T(8,128)} %copy-done), calls=%async_computation.1 | async-start | bytes 2097152 | tf_op jit(solution)/shard_map/all_to_all | solution.py:490
  40.2 8.4 %collective-permute-start = (f32[16,3,16,128]{3,2,1,0:T(8,128)S(1)}, f32[16,3,16,128]{3,2,1,0:T(8,128)S(1)}, u32[]{:S(2)}, u32[]{:S(2)}) collective-permute-start(f32[16,3,16,128]{3,2,1,0:T(8,128)S(1)} %get-tuple-element.31), channel_id=1, source_target_pairs={{0,1},{1,2},{2,3},{3,4},{4,5},{5,6},{6,7},{7,0},{8,9},{9,10},{10,1... | collective-permute-start | bytes 1179656 | tf_op jit(solution)/shard_map/ppermute | solution.py:494
  40.2 8.4 %collective-permute-start.1 = (f32[16,3,16,128]{3,2,1,0:T(8,128)S(1)}, f32[16,3,16,128]{3,2,1,0:T(8,128)S(1)}, u32[]{:S(2)}, u32[]{:S(2)}) collective-permute-start(f32[16,3,16,128]{3,2,1,0:T(8,128)S(1)} %get-tuple-element.30), channel_id=1, source_target_pairs={{0,7},{1,0},{2,1},{3,2},{4,3},{5,4},{6,5},{7,6},{8,15},{9,8},{10,9... | collective-permute-start | bytes 1179656 | tf_op jit(solution)/shard_map/ppermute | solution.py:494
  48.6 11.0 %copy-start.5 = (bf16[128,128]{1,0:T(8,128)(2,1)S(1)}, bf16[128,128]{1,0:T(8,128)(2,1)}, u32[]{:S(2)}) copy-start(bf16[128,128]{1,0:T(8,128)(2,1)} %constant.25.clone.inv_ref) | copy-start | bytes 98308
  70.9 2.0 %collective-permute-start.4 = (f32[8,128]{1,0:T(8,128)S(1)}, f32[8,128]{1,0:T(8,128)S(1)}, u32[]{:S(2)}, u32[]{:S(2)}) collective-permute-start(f32[8,128]{1,0:T(8,128)S(1)} %get-tuple-element.25), channel_id=1, source_target_pairs={{0,1},{1,0},{2,3},{3,2},{4,5},{5,4},{6,7},{7,6},{8,9},{9,8},{10,11... | collective-permute-start | bytes 12296 | tf_op jit(solution)/shard_map/ppermute | solution.py:494
  72.9 32.4 %all-to-all-start.2 = ((f32[16,2,64,128]{3,2,1,0:T(8,128)}), f32[16,2,64,128]{3,2,1,0:T(8,128)S(1)}, u32[]{:S(2)}, u32[]{:S(2)}) async-start(f32[16,2,64,128]{3,2,1,0:T(8,128)} %bitcast.32), calls=%async_computation.2 | async-start | bytes 2097152 | tf_op jit(solution)/shard_map/all_to_all | solution.py:490
  80.1 6.8 %collective-permute-start.5 = (f32[8,128]{1,0:T(8,128)S(1)}, f32[8,128]{1,0:T(8,128)S(1)}, u32[]{:S(2)}, u32[]{:S(2)}) collective-permute-start(f32[8,128]{1,0:T(8,128)S(1)} %add.38), channel_id=1, source_target_pairs={{0,4},{2,6},{4,0},{6,2},{1,5},{3,7},{5,1},{7,3},{8,12},{10,14},{12... | collective-permute-start | bytes 12296 | tf_op jit(solution)/shard_map/ppermute | solution.py:494
  83.7 4.8 %collective-permute-start.6 = (f32[8,128]{1,0:T(8,128)S(1)}, f32[8,128]{1,0:T(8,128)S(1)}, u32[]{:S(2)}, u32[]{:S(2)}) collective-permute-start(f32[8,128]{1,0:T(8,128)S(1)} %add.38), channel_id=1, source_target_pairs={{0,2},{2,4},{4,6},{6,0},{1,3},{3,5},{5,7},{7,1},{8,10},{10,12},{12... | collective-permute-start | bytes 12296 | tf_op jit(solution)/shard_map/ppermute | solution.py:494
  83.7 4.8 %collective-permute-start.7 = (f32[8,128]{1,0:T(8,128)S(1)}, f32[8,128]{1,0:T(8,128)S(1)}, u32[]{:S(2)}, u32[]{:S(2)}) collective-permute-start(f32[8,128]{1,0:T(8,128)S(1)} %add.38), channel_id=1, source_target_pairs={{0,6},{2,0},{4,2},{6,4},{1,7},{3,1},{5,3},{7,5},{8,14},{10,8},{12,... | collective-permute-start | bytes 12296 | tf_op jit(solution)/shard_map/ppermute | solution.py:494
  88.5 5.3 %collective-permute-start.10 = (f32[8,128]{1,0:T(8,128)S(1)}, f32[8,128]{1,0:T(8,128)S(1)}, u32[]{:S(2)}, u32[]{:S(2)}) collective-permute-start(f32[8,128]{1,0:T(8,128)S(1)} %add_add_fusion.2), channel_id=1, source_target_pairs={{0,24},{8,0},{16,8},{24,16},{1,25},{9,1},{17,9},{25,17},{2,26},{10... | collective-permute-start | bytes 12296 | tf_op jit(solution)/shard_map/ppermute | solution.py:494
  91.3 5.1 %collective-permute-start.8 = (f32[8,128]{1,0:T(8,128)S(1)}, f32[8,128]{1,0:T(8,128)S(1)}, u32[]{:S(2)}, u32[]{:S(2)}) collective-permute-start(f32[8,128]{1,0:T(8,128)S(1)} %add_add_fusion.2), channel_id=1, source_target_pairs={{0,16},{8,24},{16,0},{24,8},{1,17},{9,25},{17,1},{25,9},{2,18},{10... | collective-permute-start | bytes 12296 | tf_op jit(solution)/shard_map/ppermute | solution.py:494
  92.1 4.8 %collective-permute-start.9 = (f32[8,128]{1,0:T(8,128)S(1)}, f32[8,128]{1,0:T(8,128)S(1)}, u32[]{:S(2)}, u32[]{:S(2)}) collective-permute-start(f32[8,128]{1,0:T(8,128)S(1)} %add_add_fusion.2), channel_id=1, source_target_pairs={{0,8},{8,16},{16,24},{24,0},{1,9},{9,17},{17,25},{25,1},{2,10},{10... | collective-permute-start | bytes 12296 | tf_op jit(solution)/shard_map/ppermute | solution.py:494
  96.9 5.1 %collective-permute-start.11 = (f32[8,128]{1,0:T(8,128)S(1)}, f32[8,128]{1,0:T(8,128)S(1)}, u32[]{:S(2)}, u32[]{:S(2)}) collective-permute-start(f32[8,128]{1,0:T(8,128)S(1)} %add_add_fusion.1), channel_id=1, source_target_pairs={{0,64},{32,96},{64,0},{96,32},{1,65},{33,97},{65,1},{97,33},{2,66}... | collective-permute-start | bytes 12296 | tf_op jit(solution)/shard_map/ppermute | solution.py:494
  98.4 3.7 %collective-permute-start.12 = (f32[8,128]{1,0:T(8,128)S(1)}, f32[8,128]{1,0:T(8,128)S(1)}, u32[]{:S(2)}, u32[]{:S(2)}) collective-permute-start(f32[8,128]{1,0:T(8,128)S(1)} %add_add_fusion.1), channel_id=1, source_target_pairs={{0,32},{32,64},{64,96},{96,0},{1,33},{33,65},{65,97},{97,1},{2,34}... | collective-permute-start | bytes 12296 | tf_op jit(solution)/shard_map/ppermute | solution.py:494
  100.5 4.8 %collective-permute-start.13 = (f32[8,128]{1,0:T(8,128)S(1)}, f32[8,128]{1,0:T(8,128)S(1)}, u32[]{:S(2)}, u32[]{:S(2)}) collective-permute-start(f32[8,128]{1,0:T(8,128)S(1)} %add_add_fusion.1), channel_id=1, source_target_pairs={{0,96},{32,0},{64,32},{96,64},{1,97},{33,1},{65,33},{97,65},{2,98}... | collective-permute-start | bytes 12296 | tf_op jit(solution)/shard_map/ppermute | solution.py:494
  (1 other events, 1.0 us)
